TPU v7x, 32 devices: a whole 2x2x4 slice. The times are simulated.
32 devices in a mesh: dp: 8 (over y, x, core), tensor: 4 (over z).
Axes of the slice: x: 2, y: 2, z: 4, core: 2. Of those that a mesh axis runs over, the one named last changes fastest.
Arguments:
- tokens: bfloat16 [16384, 1024], P(('dp', 'tensor')), may hold values from -6 to 6
- encoded: bfloat16 [8192, 1024], P(('dp', 'tensor')), may hold values from -6 to 6
- parents: int32 [8, 16], P('dp'), may hold values from 0 to 14, as said below
- source_lengths: int32 [8], P('dp'), may hold values from 769 to 1024, as said below
- cotangent: bfloat16 [16384, 1024], P(('dp', 'tensor')), may hold values from -6 to 6
- first_gain: float32 [1024], replicated, may hold values from 0.5 to 1.5
- first_shift: float32 [1024], replicated, may hold values from -1.25 to 1.25
- self_query: bfloat16 [1024, 1024], P('dp', 'tensor'), may hold values from -0.1875 to 0.1875
- self_query_bias: float32 [1024], P('tensor'), may hold values from -1.75 to 1.75
- self_key: bfloat16 [1024, 1024], P('dp', 'tensor'), may hold values from -0.1875 to 0.1875
- self_value: bfloat16 [1024, 1024], P('dp', 'tensor'), may hold values from -0.1875 to 0.1875
- self_value_bias: float32 [1024], P('tensor'), may hold values from -1.75 to 1.75
- self_out: bfloat16 [1024, 1024], P('tensor', 'dp'), may hold values from -0.5 to 0.5
- self_out_bias: float32 [1024], replicated, may hold values from -1.75 to 1.75
- second_gain: float32 [1024], replicated, may hold values from 0.5 to 1.5
- second_shift: float32 [1024], replicated, may hold values from -1.25 to 1.25
- cross_query: bfloat16 [1024, 1024], P('dp', 'tensor'), may hold values from -0.1875 to 0.1875
- cross_query_bias: float32 [1024], P('tensor'), may hold values from -1.75 to 1.75
- cross_key: bfloat16 [1024, 1024], P('dp', 'tensor'), may hold values from -0.1875 to 0.1875
- cross_value: bfloat16 [1024, 1024], P('dp', 'tensor'), may hold values from -0.1875 to 0.1875
- cross_value_bias: float32 [1024], P('tensor'), may hold values from -1.75 to 1.75
- cross_out: bfloat16 [1024, 1024], P('tensor', 'dp'), may hold values from -0.5 to 0.5
- cross_out_bias: float32 [1024], replicated, may hold values from -1.75 to 1.75
- third_gain: float32 [1024], replicated, may hold values from 0.5 to 1.5
- third_shift: float32 [1024], replicated, may hold values from -1.25 to 1.25
- up_weight: bfloat16 [1024, 8192], P('dp', 'tensor'), may hold values from -0.1875 to 0.1875
- up_bias: float32 [8192], P('tensor'), may hold values from -3 to 3
- down_weight: bfloat16 [8192, 1024], P('tensor', 'dp'), may hold values from -0.0625 to 0.0625
- down_bias: float32 [1024], replicated, may hold values from -1.75 to 1.75
Outputs:
- block_out: bfloat16 [16384, 1024], P(('dp', 'tensor'))
- tokens_grad: float32 [16384, 1024], P(('dp', 'tensor'))
- encoded_grad: float32 [8192, 1024], P(('dp', 'tensor'))
- first_gain_grad: float32 [1024], replicated
- first_shift_grad: float32 [1024], replicated
- self_query_grad: float32 [1024, 1024], P('dp', 'tensor')
- self_query_bias_grad: float32 [1024], P('tensor')
- self_key_grad: float32 [1024, 1024], P('dp', 'tensor')
- self_value_grad: float32 [1024, 1024], P('dp', 'tensor')
- self_value_bias_grad: float32 [1024], P('tensor')
- self_out_grad: float32 [1024, 1024], P('tensor', 'dp')
- self_out_bias_grad: float32 [1024], replicated
- second_gain_grad: float32 [1024], replicated
- second_shift_grad: float32 [1024], replicated
- cross_query_grad: float32 [1024, 1024], P('dp', 'tensor')
- cross_query_bias_grad: float32 [1024], P('tensor')
- cross_key_grad: float32 [1024, 1024], P('dp', 'tensor')
- cross_value_grad: float32 [1024, 1024], P('dp', 'tensor')
- cross_value_bias_grad: float32 [1024], P('tensor')
- cross_out_grad: float32 [1024, 1024], P('tensor', 'dp')
- cross_out_bias_grad: float32 [1024], replicated
- third_gain_grad: float32 [1024], replicated
- third_shift_grad: float32 [1024], replicated
- up_weight_grad: float32 [1024, 8192], P('dp', 'tensor')
- up_bias_grad: float32 [8192], P('tensor')
- down_weight_grad: float32 [8192, 1024], P('tensor', 'dp')
- down_bias_grad: float32 [1024], replicated
Inputs may be any that keep to these rules, and one draw needn't show every extreme that they name: `parents`: for segment s of a tree, the parent segment on its path to the root: 0 for segments 0 and 1, else s - 1 or s - 2. `source_lengths`: some tree has all 1024 encoder states.
All inputs are finite; a program needn't handle non-finite values.
Results may differ from a plain program's by a relative error of at most 0.025.
Values may be sent and summed in bfloat16 or wider, within the bound.
No kernel may reach another device: no remote copies, remote signals or barrier semaphores. Data moves between devices by JAX's collectives and lax.ppermute only.
A program may use at most 192 MiB of HBM per device.

v0:
```python
import jax
import jax.numpy as jnp
from jax import lax
from jax.sharding import PartitionSpec as P

HEAD_DIM = 64
SEG = 128


epsilon = 1e-05


def norm_rows(rows, scale_gain, shift):
    average = jnp.mean(rows, axis=-1, keepdims=True)
    centered = rows - average
    variance = jnp.mean(centered * centered, axis=-1, keepdims=True)
    return centered * lax.rsqrt(variance + epsilon) * scale_gain + shift


def norm_back(rows, scale_gain, shift, grad):
    outputs_value, pullback = jax.vjp(norm_rows, rows, scale_gain, shift)
    return pullback(grad)


def gelu_exact(values):
    return jax.nn.gelu(values, approximate=False)


def inner_rows(left, right):
    return lax.dot_general(
        left, right, (((0,), (0,)), ((), ())), preferred_element_type=jnp.float32
    )


def outer_cols(left, right):
    return lax.dot_general(
        left, right, (((1,), (1,)), ((), ())), preferred_element_type=jnp.float32
    )


def split_heads(matrix):
    return matrix.reshape(matrix.shape[0], -1, HEAD_DIM)


def ancestors(parent_row):
    count = parent_row.shape[0]

    def extend(segment_index, table):
        fresh = (
            jnp.where(jnp.arange(count) == segment_index, 1.0, 0.0)
            + table[parent_row[segment_index]]
        )
        return table.at[segment_index].set(fresh)

    return lax.fori_loop(1, count, extend, jnp.eye(count, dtype=jnp.float32))


def path_allowed(table, start, count, total):
    query_place = start + jnp.arange(count)
    key_place = jnp.arange(total)
    labels = jnp.arange(table.shape[0])
    query_hot = (query_place[:, None] // SEG == labels[None, :]).astype(jnp.float32)
    key_hot = (key_place[:, None] // SEG == labels[None, :]).astype(jnp.float32)
    reach = jnp.dot(jnp.dot(query_hot, table), key_hot.T)
    return (reach > 0.5) & (key_place[None, :] <= query_place[:, None])


def block_scores(part, keys, allowed):
    scores = jnp.einsum(
        "qhd,khd->hqk", part, keys, preferred_element_type=jnp.float32
    ) * HEAD_DIM ** (-0.5)
    return jnp.where(allowed[None], scores, -1e30)


def attend_forward(query, keys, values, mask_fn):
    total = query.shape[0]
    block = min(512, total)

    def one_block(index):
        start = index * block
        part = lax.dynamic_slice_in_dim(query, start, block, 0)
        scores = block_scores(part, keys, mask_fn(start, block))
        highest = jnp.max(scores, axis=-1, keepdims=True)
        raised = jnp.exp(scores - highest)
        totals = jnp.sum(raised, axis=-1, keepdims=True)
        probs = (raised / totals).astype(jnp.bfloat16)
        output = jnp.einsum("hqk,khd->qhd", probs, values, preferred_element_type=jnp.float32)
        return (output, highest + jnp.log(totals))

    outputs, log_total = lax.map(one_block, jnp.arange(total // block))
    return (outputs.reshape(total, -1), log_total)


def attend_backward(query, keys, values, log_total, grad_mixed, mask_fn):
    total = query.shape[0]
    block = min(512, total)
    scale = HEAD_DIM ** (-0.5)

    def one_block(carry, index):
        grad_keys, grad_values = carry
        start = index * block
        part = lax.dynamic_slice_in_dim(query, start, block, 0)
        grad_part = lax.dynamic_slice_in_dim(grad_mixed, start, block, 0)
        scores = block_scores(part, keys, mask_fn(start, block))
        probs = jnp.exp(scores - log_total[index])
        grad_values = grad_values + jnp.einsum(
            "hqk,qhd->khd",
            probs.astype(jnp.bfloat16),
            grad_part,
            preferred_element_type=jnp.float32,
        )
        grad_probs = jnp.einsum(
            "qhd,khd->hqk", grad_part, values, preferred_element_type=jnp.float32
        )
        weighted = jnp.sum(probs * grad_probs, axis=-1, keepdims=True)
        grad_scores = (probs * (grad_probs - weighted)).astype(jnp.bfloat16)
        grad_query = (
            jnp.einsum("hqk,khd->qhd", grad_scores, keys, preferred_element_type=jnp.float32)
            * scale
        )
        grad_keys = (
            grad_keys
            + jnp.einsum("hqk,qhd->khd", grad_scores, part, preferred_element_type=jnp.float32)
            * scale
        )
        return ((grad_keys, grad_values), grad_query)

    empty = jnp.zeros(keys.shape, jnp.float32)
    (grad_keys, grad_values), grad_query = lax.scan(
        one_block, (empty, empty), jnp.arange(total // block)
    )
    grad_query = grad_query.reshape(total, -1).astype(jnp.bfloat16)
    grad_keys = grad_keys.reshape(keys.shape[0], -1).astype(jnp.bfloat16)
    grad_values = grad_values.reshape(keys.shape[0], -1).astype(jnp.bfloat16)
    return (grad_query, grad_keys, grad_values)


def gather_rows(normed):
    return lax.all_gather(normed, "tensor", axis=0, tiled=True)


def sum_rows(partial_value):
    return lax.psum_scatter(partial_value, "tensor", scatter_dimension=0, tiled=True)


def gather_grads(grad_low):
    return lax.all_gather(grad_low, "tensor", axis=0, tiled=True)


def sum_grads(partial_value):
    return lax.psum_scatter(partial_value, "tensor", scatter_dimension=0, tiled=True)


def column_sums(matrix):
    return jnp.sum(matrix, axis=0, dtype=jnp.float32)


def project_out(mixed, weight_part):
    return (sum_rows(jnp.dot(mixed, weight_part, preferred_element_type=jnp.float32)), mixed)


def project_back(grad_low, kept, weight_part):
    grad_gathered = gather_grads(grad_low)
    return (
        outer_cols(grad_gathered, weight_part).astype(jnp.bfloat16),
        inner_rows(kept, grad_gathered),
    )


def on_device(
    tokens,
    encoded,
    parents,
    source_lengths,
    cotangent,
    first_gain,
    first_shift,
    self_query,
    self_query_bias,
    self_key,
    self_value,
    self_value_bias,
    self_out,
    self_out_bias,
    second_gain,
    second_shift,
    cross_query,
    cross_query_bias,
    cross_key,
    cross_value,
    cross_value_bias,
    cross_out,
    cross_out_bias,
    third_gain,
    third_shift,
    up_weight,
    up_bias,
    down_weight,
    down_bias,
):
    gathered = (
        lax.all_gather(self_query, "dp", axis=0, tiled=True),
        lax.all_gather(self_key, "dp", axis=0, tiled=True),
        lax.all_gather(self_value, "dp", axis=0, tiled=True),
        lax.all_gather(self_out, "dp", axis=1, tiled=True),
        lax.all_gather(cross_query, "dp", axis=0, tiled=True),
        lax.all_gather(cross_key, "dp", axis=0, tiled=True),
        lax.all_gather(cross_value, "dp", axis=0, tiled=True),
        lax.all_gather(cross_out, "dp", axis=1, tiled=True),
        lax.all_gather(up_weight, "dp", axis=0, tiled=True),
        lax.all_gather(down_weight, "dp", axis=1, tiled=True),
    )
    (
        self_query_all,
        self_key_all,
        self_value_all,
        self_out_all,
        cross_query_all,
        cross_key_all,
        cross_value_all,
        cross_out_all,
        up_weight_all,
        down_weight_all,
    ) = gathered
    table = ancestors(parents[0])
    length = source_lengths[0]
    rows = tokens.astype(jnp.float32)
    normed_one = norm_rows(rows, first_gain, first_shift).astype(jnp.bfloat16)
    rows_one, source = (
        lax.all_gather(normed_one, "tensor", axis=0, tiled=True),
        lax.all_gather(encoded, "tensor", axis=0, tiled=True),
    )
    total_rows = rows_one.shape[0]
    total_source = source.shape[0]

    def self_mask(start, count):
        return path_allowed(table, start, count, total_rows)

    def cross_mask(start, count):
        return jnp.broadcast_to((jnp.arange(total_source) < length)[None, :], (count, total_source))

    query_one = (
        jnp.dot(rows_one, self_query_all, preferred_element_type=jnp.float32) + self_query_bias
    ).astype(jnp.bfloat16)
    keys_one = jnp.dot(rows_one, self_key_all, preferred_element_type=jnp.float32).astype(
        jnp.bfloat16
    )
    values_one = (
        jnp.dot(rows_one, self_value_all, preferred_element_type=jnp.float32) + self_value_bias
    ).astype(jnp.bfloat16)
    mixed_one, log_one = attend_forward(
        split_heads(query_one), split_heads(keys_one), split_heads(values_one), self_mask
    )
    mixed_one = mixed_one.astype(jnp.bfloat16)
    branch_one, kept_one = project_out(mixed_one, self_out_all)
    hidden_one = rows + branch_one + self_out_bias
    normed_two = norm_rows(hidden_one, second_gain, second_shift).astype(jnp.bfloat16)
    rows_two = gather_rows(normed_two)
    query_two = (
        jnp.dot(rows_two, cross_query_all, preferred_element_type=jnp.float32) + cross_query_bias
    ).astype(jnp.bfloat16)
    keys_two = jnp.dot(source, cross_key_all, preferred_element_type=jnp.float32).astype(
        jnp.bfloat16
    )
    values_two = (
        jnp.dot(source, cross_value_all, preferred_element_type=jnp.float32) + cross_value_bias
    ).astype(jnp.bfloat16)
    mixed_two, log_two = attend_forward(
        split_heads(query_two), split_heads(keys_two), split_heads(values_two), cross_mask
    )
    mixed_two = mixed_two.astype(jnp.bfloat16)
    branch_two, kept_two = project_out(mixed_two, cross_out_all)
    hidden_two = hidden_one + branch_two + cross_out_bias
    normed_three = norm_rows(hidden_two, third_gain, third_shift).astype(jnp.bfloat16)
    rows_three = gather_rows(normed_three)
    lifted = jnp.dot(rows_three, up_weight_all, preferred_element_type=jnp.float32) + up_bias
    inner = gelu_exact(lifted).astype(jnp.bfloat16)
    block_out = (
        hidden_two
        + sum_rows(jnp.dot(inner, down_weight_all, preferred_element_type=jnp.float32))
        + down_bias
    )
    back_weights = (
        lax.all_gather(self_query, "dp", axis=0, tiled=True),
        lax.all_gather(self_key, "dp", axis=0, tiled=True),
        lax.all_gather(self_value, "dp", axis=0, tiled=True),
        lax.all_gather(self_out, "dp", axis=1, tiled=True),
        lax.all_gather(cross_query, "dp", axis=0, tiled=True),
        lax.all_gather(cross_key, "dp", axis=0, tiled=True),
        lax.all_gather(cross_value, "dp", axis=0, tiled=True),
        lax.all_gather(cross_out, "dp", axis=1, tiled=True),
        lax.all_gather(up_weight, "dp", axis=0, tiled=True),
        lax.all_gather(down_weight, "dp", axis=1, tiled=True),
    )
    (
        self_query_all,
        self_key_all,
        self_value_all,
        self_out_all,
        cross_query_all,
        cross_key_all,
        cross_value_all,
        cross_out_all,
        up_weight_all,
        down_weight_all,
    ) = back_weights
    down_bias_grad = column_sums(cotangent)
    grad_rows_three = gather_grads(cotangent)
    down_weight_grad = inner_rows(inner, grad_rows_three)
    grad_inner = outer_cols(grad_rows_three, down_weight_all)
    gelu_value, gelu_pull = jax.vjp(gelu_exact, lifted)
    grad_lifted = gelu_pull(grad_inner)[0].astype(jnp.bfloat16)
    up_bias_grad = column_sums(grad_lifted)
    up_weight_grad = inner_rows(rows_three, grad_lifted)
    grad_normed_three = sum_grads(outer_cols(grad_lifted, up_weight_all))
    grad_hidden_two, third_gain_grad, third_shift_grad = norm_back(
        hidden_two, third_gain, third_shift, grad_normed_three
    )
    grad_hidden_two = cotangent.astype(jnp.float32) + grad_hidden_two
    grad_two = grad_hidden_two.astype(jnp.bfloat16)
    cross_out_bias_grad = column_sums(grad_two)
    grad_mixed_two, cross_out_grad = project_back(grad_two, kept_two, cross_out_all)
    grad_query_two, grad_keys_two, grad_values_two = attend_backward(
        split_heads(query_two),
        split_heads(keys_two),
        split_heads(values_two),
        log_two,
        split_heads(grad_mixed_two),
        cross_mask,
    )
    cross_query_bias_grad = column_sums(grad_query_two)
    cross_value_bias_grad = column_sums(grad_values_two)
    cross_query_grad = inner_rows(rows_two, grad_query_two)
    cross_key_grad = inner_rows(source, grad_keys_two)
    cross_value_grad = inner_rows(source, grad_values_two)
    grad_normed_two, encoded_grad = (
        lax.psum_scatter(
            outer_cols(grad_query_two, cross_query_all), "tensor", scatter_dimension=0, tiled=True
        ),
        lax.psum_scatter(
            outer_cols(grad_keys_two, cross_key_all) + outer_cols(grad_values_two, cross_value_all),
            "tensor",
            scatter_dimension=0,
            tiled=True,
        ),
    )
    grad_hidden_one, second_gain_grad, second_shift_grad = norm_back(
        hidden_one, second_gain, second_shift, grad_normed_two
    )
    grad_hidden_one = grad_hidden_two + grad_hidden_one
    grad_one = grad_hidden_one.astype(jnp.bfloat16)
    self_out_bias_grad = column_sums(grad_one)
    grad_mixed_one, self_out_grad = project_back(grad_one, kept_one, self_out_all)
    grad_query_one, grad_keys_one, grad_values_one = attend_backward(
        split_heads(query_one),
        split_heads(keys_one),
        split_heads(values_one),
        log_one,
        split_heads(grad_mixed_one),
        self_mask,
    )
    self_query_bias_grad = column_sums(grad_query_one)
    self_value_bias_grad = column_sums(grad_values_one)
    self_query_grad = inner_rows(rows_one, grad_query_one)
    self_key_grad = inner_rows(rows_one, grad_keys_one)
    self_value_grad = inner_rows(rows_one, grad_values_one)
    grad_normed_one = sum_grads(
        outer_cols(grad_query_one, self_query_all)
        + outer_cols(grad_keys_one, self_key_all)
        + outer_cols(grad_values_one, self_value_all)
    )
    grad_rows_input, first_gain_grad, first_shift_grad = norm_back(
        rows, first_gain, first_shift, grad_normed_one
    )
    tokens_grad = grad_hidden_one + grad_rows_input
    (
        self_query_grad,
        self_key_grad,
        self_value_grad,
        self_out_grad,
        cross_query_grad,
        cross_key_grad,
        cross_value_grad,
        cross_out_grad,
        up_weight_grad,
        down_weight_grad,
    ) = (
        lax.psum_scatter(self_query_grad, "dp", scatter_dimension=0, tiled=True),
        lax.psum_scatter(self_key_grad, "dp", scatter_dimension=0, tiled=True),
        lax.psum_scatter(self_value_grad, "dp", scatter_dimension=0, tiled=True),
        lax.psum_scatter(self_out_grad, "dp", scatter_dimension=1, tiled=True),
        lax.psum_scatter(cross_query_grad, "dp", scatter_dimension=0, tiled=True),
        lax.psum_scatter(cross_key_grad, "dp", scatter_dimension=0, tiled=True),
        lax.psum_scatter(cross_value_grad, "dp", scatter_dimension=0, tiled=True),
        lax.psum_scatter(cross_out_grad, "dp", scatter_dimension=1, tiled=True),
        lax.psum_scatter(up_weight_grad, "dp", scatter_dimension=0, tiled=True),
        lax.psum_scatter(down_weight_grad, "dp", scatter_dimension=1, tiled=True),
    )
    (
        self_query_bias_grad,
        self_value_bias_grad,
        cross_query_bias_grad,
        cross_value_bias_grad,
        up_bias_grad,
    ) = lax.psum(
        (
            self_query_bias_grad,
            self_value_bias_grad,
            cross_query_bias_grad,
            cross_value_bias_grad,
            up_bias_grad,
        ),
        "dp",
    )
    (
        first_gain_grad,
        first_shift_grad,
        second_gain_grad,
        second_shift_grad,
        third_gain_grad,
        third_shift_grad,
        self_out_bias_grad,
        cross_out_bias_grad,
        down_bias_grad,
    ) = lax.psum(
        (
            first_gain_grad,
            first_shift_grad,
            second_gain_grad,
            second_shift_grad,
            third_gain_grad,
            third_shift_grad,
            self_out_bias_grad,
            cross_out_bias_grad,
            down_bias_grad,
        ),
        ("dp", "tensor"),
    )
    return (
        block_out.astype(jnp.bfloat16),
        tokens_grad,
        encoded_grad,
        first_gain_grad,
        first_shift_grad,
        self_query_grad,
        self_query_bias_grad,
        self_key_grad,
        self_value_grad,
        self_value_bias_grad,
        self_out_grad,
        self_out_bias_grad,
        second_gain_grad,
        second_shift_grad,
        cross_query_grad,
        cross_query_bias_grad,
        cross_key_grad,
        cross_value_grad,
        cross_value_bias_grad,
        cross_out_grad,
        cross_out_bias_grad,
        third_gain_grad,
        third_shift_grad,
        up_weight_grad,
        up_bias_grad,
        down_weight_grad,
        down_bias_grad,
    )


def solution(mesh):
    placed = (
        P(("dp", "tensor"), None),
        P(("dp", "tensor"), None),
        P("dp", None),
        P("dp"),
        P(("dp", "tensor"), None),
        P(),
        P(),
        P("dp", "tensor"),
        P("tensor"),
        P("dp", "tensor"),
        P("dp", "tensor"),
        P("tensor"),
        P("tensor", "dp"),
        P(),
        P(),
        P(),
        P("dp", "tensor"),
        P("tensor"),
        P("dp", "tensor"),
        P("dp", "tensor"),
        P("tensor"),
        P("tensor", "dp"),
        P(),
        P(),
        P(),
        P("dp", "tensor"),
        P("tensor"),
        P("tensor", "dp"),
        P(),
    )
    return jax.shard_map(
        on_device,
        mesh=mesh,
        in_specs=placed,
        out_specs=(
            P(("dp", "tensor"), None),
            P(("dp", "tensor"), None),
            P(("dp", "tensor"), None),
            P(),
            P(),
            P("dp", "tensor"),
            P("tensor"),
            P("dp", "tensor"),
            P("dp", "tensor"),
            P("tensor"),
            P("tensor", "dp"),
            P(),
            P(),
            P(),
            P("dp", "tensor"),
            P("tensor"),
            P("dp", "tensor"),
            P("dp", "tensor"),
            P("tensor"),
            P("tensor", "dp"),
            P(),
            P(),
            P(),
            P("dp", "tensor"),
            P("tensor"),
            P("tensor", "dp"),
            P(),
        ),
        check_vma=False,
    )
```

profile of v0, /device:TPU:0, one launch (start us, length us, event | category | flops | bytes accessed | tf_op | source)
XLA Modules:
  0.0 2463.1 jit_solution(9129957230743042297)
XLA Ops:
  14.1 59.4 %while.76 = (s32[]{:T(128)}, f32[16,16]{1,0:T(8,128)S(1)}, s32[16]{0:T(128)S(1)}, s32[]{:T(128)}, s32[2]{0:T(128)S(1)}, /*index=5*/s32[1]{0:T(128)}, s32[]{:T(128)}, s32[]{:T(128)}, s32[]{:T(128)}) while((s32[]{:T(128)}, f32[16,16]{1,0:T(8,128)S(1)}, s32[16]{0:T(128)S(1)}, s32[]{:T(128)}, s32[2]{0:T(128)S(1)}, /*index=5*/s32[1]{0:T(128)}, ...), condition=%wide.region_4.5_spmd, body=%wide.region_2.0_spmd.sunk | while | flops 81 | bytes 527 | solution.py:55
  122.9 69.5 %while.77 = (s32[]{:T(128)}, bf16[4,512,4,64]{1,3,2,0:T(8,128)(2,1)}, f32[4,4,512,1]{2,1,3,0:T(4,128)S(1)}, s32[4]{0:T(128)S(1)}, bf16[16,16]{1,0:T(8,128)(2,1)S...) while((s32[]{:T(128)}, ...), condition=%wide.region_8.9_spmd, body=%wide.region_5.8_spmd.sunk | while | flops 1161099264 | bytes 65889020 | solution.py:90
  201.1 144.1 %reduce-scatter.18.cloned.1.call-done = f32[512,1024]{1,0:T(8,128)} async-done(((f32[2048,1024]{1,0:T(8,128)}), f32[512,1024]{1,0:T(8,128)}) %reduce-scatter.18.cloned.1.call-update) | async-done | bytes 2097168 | tf_op jit(solution)/shard_map/reduce_scatter | solution.py:143
  398.2 76.7 %all-gather.12.cloned.1.call-done = bf16[2048,1024]{1,0:T(8,128)(2,1)} async-done(((bf16[512,1024]{1,0:T(8,128)(2,1)}), bf16[2048,1024]{1,0:T(8,128)(2,1)}) %all-gather.12.cloned.1.call-update) | async-done | bytes 4194320 | tf_op jit(solution)/shard_map/all_gather | solution.py:139
  528.7 142.5 %reduce-scatter.20.cloned.1.call-done = f32[512,1024]{1,0:T(8,128)} async-done(((f32[2048,1024]{1,0:T(8,128)}), f32[512,1024]{1,0:T(8,128)}) %reduce-scatter.20.cloned.1.call-update) | async-done | bytes 2097168 | tf_op jit(solution)/shard_map/reduce_scatter | solution.py:143
  678.0 79.8 %all-gather.16.cloned.1.call-done = bf16[2048,1024]{1,0:T(8,128)(2,1)} async-done(((bf16[512,1024]{1,0:T(8,128)(2,1)}), bf16[2048,1024]{1,0:T(8,128)(2,1)}) %all-gather.16.cloned.1.call-update) | async-done | bytes 4194320 | tf_op jit(solution)/shard_map/all_gather | solution.py:139
  757.8 49.3 %multiply_convert_fusion.2 = (bf16[2048,2048]{1,0:T(8,128)(2,1)}, f32[2048,2048]{1,0:T(8,128)}, f32[2048,2048]{1,0:T(8,128)}) fusion(f32[2048]{0:T(1024)S(1)} %copy-done.110, bf16[2048,1024]{1,0:T(8,128)(2,1)} %all-gather.16.cloned.1.call-done, bf16[1024,2048]{1,0:T(8,128)(2,1)} %all-gather.18.cloned.1.call-done), kind=kOutput, calls=%fused_computation.138 | convolution fusion | flops 8866758656 | bytes 50339840 | tf_op jit(solution)/shard_map/dot_general | solution.py:276
  928.0 130.0 %reduce-scatter.24.cloned.1.call-done = f32[512,1024]{1,0:T(8,128)} async-done(((f32[2048,1024]{1,0:T(8,128)}), f32[512,1024]{1,0:T(8,128)}) %reduce-scatter.24.cloned.1.call-update) | async-done | bytes 2097168 | tf_op jit(solution)/shard_map/reduce_scatter | solution.py:151
  1061.0 144.6 %reduce-scatter.22.cloned.1.call-done = f32[512,1024]{1,0:T(8,128)} async-done(((f32[2048,1024]{1,0:T(8,128)}), f32[512,1024]{1,0:T(8,128)}) %reduce-scatter.22.cloned.1.call-update) | async-done | bytes 2097168 | tf_op jit(solution)/shard_map/reduce_scatter | solution.py:143
  1213.0 81.4 %all-gather.24.cloned.1.call-done = bf16[2048,1024]{1,0:T(8,128)(2,1)} async-done(((bf16[512,1024]{1,0:T(8,128)(2,1)}), bf16[2048,1024]{1,0:T(8,128)(2,1)}) %all-gather.24.cloned.1.call-update) | async-done | bytes 4194320 | tf_op jit(solution)/shard_map/all_gather | solution.py:147
  1300.1 73.6 %while.79 = (s32[]{:T(128)}, f32[1024,4,64]{0,2,1:T(8,128)S(1)}, f32[1024,4,64]{0,2,1:T(8,128)}, bf16[4,512,4,64]{1,3,2,0:T(8,128)(2,1)}, s32[4]{0:T(128)S(1)}, ...) while((s32[]{:T(128)}, f32[1024,4,64]{0,2,1:T(8,128)S(1)}, ...), condition=%wide.region_25.26_spmd.clone, body=%wide.region_23.25_spmd.clone.sunk | while | flops 1375075328 | bytes 91287984 | solution.py:129
  1381.8 143.1 %reduce-scatter.26.cloned.1.call-done = f32[512,1024]{1,0:T(8,128)} async-done(((f32[2048,1024]{1,0:T(8,128)}), f32[512,1024]{1,0:T(8,128)}) %reduce-scatter.26.cloned.1.call-update) | async-done | bytes 2097168 | tf_op jit(solution)/shard_map/reduce_scatter | solution.py:337
  1543.3 72.0 %all-gather.26.cloned.1.call-done = bf16[2048,1024]{1,0:T(8,128)(2,1)} async-done(((bf16[512,1024]{1,0:T(8,128)(2,1)}), bf16[2048,1024]{1,0:T(8,128)(2,1)}) %all-gather.26.cloned.1.call-update) | async-done | bytes 4194320 | tf_op jit(solution)/shard_map/all_gather | solution.py:147
  1620.9 206.1 %while.80 = (s32[]{:T(128)}, f32[2048,4,64]{0,2,1:T(8,128)}, f32[2048,4,64]{0,2,1:T(8,128)}, bf16[4,512,4,64]{1,3,2,0:T(8,128)(2,1)}, s32[4]{0:T(128)S(1)}, /*in...) while((s32[]{:T(128)}, f32[2048,4,64]{0,2,1:T(8,128)}, ...), condition=%wide.region_31.32_spmd.clone, body=%wide.region_29.31_spmd.clone.sunk | while | flops 2787047424 | bytes 180962320 | solution.py:129
  1934.8 48.9 %reduce-scatter.28.cloned.1.call-done = f32[512,1024]{1,0:T(8,128)} async-done(((f32[2048,1024]{1,0:T(8,128)}), f32[512,1024]{1,0:T(8,128)}) %reduce-scatter.28.cloned.1.call-update) | async-done | bytes 2097168 | tf_op jit(solution)/shard_map/reduce_scatter | solution.py:151
  1991.1 42.4 %all-reduce = (f32[1024]{0:T(1024)}, f32[1024]{0:T(1024)}, f32[1024]{0:T(1024)}, f32[1024]{0:T(1024)}, f32[1024]{0:T(1024)}, /*index=5*/f32[1024]{0:T(1024)}, f32[1024]{0:T(1024)}, f32[1024]{0:T(1024)}, f32[1024]{0:T(1024)}) all-reduce(f32[1024]{0:T(1024)S(1)} %get-tuple-element.677, ...), channel_id=1, replica_groups=mesh['dp'=8,'tensor'=4] {'dp','tensor'}, use_global_device_ids=true, to_apply=%region_37.38 | all-reduce | flops 9216 | bytes 73728 | tf_op jit(solution)/shard_map/psum | solution.py:425
  2060.0 75.6 %reduce-scatter.50.cloned.1.call-done = f32[2048,128]{1,0:T(8,128)} async-done(((f32[2048,1024]{1,0:T(8,128)}), f32[2048,128]{1,0:T(8,128)}) %reduce-scatter.50.cloned.1.call-update) | async-done | bytes 1048592 | tf_op jit(solution)/shard_map/reduce_scatter | solution.py:397
  2135.6 39.6 %reduce-scatter.46.cloned.1.call-done = f32[256,128]{1,0:T(8,128)} async-done(((f32[256,1024]{1,0:T(8,128)}), f32[256,128]{1,0:T(8,128)}) %reduce-scatter.46.cloned.1.call-update) | async-done | bytes 131088 | tf_op jit(solution)/shard_map/reduce_scatter | solution.py:395
  2175.2 39.7 %reduce-scatter.40.cloned.1.call-done = f32[128,256]{1,0:T(8,128)} async-done(((f32[1024,256]{1,0:T(8,128)}), f32[128,256]{1,0:T(8,128)}) %reduce-scatter.40.cloned.1.call-update) | async-done | bytes 131088 | tf_op jit(solution)/shard_map/reduce_scatter | solution.py:392
  2215.0 79.7 %reduce-scatter.30.cloned.1.call-done = f32[256,1024]{1,0:T(8,128)} async-done(((f32[1024,1024]{1,0:T(8,128)}), f32[256,1024]{1,0:T(8,128)}) %reduce-scatter.30.cloned.1.call-update) | async-done | bytes 1048592 | tf_op jit(solution)/shard_map/reduce_scatter | solution.py:340
  2294.6 40.5 %reduce-scatter.38.cloned.1.call-done = f32[256,128]{1,0:T(8,128)} async-done(((f32[256,1024]{1,0:T(8,128)}), f32[256,128]{1,0:T(8,128)}) %reduce-scatter.38.cloned.1.call-update) | async-done | bytes 131088 | tf_op jit(solution)/shard_map/reduce_scatter | solution.py:391
  2335.1 40.1 %reduce-scatter.32.cloned.1.call-done = f32[128,256]{1,0:T(8,128)} async-done(((f32[1024,256]{1,0:T(8,128)}), f32[128,256]{1,0:T(8,128)}) %reduce-scatter.32.cloned.1.call-update) | async-done | bytes 131088 | tf_op jit(solution)/shard_map/reduce_scatter | solution.py:388
  2375.2 40.1 %reduce-scatter.34.cloned.1.call-done = f32[128,256]{1,0:T(8,128)} async-done(((f32[1024,256]{1,0:T(8,128)}), f32[128,256]{1,0:T(8,128)}) %reduce-scatter.34.cloned.1.call-update) | async-done | bytes 131088 | tf_op jit(solution)/shard_map/reduce_scatter | solution.py:389
  2415.3 39.9 %reduce-scatter.36.cloned.1.call-done = f32[128,256]{1,0:T(8,128)} async-done(((f32[1024,256]{1,0:T(8,128)}), f32[128,256]{1,0:T(8,128)}) %reduce-scatter.36.cloned.1.call-update) | async-done | bytes 131088 | tf_op jit(solution)/shard_map/reduce_scatter | solution.py:390
  (675 shorter events, 877.0 us)
Async XLA Ops:
  14.0 331.1 %reduce-scatter.18.cloned.1.call-start = ((), (), s32[]{:S(2)}) async-start(), calls=%async_computation.18 | async-start | bytes 10485760 | tf_op jit(solution)/shard_map/reduce_scatter | solution.py:143
  200.3 193.2 %all-gather.14.cloned.1.call-start = ((), (), s32[]{:S(2)}) async-start(), calls=%async_computation.20 | async-start | bytes 2621440 | tf_op jit(solution)/shard_map/all_gather | solution.py:231
  201.0 273.9 %all-gather.12.cloned.1.call-start = ((), (), s32[]{:S(2)}) async-start(), calls=%async_computation.19 | async-start | bytes 5242880 | tf_op jit(solution)/shard_map/all_gather | solution.py:139
  349.3 321.9 %reduce-scatter.20.cloned.1.call-start = ((), (), s32[]{:S(2)}) async-start(), calls=%async_computation.21 | async-start | bytes 10485760 | tf_op jit(solution)/shard_map/reduce_scatter | solution.py:143
  528.6 229.2 %all-gather.16.cloned.1.call-start = ((), (), s32[]{:S(2)}) async-start(), calls=%async_computation.22 | async-start | bytes 5242880 | tf_op jit(solution)/shard_map/all_gather | solution.py:139
  676.4 162.1 %all-gather.22.cloned.1.call-start = ((), (), s32[]{:S(2)}) async-start(), calls=%async_computation.26 | async-start | bytes 5242880 | tf_op jit(solution)/shard_map/all_gather | solution.py:147
  676.9 199.2 %all-gather.20.cloned.1.call-start = ((), (), s32[]{:S(2)}) async-start(), calls=%async_computation.24 | async-start | bytes 4718592 | tf_op jit(solution)/shard_map/all_gather | solution.py:211
  677.7 380.4 %reduce-scatter.24.cloned.1.call-start = ((), (), s32[]{:S(2)}) async-start(), calls=%async_computation.27 | async-start | bytes 10485760 | tf_op jit(solution)/shard_map/reduce_scatter | solution.py:151
  913.5 292.1 %reduce-scatter.22.cloned.1.call-start = ((), (), s32[]{:S(2)}) async-start(), calls=%async_computation.25 | async-start | bytes 10485760 | tf_op jit(solution)/shard_map/reduce_scatter | solution.py:143
  928.0 366.5 %all-gather.24.cloned.1.call-start = ((), (), s32[]{:S(2)}) async-start(), calls=%async_computation.28 | async-start | bytes 5242880 | tf_op jit(solution)/shard_map/all_gather | solution.py:147
  1212.9 312.0 %reduce-scatter.26.cloned.1.call-start = ((), (), s32[]{:S(2)}) async-start(), calls=%async_computation.29 | async-start | bytes 10485760 | tf_op jit(solution)/shard_map/reduce_scatter | solution.py:337
  1381.8 233.6 %all-gather.26.cloned.1.call-start = ((), (), s32[]{:S(2)}) async-start(), calls=%async_computation.30 | async-start | bytes 5242880 | tf_op jit(solution)/shard_map/all_gather | solution.py:147
  1533.9 366.5 %reduce-scatter.42.cloned.1.call-start = ((), (), s32[]{:S(2)}) async-start(), calls=%async_computation.38 | async-start | bytes 1179648 | tf_op jit(solution)/shard_map/reduce_scatter | solution.py:393
  1538.2 363.9 %reduce-scatter.44.cloned.1.call-start = ((), (), s32[]{:S(2)}) async-start(), calls=%async_computation.39 | async-start | bytes 1179648 | tf_op jit(solution)/shard_map/reduce_scatter | solution.py:394
  1543.3 440.4 %reduce-scatter.28.cloned.1.call-start = ((), (), s32[]{:S(2)}) async-start(), calls=%async_computation.31 | async-start | bytes 10485760 | tf_op jit(solution)/shard_map/reduce_scatter | solution.py:151
  1840.5 219.6 %reduce-scatter.48.cloned.1.call-start = ((), (), s32[]{:S(2)}) async-start(), calls=%async_computation.41 | async-start | bytes 9437184 | tf_op jit(solution)/shard_map/reduce_scatter | solution.py:396
  1855.2 280.4 %reduce-scatter.50.cloned.1.call-start = ((), (), s32[]{:S(2)}) async-start(), calls=%async_computation.42 | async-start | bytes 9437184 | tf_op jit(solution)/shard_map/reduce_scatter | solution.py:397
  1870.1 305.1 %reduce-scatter.46.cloned.1.call-start = ((), (), s32[]{:S(2)}) async-start(), calls=%async_computation.40 | async-start | bytes 1179648 | tf_op jit(solution)/shard_map/reduce_scatter | solution.py:395
  1875.0 340.0 %reduce-scatter.40.cloned.1.call-start = ((), (), s32[]{:S(2)}) async-start(), calls=%async_computation.37 | async-start | bytes 1179648 | tf_op jit(solution)/shard_map/reduce_scatter | solution.py:392
  1879.6 415.1 %reduce-scatter.30.cloned.1.call-start = ((), (), s32[]{:S(2)}) async-start(), calls=%async_computation.32 | async-start | bytes 5242880 | tf_op jit(solution)/shard_map/reduce_scatter | solution.py:340
  1884.6 450.6 %reduce-scatter.38.cloned.1.call-start = ((), (), s32[]{:S(2)}) async-start(), calls=%async_computation.36 | async-start | bytes 1179648 | tf_op jit(solution)/shard_map/reduce_scatter | solution.py:391
  1890.2 485.0 %reduce-scatter.32.cloned.1.call-start = ((), (), s32[]{:S(2)}) async-start(), calls=%async_computation.33 | async-start | bytes 1179648 | tf_op jit(solution)/shard_map/reduce_scatter | solution.py:388
  1894.9 520.4 %reduce-scatter.34.cloned.1.call-start = ((), (), s32[]{:S(2)}) async-start(), calls=%async_computation.34 | async-start | bytes 1179648 | tf_op jit(solution)/shard_map/reduce_scatter | solution.py:389
  1899.7 555.5 %reduce-scatter.36.cloned.1.call-start = ((), (), s32[]{:S(2)}) async-start(), calls=%async_computation.35 | async-start | bytes 1179648 | tf_op jit(solution)/shard_map/reduce_scatter | solution.py:390
  (159 other events, 5694.1 us)
Sparse Core Ops, SparseCore 0:
  14.1 83.4 all-gather.9
  200.4 144.7 reduce-scatter.17
  346.7 46.6 all-gather.13
  395.4 79.4 all-gather.11
  528.1 142.9 reduce-scatter.19
  1213.0 81.3 all-gather.23
  1381.9 143.0 reduce-scatter.25
Sparse Core Ops, SparseCore 1:
  530.4 35.0 all-gather.17
  676.5 81.3 all-gather.15
  759.3 79.1 all-gather.21
  840.3 35.8 all-gather.19
  913.5 144.4 reduce-scatter.23
  1060.4 145.1 reduce-scatter.21
  1534.0 81.3 all-gather.25
  1618.4 34.5 reduce-scatter.41
  1656.0 35.9 reduce-scatter.43
  1840.5 143.0 reduce-scatter.27
  1987.5 72.4 reduce-scatter.47
  2064.5 71.1 reduce-scatter.49
  2139.3 35.9 reduce-scatter.45
  2179.0 35.9 reduce-scatter.39
  2217.8 76.7 reduce-scatter.29
  2298.7 36.3 reduce-scatter.37
  2339.2 35.9 reduce-scatter.31
  2379.3 35.9 reduce-scatter.33
  2419.2 35.9 reduce-scatter.35
where the time goes:
time: 2470 us; the launch traced here: 2460 us
  waiting for transfers between devices  1560 us (63%)
  matrix products  466 us (19%)
  blocking collectives  150 us (6%)
  other arithmetic  147 us (6%)
  local copies, waits for them, and re-layouts  63.3 us (3%)
  loops' own time  57.7 us (2%)
    reduce_scatter x3, waiting for transfers between devices, sum_rows(): lax.psum_scatter(partial_value, 'tensor', scatter_dimension=0, tiled=True)  431 us
    all_gather x3, waiting for transfers between devices, gather_grads(): return lax.all_gather(grad_low, 'tensor', axis=0, tiled=True)  185 us
    reduce_scatter x2, waiting for transfers between devices, sum_grads(): lax.psum_scatter(partial_value, 'tensor', scatter_dimension=0, tiled=True)  179 us
    all_gather x2, waiting for transfers between devices, gather_rows(): return lax.all_gather(normed, 'tensor', axis=0, tiled=True)  157 us
    reduce_scatter x1, waiting for transfers between devices, on_device(): lax.psum_scatter(outer_cols(grad_query_two, cross_query_all), 'tensor', s...  143 us
    reduce_scatter x1, waiting for transfers between devices, on_device(): lax.psum_scatter(outer_cols(grad_keys_two, cross_key_all) + outer_cols(gr...  79.7 us
    reduce_scatter x1, waiting for transfers between devices, on_device(): lax.psum_scatter(down_weight_grad, 'dp', scatter_dimension=1, tiled=True)  75.6 us
    dot_general x10, matrix products, inner_rows(): lax.dot_general(left, right, (((0,), (0,)), ((), ())), preferred_element_...  64.3 us
  transfers between devices with their start and end apart: 26, of which 22 were waited for; matrix products, arithmetic and copies ran while one was open for 16% of the time, Pallas kernels for 0%

commit v1 on v0

v1 whole, which is shorter than its diff:
```python
import functools
import jax
import jax.numpy as jnp
from jax import lax
from jax.experimental import pallas as pl
from jax.experimental.pallas import tpu as pltpu
from jax.sharding import Mesh, PartitionSpec as P

HEAD_DIM = 64
SEG = 128
PAIR = 2 * HEAD_DIM
LOG2E = 1.4426950408889634
SCALE = HEAD_DIM ** -0.5
NEG = -1e30
f32, bf16 = jnp.float32, jnp.bfloat16
VMEM_LIMIT = 56 * 1024 * 1024


def dot(a, b, ca=1, cb=0):
    return lax.dot_general(a, b, (((ca,), (cb,)), ((), ())), preferred_element_type=f32)


def stack_heads(x):
    lane = lax.broadcasted_iota(jnp.int32, x.shape, 1)
    zero = jnp.zeros_like(x)
    return jnp.concatenate(
        [jnp.where(lane < HEAD_DIM, x, zero), jnp.where(lane >= HEAD_DIM, x, zero)], axis=0
    )


def unstack_heads(xt):
    n = xt.shape[1] // 2
    return jnp.concatenate([xt[:HEAD_DIM, :n], xt[HEAD_DIM:, n:]], axis=0).T


def forward_chunk(k, v, qT, bias, m, l, acc):
    s = dot(k, qT) * (SCALE * LOG2E)
    if bias is not None:
        s = bias(s)
    if m is None:
        m_new = jnp.max(s, axis=0, keepdims=True)
        p = jnp.exp2(s - m_new)
        l = jnp.sum(p, axis=0, keepdims=True)
        acc[...] = dot(v, p.astype(bf16), 0, 0)
    else:
        m_new = jnp.maximum(m, jnp.max(s, axis=0, keepdims=True))
        p = jnp.exp2(s - m_new)
        fade = jnp.exp2(m - m_new)
        l = l * fade + jnp.sum(p, axis=0, keepdims=True)
        acc[...] = acc[...] * fade + dot(v, p.astype(bf16), 0, 0)
    return m_new, l


def self_forward_kernel(plan, q_ref, k_ref, v_ref, bias_ref, o_ref, lse_ref, acc, *, rows, chunk):
    segs = chunk // SEG
    qT = stack_heads(q_ref[...]).T
    wide = 2 * rows

    def own_bias(a):
        def apply(s):
            key = lax.broadcasted_iota(jnp.int32, (chunk, wide), 0) + a * chunk
            query = lax.broadcasted_iota(jnp.int32, (chunk, wide), 1) & (rows - 1)
            b = jnp.concatenate(
                [jnp.broadcast_to(bias_ref[a * segs + j : a * segs + j + 1, :], (SEG, wide)) for j in range(segs)], 0)
            return jnp.where(key <= query, s + b, NEG)
        return apply

    m = l = None
    for a in range(rows // chunk):
        m, l = forward_chunk(
            k_ref[a * chunk : (a + 1) * chunk, :], v_ref[a * chunk : (a + 1) * chunk, :], qT, own_bias(a), m, l, acc)

    def step(i, carry):
        m, l = carry
        places = [plan[1 + i * segs + j] for j in range(segs)]
        brows = [plan[1 + plan.shape[0] // 2 + i * segs + j] for j in range(segs)]
        k = jnp.concatenate([k_ref[pl.ds(pl.multiple_of(p * SEG, SEG), SEG), :] for p in places], 0)
        v = jnp.concatenate([v_ref[pl.ds(pl.multiple_of(p * SEG, SEG), SEG), :] for p in places], 0)

        def apply(s):
            b = jnp.concatenate([jnp.broadcast_to(bias_ref[pl.ds(p, 1), :], (SEG, wide)) for p in brows], 0)
            return s + b
        return forward_chunk(k, v, qT, apply, m, l, acc)

    m, l = lax.fori_loop(0, plan[0], step, (m, l))
    o_ref[...] = unstack_heads(acc[...] * (1.0 / l)).astype(bf16)
    lse_ref[0] = m + jnp.log2(l)


def self_forward(plan, q, k, v, bias, chunk=256):
    rows, total = q.shape[0], k.shape[0]
    pairs = q.shape[1] // PAIR
    return pl.pallas_call(
        functools.partial(self_forward_kernel, rows=rows, chunk=chunk),
        grid_spec=pltpu.PrefetchScalarGridSpec(
            num_scalar_prefetch=1,
            grid=(pairs,),
            in_specs=[
                pl.BlockSpec((rows, PAIR), lambda h, p: (0, h)),
                pl.BlockSpec((total, PAIR), lambda h, p: (0, h)),
                pl.BlockSpec((total, PAIR), lambda h, p: (0, h)),
                pl.BlockSpec(bias.shape, lambda h, p: (0, 0)),
            ],
            out_specs=[
                pl.BlockSpec((rows, PAIR), lambda h, p: (0, h)),
                pl.BlockSpec((1, 1, 2 * rows), lambda h, p: (h, 0, 0)),
            ],
            scratch_shapes=[pltpu.VMEM((PAIR, 2 * rows), f32)],
        ),
        out_shape=[
            jax.ShapeDtypeStruct(q.shape, bf16),
            jax.ShapeDtypeStruct((pairs, 1, 2 * rows), f32),
        ],
        compiler_params=pltpu.CompilerParams(vmem_limit_bytes=VMEM_LIMIT),
        cost_estimate=pl.CostEstimate(flops=8 * rows * total * q.shape[1], bytes_accessed=4 * q.size + 4 * k.size, transcendentals=0),
        name="self_forward",
    )(plan, q, k, v, bias)


def cross_forward_kernel(length, q_ref, k_ref, v_ref, o_ref, lse_ref, acc, *, rows, chunk, sure):
    qT = stack_heads(q_ref[...]).T
    total = k_ref.shape[0]
    m = l = None
    for a in range(total // chunk):
        def apply(s, a=a):
            key = lax.broadcasted_iota(jnp.int32, s.shape, 0) + a * chunk
            return jnp.where(key < length[0], s, NEG)
        m, l = forward_chunk(
            k_ref[a * chunk : (a + 1) * chunk, :], v_ref[a * chunk : (a + 1) * chunk, :], qT,
            apply if (a + 1) * chunk > sure else None, m, l, acc)
    o_ref[...] = unstack_heads(acc[...] * (1.0 / l)).astype(bf16)
    lse_ref[0] = m + jnp.log2(l)


def cross_forward(length, q, k, v, sure, chunk=256):
    rows, total = q.shape[0], k.shape[0]
    pairs = q.shape[1] // PAIR
    return pl.pallas_call(
        functools.partial(cross_forward_kernel, rows=rows, chunk=chunk, sure=sure),
        grid_spec=pltpu.PrefetchScalarGridSpec(
            num_scalar_prefetch=1,
            grid=(pairs,),
            in_specs=[
                pl.BlockSpec((rows, PAIR), lambda h, p: (0, h)),
                pl.BlockSpec((total, PAIR), lambda h, p: (0, h)),
                pl.BlockSpec((total, PAIR), lambda h, p: (0, h)),
            ],
            out_specs=[
                pl.BlockSpec((rows, PAIR), lambda h, p: (0, h)),
                pl.BlockSpec((1, 1, 2 * rows), lambda h, p: (h, 0, 0)),
            ],
            scratch_shapes=[pltpu.VMEM((PAIR, 2 * rows), f32)],
        ),
        out_shape=[
            jax.ShapeDtypeStruct(q.shape, bf16),
            jax.ShapeDtypeStruct((pairs, 1, 2 * rows), f32),
        ],
        compiler_params=pltpu.CompilerParams(vmem_limit_bytes=VMEM_LIMIT),
        cost_estimate=pl.CostEstimate(flops=16 * rows * total * q.shape[1], bytes_accessed=4 * q.size + 4 * k.size, transcendentals=0),
        name="cross_forward",
    )(length, q, k, v)


def backward_chunk(k, v, qst, qT, dost, doT, lse, delta, bias, dqT, first):
    s = dot(k, qT) * (SCALE * LOG2E)
    if bias is not None:
        s = bias(s)
    p = jnp.exp2(s - lse)
    ds = (p * (dot(v, doT) - delta)).astype(bf16)
    dv = dot(p.astype(bf16), dost)
    dk = dot(ds, qst) * SCALE
    part = dot(k, ds, 0, 0)
    if first:
        dqT[...] = part
    else:
        dqT[...] += part
    return dk.astype(bf16), dv.astype(bf16)


def backward_setup(q_ref, o_ref, do_ref):
    qst = stack_heads(q_ref[...])
    dost = stack_heads(do_ref[...])
    qT, doT = qst.T, dost.T
    oT = o_ref[...].T.astype(f32)
    oT2 = jnp.concatenate([oT, oT], axis=1)
    delta = jnp.sum(doT.astype(f32) * oT2, axis=0, keepdims=True)
    return qst, qT, dost, doT, delta


def self_backward_kernel(plan, q_ref, k_ref, v_ref, o_ref, do_ref, lse_ref, bias_ref, dq_ref, dk_ref, dv_ref, dqT, *, rows, chunk):
    segs = chunk // SEG
    wide = 2 * rows
    qst, qT, dost, doT, delta = backward_setup(q_ref, o_ref, do_ref)
    lse = lse_ref[0]
    dqT[...] = jnp.zeros_like(dqT)
    dk_ref[rows:, :] = jnp.zeros((dk_ref.shape[0] - rows, PAIR), bf16)
    dv_ref[rows:, :] = jnp.zeros((dv_ref.shape[0] - rows, PAIR), bf16)

    def step(i, carry):
        places = [pl.multiple_of(plan[1 + i * segs + j] * SEG, SEG) for j in range(segs)]
        brows = [plan[1 + plan.shape[0] // 2 + i * segs + j] for j in range(segs)]
        k = jnp.concatenate([k_ref[pl.ds(p, SEG), :] for p in places], 0)
        v = jnp.concatenate([v_ref[pl.ds(p, SEG), :] for p in places], 0)

        def apply(s):
            b = jnp.concatenate([jnp.broadcast_to(bias_ref[pl.ds(p, 1), :], (SEG, wide)) for p in brows], 0)
            return s + b
        dk, dv = backward_chunk(k, v, qst, qT, dost, doT, lse, delta, apply, dqT, False)
        for j in range(segs):
            dk_ref[pl.ds(places[j], SEG), :] = dk[j * SEG : (j + 1) * SEG]
            dv_ref[pl.ds(places[j], SEG), :] = dv[j * SEG : (j + 1) * SEG]
        return carry

    lax.fori_loop(0, plan[0], step, 0)

    for a in range(rows // chunk):
        def apply(s, a=a):
            key = lax.broadcasted_iota(jnp.int32, (chunk, wide), 0) + a * chunk
            query = lax.broadcasted_iota(jnp.int32, (chunk, wide), 1) & (rows - 1)
            b = jnp.concatenate(
                [jnp.broadcast_to(bias_ref[a * segs + j : a * segs + j + 1, :], (SEG, wide)) for j in range(segs)], 0)
            return jnp.where(key <= query, s + b, NEG)
        sl = slice(a * chunk, (a + 1) * chunk)
        dk, dv = backward_chunk(k_ref[sl, :], v_ref[sl, :], qst, qT, dost, doT, lse, delta, apply, dqT, False)
        dk_ref[sl, :] = dk
        dv_ref[sl, :] = dv
    dq_ref[...] = (unstack_heads(dqT[...]) * SCALE).astype(bf16)


def self_backward(plan, q, k, v, o, do, lse, bias, chunk=256):
    rows, total = q.shape[0], k.shape[0]
    pairs = q.shape[1] // PAIR
    qs = pl.BlockSpec((rows, PAIR), lambda h, p: (0, h))
    ks = pl.BlockSpec((total, PAIR), lambda h, p: (0, h))
    return pl.pallas_call(
        functools.partial(self_backward_kernel, rows=rows, chunk=chunk),
        grid_spec=pltpu.PrefetchScalarGridSpec(
            num_scalar_prefetch=1,
            grid=(pairs,),
            in_specs=[qs, ks, ks, qs, qs,
                pl.BlockSpec((1, 1, 2 * rows), lambda h, p: (h, 0, 0)),
                pl.BlockSpec(bias.shape, lambda h, p: (0, 0)),
            ],
            out_specs=[qs, ks, ks],
            scratch_shapes=[pltpu.VMEM((PAIR, 2 * rows), f32)],
        ),
        out_shape=[jax.ShapeDtypeStruct(q.shape, bf16), jax.ShapeDtypeStruct(k.shape, bf16), jax.ShapeDtypeStruct(k.shape, bf16)],
        compiler_params=pltpu.CompilerParams(vmem_limit_bytes=VMEM_LIMIT),
        cost_estimate=pl.CostEstimate(flops=20 * rows * total * q.shape[1], bytes_accessed=8 * q.size + 8 * k.size, transcendentals=0),
        name="self_backward",
    )(plan, q, k, v, o, do, lse, bias)


def cross_backward_kernel(length, q_ref, k_ref, v_ref, o_ref, do_ref, lse_ref, dq_ref, dk_ref, dv_ref, dqT, *, rows, chunk, sure):
    qst, qT, dost, doT, delta = backward_setup(q_ref, o_ref, do_ref)
    lse = lse_ref[0]
    for a in range(k_ref.shape[0] // chunk):
        def apply(s, a=a):
            key = lax.broadcasted_iota(jnp.int32, s.shape, 0) + a * chunk
            return jnp.where(key < length[0], s, NEG)
        sl = slice(a * chunk, (a + 1) * chunk)
        dk, dv = backward_chunk(k_ref[sl, :], v_ref[sl, :], qst, qT, dost, doT, lse, delta,
                                apply if (a + 1) * chunk > sure else None, dqT, a == 0)
        dk_ref[sl, :] = dk
        dv_ref[sl, :] = dv
    dq_ref[...] = (unstack_heads(dqT[...]) * SCALE).astype(bf16)


def cross_backward(length, q, k, v, o, do, lse, sure, chunk=256):
    rows, total = q.shape[0], k.shape[0]
    pairs = q.shape[1] // PAIR
    qs = pl.BlockSpec((rows, PAIR), lambda h, p: (0, h))
    ks = pl.BlockSpec((total, PAIR), lambda h, p: (0, h))
    return pl.pallas_call(
        functools.partial(cross_backward_kernel, rows=rows, chunk=chunk, sure=sure),
        grid_spec=pltpu.PrefetchScalarGridSpec(
            num_scalar_prefetch=1,
            grid=(pairs,),
            in_specs=[qs, ks, ks, qs, qs, pl.BlockSpec((1, 1, 2 * rows), lambda h, p: (h, 0, 0))],
            out_specs=[qs, ks, ks],
            scratch_shapes=[pltpu.VMEM((PAIR, 2 * rows), f32)],
        ),
        out_shape=[jax.ShapeDtypeStruct(q.shape, bf16), jax.ShapeDtypeStruct(k.shape, bf16), jax.ShapeDtypeStruct(k.shape, bf16)],
        compiler_params=pltpu.CompilerParams(vmem_limit_bytes=VMEM_LIMIT),
        cost_estimate=pl.CostEstimate(flops=40 * rows * total * q.shape[1], bytes_accessed=8 * q.size + 8 * k.size, transcendentals=0),
        name="cross_backward",
    )(length, q, k, v, o, do, lse)


ERFC = (0.254829592, -0.284496736, 1.421413741, -1.453152027, 1.061405429)


def gelu_pair(v):
    e = jnp.exp2(v * v * (-0.5 * LOG2E))
    t = 1.0 / (1.0 + jnp.abs(v) * (0.3275911 * 0.7071067811865476))
    a1, a2, a3, a4, a5 = (0.5 * a for a in ERFC)
    tail = ((((a5 * t + a4) * t + a3) * t + a2) * t + a1) * t * e
    cdf = jnp.where(v >= 0.0, 1.0 - tail, tail)
    return v * cdf, cdf + v * e * 0.3989422804014327


def feed_forward_kernel(r_ref, g_ref, w_ref, ub_ref, out_ref, back_ref, inner_ref, grad_ref):
    hidden, width = w_ref.shape[0] * w_ref.shape[2], w_ref.shape[3]
    up = w_ref[:, 0].reshape(hidden, width)
    down = w_ref[:, 1].reshape(hidden, width)
    lifted = dot(r_ref[...], up, 1, 1) + ub_ref[...]
    grad_inner = dot(g_ref[...], down, 1, 1)
    value, slope = gelu_pair(lifted)
    inner = value.astype(bf16)
    grad = (grad_inner * slope).astype(bf16)
    inner_ref[...] = inner
    grad_ref[...] = grad
    back_ref[...] = dot(grad, up).astype(bf16)
    out_ref[...] = dot(inner, down).astype(bf16)


def feed_forward(r, g, weights, ub, tile=512):
    rows, width = r.shape
    hidden = weights.shape[0] * weights.shape[2]
    row = pl.BlockSpec((tile, width), lambda i: (i, 0))
    tall = pl.BlockSpec((tile, hidden), lambda i: (i, 0))
    return pl.pallas_call(
        feed_forward_kernel,
        grid=(rows // tile,),
        in_specs=[
            row,
            row,
            pl.BlockSpec(weights.shape, lambda i: (0, 0, 0, 0)),
            pl.BlockSpec(ub.shape, lambda i: (0, 0)),
        ],
        out_specs=[row, row, tall, tall],
        out_shape=[
            jax.ShapeDtypeStruct((rows, width), bf16),
            jax.ShapeDtypeStruct((rows, width), bf16),
            jax.ShapeDtypeStruct((rows, hidden), bf16),
            jax.ShapeDtypeStruct((rows, hidden), bf16),
        ],
        compiler_params=pltpu.CompilerParams(vmem_limit_bytes=VMEM_LIMIT),
        cost_estimate=pl.CostEstimate(
            flops=8 * rows * width * hidden,
            bytes_accessed=12 * rows * width + 2 * weights.size,
            transcendentals=0,
        ),
        name="feed_forward",
    )(r, g, weights, ub)


EPSILON = 1e-05


def normed(rows, gain, shift):
    average = jnp.mean(rows, axis=-1, keepdims=True)
    centered = rows - average
    variance = jnp.mean(centered * centered, axis=-1, keepdims=True)
    return (centered * lax.rsqrt(variance + EPSILON) * gain + shift).astype(bf16)


def norm_back(rows, gain, grad):
    average = jnp.mean(rows, axis=-1, keepdims=True)
    centered = rows - average
    scale = lax.rsqrt(jnp.mean(centered * centered, axis=-1, keepdims=True) + EPSILON)
    xhat = centered * scale
    scaled = grad * gain
    back = scale * (
        scaled
        - jnp.mean(scaled, axis=-1, keepdims=True)
        - xhat * jnp.mean(scaled * xhat, axis=-1, keepdims=True)
    )
    return back, jnp.sum(grad * xhat, axis=0), jnp.sum(grad, axis=0)


def column_sums(matrix):
    return jnp.sum(matrix.astype(f32), axis=0)


def flip(x, k, size):
    return lax.ppermute(x, "low", [(i, i ^ k) for i in range(size)])


def gather_low(x, size):
    if size != 8:
        return [x if k == 0 else flip(x, k, size) for k in range(size)]
    half = x.shape[0] // 2
    first, second = x[:half], x[half:]
    x0, y1 = flip(first, 2, size), flip(second, 4, size)
    x1, y0 = flip(second, 2, size), flip(first, 4, size)
    xy0, xy1 = flip(x0, 4, size), flip(y1, 2, size)
    even = [
        x,
        jnp.concatenate([x0, x1], 0),
        jnp.concatenate([y0, y1], 0),
        jnp.concatenate([xy0, xy1], 0),
    ]
    odd = [flip(e, 1, size) for e in even]
    return [p for pair in zip(even, odd) for p in pair]


def scatter_low(pieces, size):
    if size != 8:
        total = pieces[0].astype(f32)
        for k in range(1, size):
            total = total + flip(pieces[k], k, size).astype(f32)
        return total
    even = [
        (pieces[k].astype(f32) + flip(pieces[k + 1], 1, size).astype(f32)) for k in (6, 4, 2, 0)
    ]
    back = [flip(e.astype(bf16), k, size).astype(f32) for e, k in zip(even[:3], (6, 4, 2))]
    return even[3] + back[0] + back[1] + back[2]


def arrange(pieces, low, axis):
    count, extent = len(pieces), pieces[0].shape[axis]
    shape = list(pieces[0].shape)
    shape[axis] = count * extent
    whole = jnp.zeros(shape, pieces[0].dtype)
    for k, piece in enumerate(pieces):
        whole = lax.dynamic_update_slice_in_dim(whole, piece, (low ^ k) * extent, axis)
    return whole


def gather_tensor(x, size, place, axis):
    shape = list(x.shape)
    extent = shape[axis]
    shape[axis] = extent * size
    whole = lax.dynamic_update_slice_in_dim(jnp.zeros(shape, x.dtype), x, place * extent, axis)
    for k in range(1, size):
        got = lax.ppermute(x, "tensor", [(i, (i + k) % size) for i in range(size)])
        whole = lax.dynamic_update_slice_in_dim(
            whole, got, lax.rem(place + size - k, size) * extent, axis
        )
    return whole


def gather_weights(shards, sizes, low, place):
    wide = gather_tensor(jnp.stack(shards), sizes[2], place, 2)
    rows = wide.shape[1]
    pieces = gather_low(wide.transpose(1, 0, 2).reshape(rows, -1), sizes[1])
    matrices = arrange(pieces, low, 0)
    if sizes[0] > 1:
        matrices = lax.all_gather(matrices, "high", axis=0, tiled=True)
    width = wide.shape[2]
    return [matrices[:, i * width : (i + 1) * width] for i in range(len(shards))]


def scatter_weights(grads, sizes, low, place):
    count, width = len(grads), grads[0].shape[1]
    stacked = jnp.concatenate([g.astype(bf16) for g in grads], axis=1)
    if sizes[0] > 1:
        stacked = lax.psum_scatter(stacked, "high", scatter_dimension=0, tiled=True)
    extent = stacked.shape[0] // sizes[1]
    pieces = [
        lax.dynamic_slice_in_dim(stacked, (low ^ k) * extent, extent, 0) for k in range(sizes[1])
    ]
    mine = scatter_low(pieces, sizes[1]).astype(bf16)
    mine = mine.reshape(extent, count, sizes[2], width // sizes[2]).transpose(2, 1, 0, 3)
    parts = lax.all_to_all(mine, "tensor", split_axis=0, concat_axis=0, tiled=True)
    total = jnp.sum(parts.astype(f32), axis=0)
    return [total[i] for i in range(count)]


def path_plan(parents, place, own, blocks):
    count = parents.shape[0]
    labels = jnp.arange(count)
    table = (
        (labels[:, None] == labels[None, :])
        | ((parents[:, None] == labels[None, :]) & (labels[:, None] > 0))
    ).astype(f32)
    reach = 1
    while reach < count:
        table = jnp.minimum(jnp.dot(table, table), 1.0)
        reach *= 2
    slots = jnp.arange(blocks * own)
    back, inside = slots // own, slots % own
    segment = (place - back) * own + inside
    pick = (labels[:, None] == segment[None, :]).astype(f32)
    mine = (labels[None, :] == (place * own + jnp.arange(own))[:, None]).astype(f32)
    seen = jnp.dot(jnp.dot(mine, table), pick)
    needed = jnp.any(seen > 0.5, axis=0) & (back > 0)
    rank = jnp.cumsum(needed.astype(jnp.int32)) - 1
    total = jnp.sum(needed.astype(jnp.int32))
    steps = jnp.arange(slots.shape[0])
    chosen = needed[None, :] & (rank[None, :] == steps[:, None])
    order = jnp.sum(jnp.where(chosen, slots[None, :], 0), axis=1)
    rows = jnp.where(steps < total, order, slots.shape[0])
    lanes = jnp.arange(2 * own * SEG)
    spread = (((lanes // SEG) % own)[None, :] == jnp.arange(own)[:, None]).astype(f32)
    bias = jnp.where(jnp.dot(seen.T, spread) > 0.5, 0.0, NEG)
    bias = jnp.concatenate([bias, jnp.full((8, bias.shape[1]), NEG, f32)], axis=0)
    per_step = CHUNK // SEG
    plan = jnp.concatenate([((total + per_step - 1) // per_step)[None], order, jnp.zeros((1,), jnp.int32), rows])
    return plan.astype(jnp.int32), bias


CHUNK = 512


def on_device(sizes, sure):
    high, low_size, size = sizes

    def run(
        tokens,
        encoded,
        parents,
        source_lengths,
        cotangent,
        first_gain,
        first_shift,
        self_query,
        self_query_bias,
        self_key,
        self_value,
        self_value_bias,
        self_out,
        self_out_bias,
        second_gain,
        second_shift,
        cross_query,
        cross_query_bias,
        cross_key,
        cross_value,
        cross_value_bias,
        cross_out,
        cross_out_bias,
        third_gain,
        third_shift,
        up_weight,
        up_bias,
        down_weight,
        down_bias,
    ):
        low = lax.axis_index("low")
        place = lax.axis_index("tensor")
        rows, width = tokens.shape
        up_chain = [(i, i + 1) for i in range(size - 1)]
        down_chain = [(i + 1, i) for i in range(size - 1)]

        blocks = [tokens]
        for _ in range(size - 1):
            blocks.append(lax.ppermute(blocks[-1], "tensor", up_chain))
        wq, wk, wv = gather_weights([self_query, self_key, self_value], sizes, low, place)
        wo, xq, xk, xv, xo = gather_weights(
            [self_out.T, cross_query, cross_key, cross_value, cross_out.T], sizes, low, place
        )
        source = lax.all_gather(encoded, "tensor", axis=0, tiled=True)
        both = jnp.stack([up_weight.T, down_weight])
        both = lax.all_to_all(both, "low", split_axis=1, concat_axis=2, tiled=True)
        if high > 1:
            both = lax.all_gather(both, "high", axis=2, tiled=True)
        hidden = both.shape[1]
        lifts = lax.all_gather(both[None], "tensor", axis=0, tiled=True)
        ub = lax.all_gather(
            lax.dynamic_slice_in_dim(up_bias, low * hidden, hidden, 0), "tensor", axis=0, tiled=True
        )
        biases = lax.all_gather(
            jnp.stack([self_query_bias, self_value_bias, cross_query_bias, cross_value_bias]),
            "tensor", axis=1, tiled=True,
        )
        q_bias, v_bias, xq_bias, xv_bias = [biases[i] for i in range(4)]
        cots = gather_low(cotangent, low_size)
        plan, bias = path_plan(parents[0], place, rows // SEG, size)

        tokens_f = tokens.astype(f32)
        one = normed(jnp.concatenate(blocks, 0).astype(f32), first_gain, first_shift)
        own = one[:rows]
        q1 = (dot(own, wq) + q_bias).astype(bf16)
        k1 = dot(one, wk).astype(bf16)
        v1 = (dot(one, wv) + v_bias).astype(bf16)
        mixed_one, lse_one = self_forward(plan, q1, k1, v1, bias, CHUNK)
        hidden_one = tokens_f + dot(mixed_one, wo, 1, 1) + self_out_bias
        two = normed(hidden_one, second_gain, second_shift)
        q2 = (dot(two, xq) + xq_bias).astype(bf16)
        k2 = dot(source, xk).astype(bf16)
        v2 = (dot(source, xv) + xv_bias).astype(bf16)
        mixed_two, lse_two = cross_forward(source_lengths, q2, k2, v2, sure, CHUNK)
        hidden_two = hidden_one + dot(mixed_two, xo, 1, 1) + cross_out_bias
        three = normed(hidden_two, third_gain, third_shift)

        threes = gather_low(three, low_size)
        outs, backs, inners, lifted_grads = [], [], [], []
        for k in range(0, low_size, 2):
            r = jnp.concatenate(threes[k : k + 2], 0)
            g = jnp.concatenate(cots[k : k + 2], 0)
            out, back, inner, grad = feed_forward(r, g, lifts, ub[None])
            outs += [out[:rows], out[rows:]]
            backs += [back[:rows], back[rows:]]
            inners.append((inner, g))
            lifted_grads.append((grad, r))
        grad_three = scatter_low(backs, low_size)
        block_out = hidden_two + scatter_low(outs, low_size) + down_bias
        up_bias_part = sum(column_sums(grad) for grad, _ in lifted_grads)
        up_grad = sum(dot(grad, r, 0, 0) for grad, r in lifted_grads)
        down_grad = sum(dot(inner, g, 0, 0) for inner, g in inners)
        lift_grads = jnp.stack(
            [up_grad.reshape(size, hidden, width), down_grad.reshape(size, hidden, width)], 1
        ).astype(bf16)
        lift_grads = lax.psum_scatter(lift_grads, "tensor", scatter_dimension=0, tiled=True)[0]
        if high > 1:
            lift_grads = lax.psum_scatter(lift_grads, "high", scatter_dimension=2, tiled=True)
        lift_grads = lax.all_to_all(lift_grads, "low", split_axis=2, concat_axis=1, tiled=True)
        up_weight_grad = lift_grads[0].T.astype(f32)
        down_weight_grad = lift_grads[1].astype(f32)

        down_bias_grad = column_sums(cotangent)
        back, third_gain_grad, third_shift_grad = norm_back(hidden_two, third_gain, grad_three)
        grad_hidden_two = cotangent.astype(f32) + back
        grad_two = grad_hidden_two.astype(bf16)
        cross_out_bias_grad = column_sums(grad_two)
        xo_grad = dot(grad_two, mixed_two, 0, 0)
        do2 = dot(grad_two, xo).astype(bf16)
        dq2, dk2, dv2 = cross_backward(
            source_lengths, q2, k2, v2, mixed_two, do2, lse_two, sure, CHUNK
        )
        xq_grad = dot(two, dq2, 0, 0)
        xk_grad = dot(source, dk2, 0, 0)
        xv_grad = dot(source, dv2, 0, 0)
        encoded_grad = lax.psum_scatter(
            (dot(dk2, xk, 1, 1) + dot(dv2, xv, 1, 1)).astype(bf16),
            "tensor", scatter_dimension=0, tiled=True,
        ).astype(f32)
        back, second_gain_grad, second_shift_grad = norm_back(
            hidden_one, second_gain, dot(dq2, xq, 1, 1)
        )
        grad_hidden_one = grad_hidden_two + back
        grad_one = grad_hidden_one.astype(bf16)
        self_out_bias_grad = column_sums(grad_one)
        wo_grad = dot(grad_one, mixed_one, 0, 0)
        do1 = dot(grad_one, wo).astype(bf16)
        dq1, dk1, dv1 = self_backward(plan, q1, k1, v1, mixed_one, do1, lse_one, bias, CHUNK)
        wq_grad = dot(own, dq1, 0, 0)
        wk_grad = dot(one, dk1, 0, 0)
        wv_grad = dot(one, dv1, 0, 0)
        shares = dot(dk1, wk, 1, 1) + dot(dv1, wv, 1, 1)
        share = shares[(size - 1) * rows :]
        for r in range(size - 2, -1, -1):
            got = lax.ppermute(share.astype(bf16), "tensor", down_chain)
            share = shares[r * rows : (r + 1) * rows] + got.astype(f32)
        grad_rows = share + dot(dq1, wq, 1, 1)
        back, first_gain_grad, first_shift_grad = norm_back(tokens_f, first_gain, grad_rows)
        tokens_grad = grad_hidden_one + back

        wo_g, xq_g, xk_g, xv_g, xo_g = scatter_weights(
            [wo_grad, xq_grad, xk_grad, xv_grad, xo_grad], sizes, low, place
        )
        wq_g, wk_g, wv_g = scatter_weights([wq_grad, wk_grad, wv_grad], sizes, low, place)

        spread = jnp.zeros((size, up_bias.shape[0]), f32)
        spread = lax.dynamic_update_slice(
            spread, up_bias_part.reshape(size, hidden), (0, low * hidden)
        )
        vectors = [
            first_gain_grad,
            first_shift_grad,
            second_gain_grad,
            second_shift_grad,
            third_gain_grad,
            third_shift_grad,
            self_out_bias_grad,
            cross_out_bias_grad,
            down_bias_grad,
            column_sums(dq1),
            column_sums(dv1),
            column_sums(dq2),
            column_sums(dv2),
            spread.reshape(-1),
        ]
        summed = lax.psum(jnp.concatenate(vectors), ("high", "low", "tensor"))
        small = [summed[i * width : (i + 1) * width] for i in range(13)]
        part = width // size
        split = [lax.dynamic_slice_in_dim(s, place * part, part, 0) for s in small[9:]]
        up_bias_grad = lax.dynamic_slice_in_dim(
            summed[13 * width :], place * up_bias.shape[0], up_bias.shape[0], 0
        )
        return (
            block_out.astype(bf16),
            tokens_grad,
            encoded_grad,
            small[0],
            small[1],
            wq_g,
            split[0],
            wk_g,
            wv_g,
            split[1],
            wo_g.T,
            small[6],
            small[2],
            small[3],
            xq_g,
            split[2],
            xk_g,
            xv_g,
            split[3],
            xo_g.T,
            small[7],
            small[4],
            small[5],
            up_weight_grad,
            up_bias_grad,
            down_weight_grad,
            small[8],
        )

    return run


def solution(mesh):
    dp, size = mesh.shape["dp"], mesh.shape["tensor"]
    low = min(8, dp)
    sizes = (dp // low, low, size)
    fine = Mesh(mesh.devices.reshape(sizes), ("high", "low", "tensor"))
    depth = ("high", "low")
    rows = P((*depth, "tensor"), None)
    block, turned = P(depth, "tensor"), P("tensor", depth)
    part, whole = P("tensor"), P()
    placed = (
        rows, rows, P(depth, None), P(depth), rows, whole, whole,
        block, part, block, block, part, turned, whole, whole, whole,
        block, part, block, block, part, turned, whole, whole, whole,
        block, part, turned, whole,
    )
    out = (
        rows, rows, rows, whole, whole,
        block, part, block, block, part, turned, whole, whole, whole,
        block, part, block, block, part, turned, whole, whole, whole,
        block, part, turned, whole,
    )
    return jax.shard_map(
        on_device(sizes, 768), mesh=fine, in_specs=placed, out_specs=out, check_vma=False
    )
```

time: 2470 us -> 1170 us (0.47)
  waiting for transfers between devices: 1560 us -> 375 us
  matrix products: 466 us -> 163 us
  local copies, waits for them, and re-layouts: 63.3 us -> 200 us
  Pallas kernels: 0 us -> 129 us
  starting transfers between devices: 1.58 us -> 121 us
  blocking collectives: 150 us -> 60.2 us
  loops' own time: 57.7 us -> 0 us
  other arithmetic: 147 us -> 93.7 us
    reduce_scatter x17 -> x1, waiting for transfers between devices: 1170 us -> 42.8 us  [run(): lax.psum_scatter((dot(dk2, xk, 1, 1) + dot(dv2, xv, 1, 1)).astype(bf16),...]
    all_gather x9 -> x2, waiting for transfers between devices: 382 us -> 0.01 us  [the longest x1 0.01 us: run(): source = lax.all_gather(encoded, 'tensor', axis=0, tiled=True)]
    dot_general x94 -> x37, matrix products: 466 us -> 163 us  [the longest x32 162 us: dot(): lax.dot_general(a, b, (((ca,), (cb,)), ((), ())), preferred_element_type=...]
    ppermute x0 -> x80, waiting for transfers between devices: none -> 273 us  [the longest x68 186 us: flip(): return lax.ppermute(x, 'low', [(i, i ^ k) for i in range(size)])]
    pallas_call x0 -> x8, Pallas kernels: none -> 129 us  [the longest x4 57 us: feed_forward(): pl.pallas_call(feed_forward_kernel, grid=(rows // tile,), in_specs=[row,...]
    ppermute x0 -> x80, starting transfers between devices: none -> 70.9 us  [the longest x68 40.1 us: flip(): return lax.ppermute(x, 'low', [(i, i ^ k) for i in range(size)])]
    psum x2 -> x0, blocking collectives: 67.8 us -> none  [the longest x1 42.4 us: on_device(): lax.psum((first_gain_grad, first_shift_grad, second_gain_grad, second_shi...]
    another operation x5 -> x0, loops' own time: 57.7 us -> none  [the longest x1 29.6 us: ancestors(): return lax.fori_loop(1, count, extend, jnp.eye(count, dtype=jnp.float32))]
  transfers between devices with their start and end apart: 26 -> 89, of which waited for: 22 -> 28; matrix products, arithmetic and copies ran while one was open for 16% -> 37% of each run, Pallas kernels for 0% -> 9%
where the time goes in v1:
time: 1170 us; the launch traced here: 1160 us
  waiting for transfers between devices  375 us (32%)
  local copies, waits for them, and re-layouts  200 us (17%)
  matrix products  163 us (14%)
  Pallas kernels  129 us (11%)
  starting transfers between devices  121 us (10%)
  other arithmetic  93.7 us (8%)
  blocking collectives  60.2 us (5%)
  between operations  17.3 us (1%)
    ppermute x68, waiting for transfers between devices, flip(): return lax.ppermute(x, 'low', [(i, i ^ k) for i in range(size)])  186 us
    dot_general x32, matrix products, dot(): lax.dot_general(a, b, (((ca,), (cb,)), ((), ())), preferred_element_type=...  162 us
    ppermute x3, waiting for transfers between devices, run(): got = lax.ppermute(share.astype(bf16), 'tensor', down_chain)  64.8 us
    pallas_call x4, Pallas kernels, feed_forward(): pl.pallas_call(feed_forward_kernel, grid=(rows // tile,), in_specs=[row,...  57 us
    psum x1, waiting for transfers between devices, run(): summed = lax.psum(jnp.concatenate(vectors), ('high', 'low', 'tensor'))  55.8 us
    reduce_scatter x1, waiting for transfers between devices, run(): lax.psum_scatter((dot(dk2, xk, 1, 1) + dot(dv2, xv, 1, 1)).astype(bf16),...  42.8 us
    unnamed x246, local copies, waits for them, and re-layouts  42.4 us
    all_to_all x2, starting transfers between devices, scatter_weights(): lax.all_to_all(mine, 'tensor', split_axis=0, concat_axis=0, tiled=True)  41.2 us
  transfers between devices with their start and end apart: 89, of which 28 were waited for; matrix products, arithmetic and copies ran while one was open for 37% of the time, Pallas kernels for 9%

profile of v1, /device:TPU:0, one launch (start us, length us, event | category | flops | bytes accessed | tf_op | source)
XLA Modules:
  0.0 1158.8 jit_solution(1560403711614004257)
XLA Ops:
  46.5 20.4 %all-gather = f32[4,1,256]{2,1,0:T(1,128)} all-gather(f32[1,1,256]{2,1,0:T(1,128)S(1)} %bitcast.183), channel_id=1, replica_groups=mesh['dp'=8,'tensor'=4] {'tensor'}, dimensions={0}, use_global_device_ids=true | all-gather | bytes 5120 | tf_op jit(solution)/shard_map/all_gather | solution.py:551
  68.0 39.8 %all_gather.12 = f32[4,1024]{1,0:T(4,128)S(1)} all-gather(f32[4,256]{1,0:T(4,128)S(1)} %pad_maximum_fusion.12), channel_id=1, replica_groups=mesh['dp'=8,'tensor'=4] {'tensor'}, dimensions={1}, use_global_device_ids=true | all-gather | bytes 20480 | tf_op jit(solution)/shard_map/all_gather | solution.py:554
  304.2 12.8 %collective-permute-done.1 = bf16[512,1024]{1,0:T(8,128)(2,1)S(1)} collective-permute-done((bf16[512,1024]{1,0:T(8,128)(2,1)}, bf16[512,1024]{1,0:T(8,128)(2,1)S(1)}, u32[]{:S(2)}, u32[]{:S(2)}) %collective-permute-start.1) | collective-permute-done | bytes 1048608 | tf_op jit(solution)/shard_map/ppermute | solution.py:539
  378.9 11.9 %self_forward.1 = (bf16[512,1024]{1,0:T(8,128)(2,1)}, f32[8,1,1024]{2,1,0:T(1,128)}) custom-call(s32[34]{0:T(128)} %pad_add_fusion.plan, bf16[512,1024]{1,0:T(8,128)(2,1)} %add_convert_fusion.19.q_ref, bf16[2048,1024]{1,0:T(8,128)(2,1)} %convolution_convert_fusion.k_ref, bf16[2048,1024]{1,0:T(8,128)(2,1)} %add_convert_fusion.v_ref, ...), custom_call_target="tpu_custom_call" | custom-call | flops 8589934592 | bytes 10485760 | tf_op jit(solution)/shard_map/self_forward/pallas_call | solution.py:93
  410.8 17.0 %cross_forward.1 = (bf16[512,1024]{1,0:T(8,128)(2,1)}, f32[8,1,1024]{2,1,0:T(1,128)}) custom-call(s32[1]{0:T(128)S(6)} %copy.381.length, bf16[512,1024]{1,0:T(8,128)(2,1)} %add_convert_fusion.17.q_ref, bf16[1024,1024]{1,0:T(8,128)(2,1)} %convert_bitcast_fusion.k_ref, bf16[1024,1024]{1,0:T(8,128)(2,1)} %fusion.18.v_ref), custom_call_target="tpu_custom_call" | custom-call | flops 8589934592 | bytes 6291456 | tf_op jit(solution)/shard_map/cross_forward/pallas_call | solution.py:138
  475.2 14.4 %feed_forward.4 = (bf16[1024,1024]{1,0:T(8,128)(2,1)}, bf16[1024,1024]{1,0:T(8,128)(2,1)}, bf16[1024,1024]{1,0:T(8,128)(2,1)}, bf16[1024,1024]{1,0:T(8,128)(2,1)}) custom-call(bf16[1024,1024]{1,0:T(8,128)(2,1)} %pad_maximum_fusion.3.r_ref, bf16[1024,1024]{1,0:T(8,128)(2,1)} %constant_dynamic-update-slice_fusion.17.g_ref, ...), custom_call_target="tpu_custom_call" | custom-call | flops 8589934592 | bytes 16777216 | tf_op jit(solution)/shard_map/feed_forward/pallas_call | solution.py:322
  496.1 14.0 %feed_forward.5 = (bf16[1024,1024]{1,0:T(8,128)(2,1)}, bf16[1024,1024]{1,0:T(8,128)(2,1)}, bf16[1024,1024]{1,0:T(8,128)(2,1)}, bf16[1024,1024]{1,0:T(8,128)(2,1)}) custom-call(bf16[1024,1024]{1,0:T(8,128)(2,1)} %constant_dynamic-update-slice_fusion.19.r_ref, bf16[1024,1024]{1,0:T(8,128)(2,1)} %copy-done.59, ...), custom_call_target="tpu_custom_call" | custom-call | flops 8589934592 | bytes 16777216 | tf_op jit(solution)/shard_map/feed_forward/pallas_call | solution.py:322
  514.1 14.2 %feed_forward.7 = (bf16[1024,1024]{1,0:T(8,128)(2,1)}, bf16[1024,1024]{1,0:T(8,128)(2,1)}, bf16[1024,1024]{1,0:T(8,128)(2,1)}, bf16[1024,1024]{1,0:T(8,128)(2,1)}) custom-call(bf16[1024,1024]{1,0:T(8,128)(2,1)} %copy-done.61, bf16[1024,1024]{1,0:T(8,128)(2,1)} %copy-done.57, bf16[4,2,256,1024]{3,2,1,0:T(8,128)(2,1)} %all-gather.6.cloned.1.call-done.w_ref, ...), custom_call_target="tpu_custom_call" | custom-call | flops 8589934592 | bytes 16777216 | tf_op jit(solution)/shard_map/feed_forward/pallas_call | solution.py:322
  540.4 14.4 %feed_forward.6 = (bf16[1024,1024]{1,0:T(8,128)(2,1)}, bf16[1024,1024]{1,0:T(8,128)(2,1)}, bf16[1024,1024]{1,0:T(8,128)(2,1)}, bf16[1024,1024]{1,0:T(8,128)(2,1)}) custom-call(bf16[1024,1024]{1,0:T(8,128)(2,1)} %copy-done.53, bf16[1024,1024]{1,0:T(8,128)(2,1)} %constant_dynamic-update-slice_fusion.28.g_ref, ...), custom_call_target="tpu_custom_call" | custom-call | flops 8589934592 | bytes 16777216 | tf_op jit(solution)/shard_map/feed_forward/pallas_call | solution.py:322
  609.2 12.6 %collective-permute-done.58 = bf16[512,1024]{1,0:T(8,128)(2,1)} collective-permute-done((bf16[512,1024]{1,0:T(8,128)(2,1)S(1)}, bf16[512,1024]{1,0:T(8,128)(2,1)}, u32[]{:S(2)}, u32[]{:S(2)}) %collective-permute-start.58) | collective-permute-done | bytes 1048608 | tf_op jit(solution)/shard_map/ppermute | solution.py:377
  622.3 22.1 %collective-permute-done.62 = bf16[512,1024]{1,0:T(8,128)(2,1)} collective-permute-done((bf16[512,1024]{1,0:T(8,128)(2,1)S(1)}, bf16[512,1024]{1,0:T(8,128)(2,1)}, u32[]{:S(2)}, u32[]{:S(2)}) %collective-permute-start.62) | collective-permute-done | bytes 1048608 | tf_op jit(solution)/shard_map/ppermute | solution.py:377
  651.6 15.1 %collective-permute-done.43 = bf16[512,1024]{1,0:T(8,128)(2,1)} collective-permute-done((bf16[512,1024]{1,0:T(8,128)(2,1)}, bf16[512,1024]{1,0:T(8,128)(2,1)}, u32[]{:S(2)}, u32[]{:S(2)}) %collective-permute-start.43) | collective-permute-done | bytes 1048608 | tf_op jit(solution)/shard_map/ppermute | solution.py:377
  666.7 21.8 %collective-permute-done.55 = bf16[512,1024]{1,0:T(8,128)(2,1)} collective-permute-done((bf16[512,1024]{1,0:T(8,128)(2,1)}, bf16[512,1024]{1,0:T(8,128)(2,1)}, u32[]{:S(2)}, u32[]{:S(2)}) %collective-permute-start.55) | collective-permute-done | bytes 1048608 | tf_op jit(solution)/shard_map/ppermute | solution.py:377
  696.7 24.8 %cross_backward.1 = (bf16[512,1024]{1,0:T(8,128)(2,1)}, bf16[1024,1024]{1,0:T(8,128)(2,1)}, bf16[1024,1024]{1,0:T(8,128)(2,1)}) custom-call(s32[1]{0:T(128)S(6)} %copy.381.length, bf16[512,1024]{1,0:T(8,128)(2,1)} %add_convert_fusion.17.q_ref, bf16[1024,1024]{1,0:T(8,128)(2,1)} %convert_bitcast_fusion.k_ref, bf16[1024,1024]{1,0:T(8,128)(2,1)} %fusion.18.v_ref, ...), custom_call_target="tpu_custom_call" | custom-call | flops 21474836480 | bytes 12582912 | tf_op jit(solution)/shard_map/cross_backward/pallas_call | solution.py:274
  729.7 18.4 %self_backward.1 = (bf16[512,1024]{1,0:T(8,128)(2,1)}, bf16[2048,1024]{1,0:T(8,128)(2,1)}, bf16[2048,1024]{1,0:T(8,128)(2,1)}) custom-call(s32[34]{0:T(128)} %pad_add_fusion.plan, bf16[512,1024]{1,0:T(8,128)(2,1)} %add_convert_fusion.19.q_ref, bf16[2048,1024]{1,0:T(8,128)(2,1)} %convolution_convert_fusion.k_ref, bf16[2048,1024]{1,0:T(8,128)(2,1)} %add_convert_fusion.v_ref, ...), custom_call_target="tpu_custom_call" | custom-call | flops 21474836480 | bytes 20971520 | tf_op jit(solution)/shard_map/self_backward/pallas_call | solution.py:235
  778.1 12.2 %pad_maximum_fusion = bf16[1024,3072]{0,1:T(8,128)(2,1)S(1)} fusion(bf16[1024,1024]{0,1:T(8,128)(2,1)S(1)} %copy-done.38, bf16[1024,1024]{0,1:T(8,128)(2,1)S(1)} %copy-done.39, bf16[1024,1024]{0,1:T(8,128)(2,1)S(1)} %convolution_convert_fusion.3), kind=kLoop, calls=%fused_computation.10 | loop fusion | flops 18874368 | bytes 12582912 | tf_op jit(solution)/shard_map/concatenate | solution.py:447
  827.6 23.6 %collective-permute-done.63 = bf16[512,1024]{1,0:T(8,128)(2,1)} collective-permute-done((bf16[512,1024]{1,0:T(8,128)(2,1)S(1)}, bf16[512,1024]{1,0:T(8,128)(2,1)}, u32[]{:S(2)}, u32[]{:S(2)}) %collective-permute-start.63) | collective-permute-done | bytes 1048608 | tf_op jit(solution)/shard_map/ppermute | solution.py:635
  859.1 41.2 %collective-permute-done.64 = bf16[512,1024]{1,0:T(8,128)(2,1)S(1)} collective-permute-done((bf16[512,1024]{1,0:T(8,128)(2,1)S(1)}, bf16[512,1024]{1,0:T(8,128)(2,1)S(1)}, u32[]{:S(2)}, u32[]{:S(2)}) %collective-permute-start.64) | collective-permute-done | bytes 1048608 | tf_op jit(solution)/shard_map/ppermute | solution.py:635
  910.4 11.5 collective-permute-done.68
  923.2 15.4 %collective-permute-done.72 = bf16[128,3072]{0,1:T(8,128)(2,1)S(1)} collective-permute-done((bf16[128,3072]{0,1:T(8,128)(2,1)}, bf16[128,3072]{0,1:T(8,128)(2,1)S(1)}, u32[]{:S(2)}, u32[]{:S(2)}) %collective-permute-start.72) | collective-permute-done | bytes 786464 | tf_op jit(solution)/shard_map/ppermute | solution.py:377
  943.0 21.3 %all-to-all-start.1 = ((bf16[4,3,128,256]{2,3,1,0:T(8,128)(2,1)}), bf16[4,3,128,256]{2,3,1,0:T(8,128)(2,1)}, u32[]{:S(2)}, u32[]{:S(2)}) async-start(bf16[4,3,128,256]{2,3,1,0:T(8,128)(2,1)} %bitcast.163), calls=%async_computation.2 | async-start | bytes 1572864 | tf_op jit(solution)/shard_map/all_to_all | solution.py:456
  1006.3 20.0 %all-to-all-start.2 = ((bf16[4,5,128,256]{2,3,1,0:T(8,128)(2,1)}), bf16[4,5,128,256]{2,3,1,0:T(8,128)(2,1)}, u32[]{:S(2)}, u32[]{:S(2)}) async-start(bf16[4,5,128,256]{2,3,1,0:T(8,128)(2,1)} %bitcast.155), calls=%async_computation.3 | async-start | bytes 2621440 | tf_op jit(solution)/shard_map/all_to_all | solution.py:456
  1041.3 55.8 %all-reduce.5.cloned.1.call-done = f32[21504]{0:T(1024)} async-done(((f32[21504]{0:T(1024)}), f32[21504]{0:T(1024)}) %all-reduce.5.cloned.1.call-update) | async-done | bytes 86032 | tf_op jit(solution)/shard_map/psum | solution.py:666
  1102.4 42.8 %reduce-scatter.5.cloned.1.call-done = bf16[256,1024]{1,0:T(8,128)(2,1)} async-done(((bf16[1024,1024]{1,0:T(8,128)(2,1)}), bf16[256,1024]{1,0:T(8,128)(2,1)}) %reduce-scatter.5.cloned.1.call-update) | async-done | bytes 524304 | tf_op jit(solution)/shard_map/reduce_scatter | solution.py:616
  (630 shorter events, 623.9 us)
Async XLA Ops:
  7.2 392.2 %all-gather.4.cloned.1.call-start = ((), (), s32[]{:S(2)}) async-start(), calls=%async_computation.5 | async-start | bytes 2621440 | tf_op jit(solution)/shard_map/all_gather | solution.py:544
  12.0 120.7 %collective-permute-start.18 = (bf16[5,128,256]{1,2,0:T(8,128)(2,1)S(1)}, bf16[5,128,256]{1,2,0:T(8,128)(2,1)}, u32[]{:S(2)}, u32[]{:S(2)}) collective-permute-start(bf16[5,128,256]{1,2,0:T(8,128)(2,1)S(1)} %constant_dynamic-update-slice_fusion.6), channel_id=1, source_target_pairs={{0,3},{1,0},{2,1},{3,2},{4,7},{5,4},{6,5},{7,6},{8,11},{9,8},{10,9... | collective-permute-start | bytes 983048 | tf_op jit(solution)/shard_map/ppermute | solution.py:427
  17.1 113.1 %collective-permute-start.17 = (bf16[5,128,256]{1,2,0:T(8,128)(2,1)S(1)}, bf16[5,128,256]{1,2,0:T(8,128)(2,1)}, u32[]{:S(2)}, u32[]{:S(2)}) collective-permute-start(bf16[5,128,256]{1,2,0:T(8,128)(2,1)S(1)} %constant_dynamic-update-slice_fusion.6), channel_id=1, source_target_pairs={{0,2},{1,3},{2,0},{3,1},{4,6},{5,7},{6,4},{7,5},{8,10},{9,11},{10,... | collective-permute-start | bytes 983048 | tf_op jit(solution)/shard_map/ppermute | solution.py:427
  17.1 111.5 %collective-permute-start.16 = (bf16[5,128,256]{1,2,0:T(8,128)(2,1)S(1)}, bf16[5,128,256]{1,2,0:T(8,128)(2,1)}, u32[]{:S(2)}, u32[]{:S(2)}) collective-permute-start(bf16[5,128,256]{1,2,0:T(8,128)(2,1)S(1)} %constant_dynamic-update-slice_fusion.6), channel_id=1, source_target_pairs={{0,1},{1,2},{2,3},{3,0},{4,5},{5,6},{6,7},{7,4},{8,9},{9,10},{10,1... | collective-permute-start | bytes 983048 | tf_op jit(solution)/shard_map/ppermute | solution.py:427
  21.8 92.5 %collective-permute-start.4 = (bf16[3,128,256]{1,2,0:T(8,128)(2,1)}, bf16[3,128,256]{1,2,0:T(8,128)(2,1)}, u32[]{:S(2)}, u32[]{:S(2)}) collective-permute-start(bf16[3,128,256]{1,2,0:T(8,128)(2,1)} %get-tuple-element.292), channel_id=1, source_target_pairs={{0,2},{1,3},{2,0},{3,1},{4,6},{5,7},{6,4},{7,5},{8,10},{9,11},{10,... | collective-permute-start | bytes 589832 | tf_op jit(solution)/shard_map/ppermute | solution.py:427
  23.8 85.8 %collective-permute-start.3 = (bf16[3,128,256]{1,2,0:T(8,128)(2,1)}, bf16[3,128,256]{1,2,0:T(8,128)(2,1)}, u32[]{:S(2)}, u32[]{:S(2)}) collective-permute-start(bf16[3,128,256]{1,2,0:T(8,128)(2,1)} %get-tuple-element.292), channel_id=1, source_target_pairs={{0,1},{1,2},{2,3},{3,0},{4,5},{5,6},{6,7},{7,4},{8,9},{9,10},{10,1... | collective-permute-start | bytes 589832 | tf_op jit(solution)/shard_map/ppermute | solution.py:427
  35.1 152.4 %all-to-all-start = ((bf16[2,2048,128]{2,0,1:T(2,128)(2,1)}), bf16[2,2048,128]{2,0,1:T(2,128)(2,1)}, u32[]{:S(2)}, u32[]{:S(2)}) async-start(bf16[2,2048,128]{2,0,1:T(2,128)(2,1)} %copy.273), calls=%async_computation | async-start | bytes 2097152 | tf_op jit(solution)/shard_map/all_to_all | solution.py:546
  39.4 435.8 %all-gather.6.cloned.1.call-start = ((), (), s32[]{:S(2)}) async-start(), calls=%async_computation.6 | async-start | bytes 5242880 | tf_op jit(solution)/shard_map/all_gather | solution.py:550
  132.7 111.2 %collective-permute-start.30 = (bf16[512,1024]{1,0:T(8,128)(2,1)}, bf16[512,1024]{1,0:T(8,128)(2,1)}, u32[]{:S(2)}, u32[]{:S(2)}) collective-permute-start(bf16[512,1024]{1,0:T(8,128)(2,1)} %param.33), channel_id=1, source_target_pairs={{0,4},{4,0},{8,12},{12,8},{16,20},{20,16},{24,28},{28,24},{1,5},{5... | collective-permute-start | bytes 3145736 | tf_op jit(solution)/shard_map/ppermute | solution.py:377
  146.8 143.7 %collective-permute-start = (bf16[512,1024]{1,0:T(8,128)(2,1)S(1)}, bf16[512,1024]{1,0:T(8,128)(2,1)}, u32[]{:S(2)}, u32[]{:S(2)}) collective-permute-start(bf16[512,1024]{1,0:T(8,128)(2,1)S(1)} %copy-done), channel_id=1, source_target_pairs={{0,1},{1,2},{2,3},{4,5},{5,6},{6,7},{8,9},{9,10},{10,11},{12,13},{... | collective-permute-start | bytes 3145736 | tf_op jit(solution)/shard_map/ppermute | solution.py:539
  192.7 787.3 %all-reduce.7.cloned.1.call-start = ((), (), s32[]{:S(2)}) async-start(), calls=%async_computation.9 | async-start | bytes 8388608
  241.6 192.8 %collective-permute-start.47 = (bf16[512,1024]{1,0:T(8,128)(2,1)}, bf16[512,1024]{1,0:T(8,128)(2,1)}, u32[]{:S(2)}, u32[]{:S(2)}) collective-permute-start(bf16[512,1024]{1,0:T(8,128)(2,1)} %pad_maximum_fusion.8), channel_id=1, source_target_pairs={{0,4},{4,0},{8,12},{12,8},{16,20},{20,16},{24,28},{28,24},{1,5},{5... | collective-permute-start | bytes 3145736 | tf_op jit(solution)/shard_map/ppermute | solution.py:377
  246.7 190.5 %collective-permute-start.53 = (bf16[512,1024]{1,0:T(8,128)(2,1)}, bf16[512,1024]{1,0:T(8,128)(2,1)}, u32[]{:S(2)}, u32[]{:S(2)}) collective-permute-start(bf16[512,1024]{1,0:T(8,128)(2,1)} %pad_maximum_fusion.10), channel_id=1, source_target_pairs={{0,4},{4,0},{8,12},{12,8},{16,20},{20,16},{24,28},{28,24},{1,5},{5... | collective-permute-start | bytes 3145736 | tf_op jit(solution)/shard_map/ppermute | solution.py:377
  317.0 132.2 %collective-permute-start.41 = (bf16[512,1024]{1,0:T(8,128)(2,1)}, bf16[512,1024]{1,0:T(8,128)(2,1)}, u32[]{:S(2)}, u32[]{:S(2)}) collective-permute-start(bf16[512,1024]{1,0:T(8,128)(2,1)} %pad_maximum_fusion.6), channel_id=1, source_target_pairs={{0,4},{4,0},{8,12},{12,8},{16,20},{20,16},{24,28},{28,24},{1,5},{5... | collective-permute-start | bytes 3145736 | tf_op jit(solution)/shard_map/ppermute | solution.py:377
  513.6 76.4 %collective-permute-start.57 = (bf16[512,1024]{1,0:T(8,128)(2,1)}, bf16[512,1024]{1,0:T(8,128)(2,1)}, u32[]{:S(2)}, u32[]{:S(2)}) collective-permute-start(bf16[512,1024]{1,0:T(8,128)(2,1)} %slice.246), channel_id=1, source_target_pairs={{0,4},{4,0},{8,12},{12,8},{16,20},{20,16},{24,28},{28,24},{1,5},{5... | collective-permute-start | bytes 3145736 | tf_op jit(solution)/shard_map/ppermute | solution.py:377
  514.1 80.5 %collective-permute-start.42 = (bf16[512,1024]{1,0:T(8,128)(2,1)}, bf16[512,1024]{1,0:T(8,128)(2,1)}, u32[]{:S(2)}, u32[]{:S(2)}) collective-permute-start(bf16[512,1024]{1,0:T(8,128)(2,1)} %slice.238), channel_id=1, source_target_pairs={{0,4},{4,0},{8,12},{12,8},{16,20},{20,16},{24,28},{28,24},{1,5},{5... | collective-permute-start | bytes 3145736 | tf_op jit(solution)/shard_map/ppermute | solution.py:377
  621.7 66.8 %collective-permute-start.55 = (bf16[512,1024]{1,0:T(8,128)(2,1)}, bf16[512,1024]{1,0:T(8,128)(2,1)}, u32[]{:S(2)}, u32[]{:S(2)}) collective-permute-start(bf16[512,1024]{1,0:T(8,128)(2,1)} %add_convert_fusion.13), channel_id=1, source_target_pairs={{0,8},{4,12},{8,0},{12,4},{16,24},{20,28},{24,16},{28,20},{1,9},{5... | collective-permute-start | bytes 3145736 | tf_op jit(solution)/shard_map/ppermute | solution.py:377
  793.1 62.3 %collective-permute-start.67 = (bf16[128,3072]{0,1:T(8,128)(2,1)}, bf16[128,3072]{0,1:T(8,128)(2,1)}, u32[]{:S(2)}, u32[]{:S(2)}) collective-permute-start(bf16[128,3072]{0,1:T(8,128)(2,1)} %get-tuple-element.268), channel_id=1, source_target_pairs={{0,4},{4,0},{8,12},{12,8},{16,20},{20,16},{24,28},{28,24},{1,5},{5... | collective-permute-start | bytes 2359304 | tf_op jit(solution)/shard_map/ppermute | solution.py:377
  818.1 84.8 %collective-permute-start.78 = (bf16[128,5120]{0,1:T(8,128)(2,1)}, bf16[128,5120]{0,1:T(8,128)(2,1)S(1)}, u32[]{:S(2)}, u32[]{:S(2)}) collective-permute-start(bf16[128,5120]{0,1:T(8,128)(2,1)} %get-tuple-element.259), channel_id=1, source_target_pairs={{0,4},{4,0},{8,12},{12,8},{16,20},{20,16},{24,28},{28,24},{1,5},{5... | collective-permute-start | bytes 3932168 | tf_op jit(solution)/shard_map/ppermute | solution.py:377
  910.4 80.4 %collective-permute-start.73 = (bf16[128,5120]{0,1:T(8,128)(2,1)}, bf16[128,5120]{0,1:T(8,128)(2,1)}, u32[]{:S(2)}, u32[]{:S(2)}) collective-permute-start(bf16[128,5120]{0,1:T(8,128)(2,1)} %get-tuple-element.258), channel_id=1, source_target_pairs={{0,4},{4,0},{8,12},{12,8},{16,20},{20,16},{24,28},{28,24},{1,5},{5... | collective-permute-start | bytes 3932168 | tf_op jit(solution)/shard_map/ppermute | solution.py:377
  922.0 68.9 %collective-permute-start.75 = (bf16[128,5120]{0,1:T(8,128)(2,1)}, bf16[128,5120]{0,1:T(8,128)(2,1)}, u32[]{:S(2)}, u32[]{:S(2)}) collective-permute-start(bf16[128,5120]{0,1:T(8,128)(2,1)} %get-tuple-element.262), channel_id=1, source_target_pairs={{0,24},{4,28},{8,16},{12,20},{16,8},{20,12},{24,0},{28,4},{1,25},{... | collective-permute-start | bytes 3932168 | tf_op jit(solution)/shard_map/ppermute | solution.py:377
  964.2 132.9 %all-reduce.5.cloned.1.call-start = ((), (), s32[]{:S(2)}) async-start(), calls=%async_computation.8 | async-start | bytes 172032 | tf_op jit(solution)/shard_map/psum | solution.py:666
  971.7 173.5 %reduce-scatter.5.cloned.1.call-start = ((), (), s32[]{:S(2)}) async-start(), calls=%async_computation.7 | async-start | bytes 2621440 | tf_op jit(solution)/shard_map/reduce_scatter | solution.py:616
  1006.3 141.1 %all-to-all-start.2 = ((bf16[4,5,128,256]{2,3,1,0:T(8,128)(2,1)}), bf16[4,5,128,256]{2,3,1,0:T(8,128)(2,1)}, u32[]{:S(2)}, u32[]{:S(2)}) async-start(bf16[4,5,128,256]{2,3,1,0:T(8,128)(2,1)} %bitcast.155), calls=%async_computation.3 | async-start | bytes 2621440 | tf_op jit(solution)/shard_map/all_to_all | solution.py:456
  (164 other events, 2996.0 us)
Sparse Core Ops, SparseCore 0:
  25.4 66.5 all-gather.3
  192.8 80.8 all-gather.5
  647.8 177.5 all-reduce.6
  971.8 125.2 all-reduce.4
  1099.4 45.7 reduce-scatter.4

commit v2 on v1

v2 whole, which is shorter than its diff:
```python
import functools

import jax
import jax.numpy as jnp
from jax import lax
from jax.experimental import pallas as pl
from jax.experimental.pallas import tpu as pltpu
from jax.sharding import Mesh, PartitionSpec as P

HEAD_DIM = 64
SEG = 128
PAIR = 2 * HEAD_DIM
EPSILON = 1e-05
LOG2E = 1.4426950408889634
SCALE = HEAD_DIM ** -0.5
NEG = -1e30
CHUNK = 512
VMEM_LIMIT = 56 * 1024 * 1024
f32, bf16 = jnp.float32, jnp.bfloat16


def dot(a, b, ca=1, cb=0):
    return lax.dot_general(a, b, (((ca,), (cb,)), ((), ())), preferred_element_type=f32)


def cost(flops, moved):
    return pl.CostEstimate(flops=int(flops), bytes_accessed=int(moved), transcendentals=0)


def params():
    return pltpu.CompilerParams(vmem_limit_bytes=VMEM_LIMIT)


def move(name, scalars, sources, outs, plan):
    count = len(plan([0] * scalars.shape[0]))

    def kernel(scalars_ref, *refs):
        ins, dests, sems = refs[: len(sources)], refs[len(sources) : -1], refs[-1]
        values = [scalars_ref[i] for i in range(scalars.shape[0])]
        copies = [
            pltpu.make_async_copy(ins[a].at[ai], dests[b].at[bi], sems.at[n])
            for n, (a, ai, b, bi) in enumerate(plan(values))
        ]
        for copy in copies:
            copy.start()
        for copy in copies:
            copy.wait()

    anywhere = pl.BlockSpec(memory_space=pl.ANY)
    return pl.pallas_call(
        kernel,
        in_specs=[pl.BlockSpec(memory_space=pltpu.SMEM)]
        + [pl.BlockSpec(memory_space=pltpu.VMEM)] * len(sources),
        out_specs=[anywhere] * len(outs),
        out_shape=[jax.ShapeDtypeStruct(s, bf16) for s in outs],
        scratch_shapes=[pltpu.SemaphoreType.DMA((count,))],
        compiler_params=params(),
        cost_estimate=cost(0, 4 * sum(x.size for x in sources)),
        name=name,
    )(scalars, *sources)


def at(start, extent):
    return pl.ds(start if isinstance(start, int) else pl.multiple_of(start, extent), extent)


def stack_heads(x):
    lane = lax.broadcasted_iota(jnp.int32, x.shape, 1)
    zero = jnp.zeros_like(x)
    return jnp.concatenate(
        [jnp.where(lane < HEAD_DIM, x, zero), jnp.where(lane >= HEAD_DIM, x, zero)], axis=0
    )


def unstack_heads(xt):
    n = xt.shape[1] // 2
    return jnp.concatenate([xt[:HEAD_DIM, :n], xt[HEAD_DIM:, n:]], axis=0).T


def segment_bias(bias_ref, block, s, causal):
    keys, wide = s.shape
    segs = keys // SEG
    b = jnp.concatenate(
        [
            jnp.broadcast_to(bias_ref[block * segs + j : block * segs + j + 1, :], (SEG, wide))
            for j in range(segs)
        ],
        0,
    )
    s = s + b
    if causal:
        key = lax.broadcasted_iota(jnp.int32, s.shape, 0)
        query = lax.broadcasted_iota(jnp.int32, s.shape, 1) & (wide // 2 - 1)
        s = jnp.where(key <= query, s, NEG)
    return s


def forward_step(k, v, qT, mask, m_ref, l_ref, acc, first):
    s = mask(dot(k, qT) * (SCALE * LOG2E))
    top = jnp.max(s, axis=0, keepdims=True)
    if first:
        p = jnp.exp2(s - top)
        m_ref[...] = top
        l_ref[...] = jnp.sum(p, axis=0, keepdims=True)
        acc[...] = dot(v, p.astype(bf16), 0, 0)
    else:
        m = jnp.maximum(m_ref[...], top)
        p = jnp.exp2(s - m)
        fade = jnp.exp2(m_ref[...] - m)
        m_ref[...] = m
        l_ref[...] = l_ref[...] * fade + jnp.sum(p, axis=0, keepdims=True)
        acc[...] = acc[...] * fade + dot(v, p.astype(bf16), 0, 0)


def forward_finish(o_ref, lse_ref, m_ref, l_ref, acc):
    o_ref[...] = unstack_heads(acc[...] * (1.0 / l_ref[...])).astype(bf16)
    lse_ref[0] = m_ref[...] + jnp.log2(l_ref[...])


def self_forward(place, q, ks, vs, bias, blocks, state, final):
    rows, count = q.shape[0], len(blocks)
    pairs = q.shape[1] // PAIR
    given = 0 if state is None else 3

    def kernel(place_ref, q_ref, *refs):
        k_refs, v_refs, bias_ref = refs[:count], refs[count : 2 * count], refs[2 * count]
        before = refs[2 * count + 1 : 2 * count + 1 + given]
        outs = refs[2 * count + 1 + given :]
        if final:
            o_ref, lse_ref, m_ref, l_ref, acc = outs
        else:
            m_out, l_out, acc_out, m_ref, l_ref, acc = outs
        if given:
            m_ref[...], l_ref[...], acc[...] = before[0][0], before[1][0], before[2][0]
        qT = stack_heads(q_ref[...]).T
        for n, r in enumerate(blocks):
            def step(n=n, r=r):
                forward_step(
                    k_refs[n][...], v_refs[n][...], qT,
                    lambda s: segment_bias(bias_ref, r, s, r == 0), m_ref, l_ref, acc, r == 0,
                )
            if r == 0:
                step()
            else:
                pl.when(place_ref[0] >= r)(step)
        if final:
            forward_finish(o_ref, lse_ref, m_ref, l_ref, acc)
        else:
            m_out[0], l_out[0], acc_out[0] = m_ref[...], l_ref[...], acc[...]

    col = pl.BlockSpec((rows, PAIR), lambda h, p: (0, h))
    line = pl.BlockSpec((1, 1, 2 * rows), lambda h, p: (h, 0, 0))
    slab = pl.BlockSpec((1, PAIR, 2 * rows), lambda h, p: (h, 0, 0))
    lines = jax.ShapeDtypeStruct((pairs, 1, 2 * rows), f32)
    slabs = jax.ShapeDtypeStruct((pairs, PAIR, 2 * rows), f32)
    stat = pltpu.VMEM((1, 2 * rows), f32)
    return pl.pallas_call(
        kernel,
        grid_spec=pltpu.PrefetchScalarGridSpec(
            num_scalar_prefetch=1,
            grid=(pairs,),
            in_specs=[col] * (1 + 2 * count)
            + [pl.BlockSpec(bias.shape, lambda h, p: (0, 0))]
            + [line, line, slab][:given],
            out_specs=[col, line] if final else [line, line, slab],
            scratch_shapes=[stat, stat, pltpu.VMEM((PAIR, 2 * rows), f32)],
        ),
        out_shape=[jax.ShapeDtypeStruct(q.shape, bf16), lines] if final else [lines, lines, slabs],
        compiler_params=params(),
        cost_estimate=cost(16 * count * rows * q.size, 4 * q.size * (1 + count)),
        name="self_forward",
    )(place, q, *[ks[r] for r in blocks], *[vs[r] for r in blocks], bias, *(state or ()))


def cross_forward(length, q, k, v, sure):
    rows, total = q.shape[0], k.shape[0]
    pairs = q.shape[1] // PAIR

    def kernel(length_ref, q_ref, k_ref, v_ref, o_ref, lse_ref, m_ref, l_ref, acc):
        qT = stack_heads(q_ref[...]).T
        for a in range(0, total, CHUNK):
            sl = slice(a, a + CHUNK)
            forward_step(
                k_ref[sl, :], v_ref[sl, :], qT,
                lambda s: length_mask(length_ref, s, a, sure), m_ref, l_ref, acc, a == 0,
            )
        forward_finish(o_ref, lse_ref, m_ref, l_ref, acc)

    col = pl.BlockSpec((rows, PAIR), lambda h, p: (0, h))
    tall = pl.BlockSpec((total, PAIR), lambda h, p: (0, h))
    stat = pltpu.VMEM((1, 2 * rows), f32)
    return pl.pallas_call(
        kernel,
        grid_spec=pltpu.PrefetchScalarGridSpec(
            num_scalar_prefetch=1,
            grid=(pairs,),
            in_specs=[col, tall, tall],
            out_specs=[col, pl.BlockSpec((1, 1, 2 * rows), lambda h, p: (h, 0, 0))],
            scratch_shapes=[stat, stat, pltpu.VMEM((PAIR, 2 * rows), f32)],
        ),
        out_shape=[
            jax.ShapeDtypeStruct(q.shape, bf16),
            jax.ShapeDtypeStruct((pairs, 1, 2 * rows), f32),
        ],
        compiler_params=params(),
        cost_estimate=cost(16 * total * q.size, 4 * q.size + 4 * k.size),
        name="cross_forward",
    )(length, q, k, v)


def length_mask(length_ref, s, start, sure):
    if start + s.shape[0] <= sure:
        return s
    key = lax.broadcasted_iota(jnp.int32, s.shape, 0) + start
    return jnp.where(key < length_ref[0], s, NEG)


def backward_setup(q_ref, o_ref, do_ref):
    qst = stack_heads(q_ref[...])
    dost = stack_heads(do_ref[...])
    qT, doT = qst.T, dost.T
    oT = o_ref[...].T.astype(f32)
    delta = jnp.sum(doT.astype(f32) * jnp.concatenate([oT, oT], axis=1), axis=0, keepdims=True)
    return qst, qT, dost, doT, delta


def backward_step(k, v, query, lse, mask):
    qst, qT, dost, doT, delta = query
    p = jnp.exp2(mask(dot(k, qT) * (SCALE * LOG2E)) - lse)
    ds = (p * (dot(v, doT) - delta)).astype(bf16)
    dv = dot(p.astype(bf16), dost).astype(bf16)
    dk = (dot(ds, qst) * SCALE).astype(bf16)
    return dk, dv, dot(k, ds, 0, 0)


def self_backward(place, q, ks, vs, o, do, lse, bias, blocks, dq_before):
    rows, count = q.shape[0], len(blocks)
    pairs = q.shape[1] // PAIR
    last = 0 in blocks
    given = dq_before is not None

    def kernel(place_ref, q_ref, *refs):
        k_refs, v_refs = refs[:count], refs[count : 2 * count]
        o_ref, do_ref, lse_ref, bias_ref = refs[2 * count : 2 * count + 4]
        rest = refs[2 * count + 4 :]
        before_ref, rest = (rest[0], rest[1:]) if given else (None, rest)
        dq_ref, dk_refs, dv_refs, dqT = rest[0], rest[1 : 1 + count], rest[1 + count : 1 + 2 * count], rest[-1]

        def work():
            query = backward_setup(q_ref, o_ref, do_ref)
            dqT[...] = jnp.zeros_like(dqT)
            for n, r in enumerate(blocks):
                def step(n=n, r=r):
                    dk, dv, dq = backward_step(
                        k_refs[n][...], v_refs[n][...], query, lse_ref[0],
                        lambda s: segment_bias(bias_ref, r, s, r == 0),
                    )
                    dk_refs[n][...] = dk
                    dv_refs[n][...] = dv
                    dqT[...] += dq
                if r == 0:
                    step()
                else:
                    pl.when(place_ref[0] >= r)(step)
            part = unstack_heads(dqT[...]) * SCALE
            if given:
                part = part + before_ref[...]
            dq_ref[...] = part.astype(dq_ref.dtype)

        for n, r in enumerate(blocks):
            if r > 0:
                @pl.when(place_ref[0] < r)
                def _(n=n):
                    dk_refs[n][...] = jnp.zeros_like(dk_refs[n])
                    dv_refs[n][...] = jnp.zeros_like(dv_refs[n])
        if last:
            work()
        else:
            pl.when(place_ref[0] >= min(blocks))(work)

            @pl.when(place_ref[0] < min(blocks))
            def _():
                dq_ref[...] = before_ref[...] if given else jnp.zeros_like(dq_ref)

    col = pl.BlockSpec((rows, PAIR), lambda h, p: (0, h))
    args = [q, *[ks[r] for r in blocks], *[vs[r] for r in blocks], o, do, lse, bias]
    specs = [col] * (3 + 2 * count) + [
        pl.BlockSpec((1, 1, 2 * rows), lambda h, p: (h, 0, 0)),
        pl.BlockSpec(bias.shape, lambda h, p: (0, 0)),
    ]
    if given:
        args.append(dq_before)
        specs.append(col)
    shape = jax.ShapeDtypeStruct(q.shape, bf16)
    out = pl.pallas_call(
        kernel,
        grid_spec=pltpu.PrefetchScalarGridSpec(
            num_scalar_prefetch=1,
            grid=(pairs,),
            in_specs=specs,
            out_specs=[col] * (1 + 2 * count),
            scratch_shapes=[pltpu.VMEM((PAIR, 2 * rows), f32)],
        ),
        out_shape=[jax.ShapeDtypeStruct(q.shape, bf16 if last else f32)] + [shape] * (2 * count),
        compiler_params=params(),
        cost_estimate=cost(40 * count * rows * q.size, 8 * q.size * (2 + count)),
        name="self_backward",
    )(place, *args)
    return out[0], out[1 : 1 + count], out[1 + count :]


def cross_backward(length, q, k, v, o, do, lse, sure):
    rows, total = q.shape[0], k.shape[0]
    pairs = q.shape[1] // PAIR

    def kernel(length_ref, q_ref, k_ref, v_ref, o_ref, do_ref, lse_ref, dq_ref, dk_ref, dv_ref, dqT):
        query = backward_setup(q_ref, o_ref, do_ref)
        for a in range(0, total, CHUNK):
            sl = slice(a, a + CHUNK)
            dk, dv, dq = backward_step(
                k_ref[sl, :], v_ref[sl, :], query, lse_ref[0],
                lambda s: length_mask(length_ref, s, a, sure),
            )
            dk_ref[sl, :] = dk
            dv_ref[sl, :] = dv
            if a == 0:
                dqT[...] = dq
            else:
                dqT[...] += dq
        dq_ref[...] = (unstack_heads(dqT[...]) * SCALE).astype(bf16)

    col = pl.BlockSpec((rows, PAIR), lambda h, p: (0, h))
    tall = pl.BlockSpec((total, PAIR), lambda h, p: (0, h))
    return pl.pallas_call(
        kernel,
        grid_spec=pltpu.PrefetchScalarGridSpec(
            num_scalar_prefetch=1,
            grid=(pairs,),
            in_specs=[col, tall, tall, col, col, pl.BlockSpec((1, 1, 2 * rows), lambda h, p: (h, 0, 0))],
            out_specs=[col, tall, tall],
            scratch_shapes=[pltpu.VMEM((PAIR, 2 * rows), f32)],
        ),
        out_shape=[
            jax.ShapeDtypeStruct(q.shape, bf16),
            jax.ShapeDtypeStruct(k.shape, bf16),
            jax.ShapeDtypeStruct(k.shape, bf16),
        ],
        compiler_params=params(),
        cost_estimate=cost(40 * total * q.size, 8 * q.size + 8 * k.size),
        name="cross_backward",
    )(length, q, k, v, o, do, lse)


ERFC = (0.254829592, -0.284496736, 1.421413741, -1.453152027, 1.061405429)


def gelu_pair(v):
    e = jnp.exp2(v * v * (-0.5 * LOG2E))
    t = 1.0 / (1.0 + jnp.abs(v) * (0.3275911 * 0.7071067811865476))
    a1, a2, a3, a4, a5 = (0.5 * a for a in ERFC)
    tail = ((((a5 * t + a4) * t + a3) * t + a2) * t + a1) * t * e
    cdf = jnp.where(v >= 0.0, 1.0 - tail, tail)
    return v * cdf, cdf + v * e * 0.3989422804014327


def feed_forward(low, pair, r0, r1, cots, lifts, ub, outs):
    rows, width = r0.shape
    part, count = lifts[0].shape[3], len(lifts)
    hidden = part * count
    given = 0 if outs is None else 1

    def kernel(low_ref, r0_ref, r1_ref, g_ref, *refs):
        w_refs, ub_ref = refs[:count], refs[count]
        out_ref, back0, back1, inner_ref, grad_ref, sums_ref, r_ref, back_s = refs[count + 1 + given :]
        i = pl.program_id(0)

        @pl.when(i == 0)
        def _():
            r_ref[...] = r0_ref[...]
            sums_ref[...] = jnp.zeros_like(sums_ref)

        @pl.when(i == 1)
        def _():
            r_ref[...] = r1_ref[...]

        ups = [w[:, 0].reshape(width, part) for w in w_refs]
        downs = [w[:, 1].reshape(width, part) for w in w_refs]
        out = back = None
        for n in range(count):
            cols = slice(n * part, (n + 1) * part)
            lifted = dot(r_ref[...], ups[n]) + ub_ref[:, cols]
            grad_inner = dot(g_ref[...], downs[n])
            value, slope = gelu_pair(lifted)
            inner_ref[:, cols] = value.astype(bf16)
            grad = (grad_inner * slope).astype(bf16)
            grad_ref[:, cols] = grad
            sums_ref[:, cols] += jnp.sum(grad.astype(f32), axis=0, keepdims=True)
        for n in range(count):
            cols = slice(n * part, (n + 1) * part)
            o = dot(inner_ref[:, cols], downs[n], 1, 1)
            b = dot(grad_ref[:, cols], ups[n], 1, 1)
            out, back = (o, b) if n == 0 else (out + o, back + b)
        out_ref[...] = out.astype(bf16)
        back_s[...] = back.astype(bf16)

        @pl.when(i == 0)
        def _():
            back0[...] = back_s[...]

        @pl.when(i == 1)
        def _():
            back1[...] = back_s[...]

    whole = lambda x: pl.BlockSpec(x.shape, lambda i, s: (0,) * x.ndim)
    row = jax.ShapeDtypeStruct((rows, width), bf16)
    tall = jax.ShapeDtypeStruct((2 * rows, hidden), bf16)
    tall_spec = pl.BlockSpec((rows, hidden), lambda i, s: (i, 0))
    by_device = pl.BlockSpec((rows, width), lambda i, s: (s[0] ^ (pair + i), 0))
    return pl.pallas_call(
        kernel,
        grid_spec=pltpu.PrefetchScalarGridSpec(
            num_scalar_prefetch=1,
            grid=(2,),
            in_specs=[whole(r0), whole(r1), by_device]
            + [whole(x) for x in lifts] + [whole(ub)]
            + [pl.BlockSpec(memory_space=pl.ANY)] * given,
            out_specs=[by_device] + [whole(r0)] * 2 + [tall_spec] * 2 + [whole(ub)],
            scratch_shapes=[pltpu.VMEM((rows, width), bf16)] * 2,
        ),
        out_shape=[jax.ShapeDtypeStruct(cots.shape, bf16)] + [row] * 2 + [tall] * 2
        + [jax.ShapeDtypeStruct(ub.shape, f32)],
        input_output_aliases={5 + count: 0} if given else {},
        compiler_params=params(),
        cost_estimate=cost(16 * rows * width * hidden, 24 * rows * width + 4 * hidden * width),
        name="feed_forward",
    )(low, r0, r1, cots, *lifts, ub, *([outs] if given else []))


def lift_grad(low, lefts, rights, place, before):
    ordered = not isinstance(rights, list)
    ins = [rights] if ordered else rights
    hidden, wide = lefts[0].shape[1], ins[0].shape[1]
    count = len(lefts)
    piece = lefts[0].shape[0] // 2
    tiles, given = 4, 0 if before is None else 4
    tile = hidden // tiles

    def kernel(low_ref, *refs):
        l_refs, r_refs = refs[:count], refs[count : count + len(ins)]
        out_refs = refs[count + len(ins) + given :]
        total = None
        for k in range(2 * count):
            if ordered:
                right = r_refs[0][pl.ds(pl.multiple_of((low_ref[0] ^ k) * piece, piece), piece), :]
            else:
                right = r_refs[k][...]
            start = (k % 2) * piece
            part = dot(l_refs[k // 2][start : start + piece, :], right, 0, 0)
            total = part if total is None else total + part
        total = total.astype(bf16)
        for n in range(tiles):
            @pl.when(pl.program_id(0) == n)
            def _(n=n):
                out_refs[n][0] = total

    depth = 2 * count * piece
    return pl.pallas_call(
        kernel,
        grid_spec=pltpu.PrefetchScalarGridSpec(
            num_scalar_prefetch=1,
            grid=(tiles,),
            in_specs=[pl.BlockSpec((2 * piece, tile), lambda i, s: (0, i))] * count
            + [pl.BlockSpec(x.shape, lambda i, s: (0, 0)) for x in ins]
            + [pl.BlockSpec(memory_space=pl.ANY)] * given,
            out_specs=[pl.BlockSpec((1, tile, wide), lambda i, s: (place, 0, 0))] * tiles,
        ),
        out_shape=[jax.ShapeDtypeStruct((2, tile, wide), bf16)] * tiles,
        input_output_aliases={1 + count + len(ins) + n: n for n in range(given)},
        compiler_params=params(),
        cost_estimate=cost(2 * depth * hidden * wide, 2 * depth * (hidden + wide) + 2 * hidden * wide),
        name="lift_grad",
    )(low, *lefts, *ins, *(before or ()))


def shard_grad(low, lefts, rights, column, columns, before):
    high, wide = lefts[0].shape[1], rights[0].shape[1]
    count = len(lefts)
    rows = high // 8
    given = 0 if before is None else 2

    def kernel(low_ref, *refs):
        even_ref, odd_ref = refs[2 * count + given :]
        total = None
        for l_ref, r_ref in zip(refs[:count], refs[count : 2 * count]):
            part = dot(l_ref[...], r_ref[...], 0, 0)
            total = part if total is None else total + part
        total = total.astype(bf16)

        @pl.when((low_ref[0] & 1) == 0)
        def _():
            even_ref[0] = total[:rows]
            odd_ref[0] = total[rows:]

        @pl.when((low_ref[0] & 1) == 1)
        def _():
            even_ref[0] = total[rows:]
            odd_ref[0] = total[:rows]

    depth = sum(x.shape[0] for x in lefts)
    shape = jax.ShapeDtypeStruct((4, rows, columns * wide), bf16)
    return pl.pallas_call(
        kernel,
        grid_spec=pltpu.PrefetchScalarGridSpec(
            num_scalar_prefetch=1,
            grid=(4,),
            in_specs=[pl.BlockSpec((x.shape[0], 2 * rows), lambda i, s: (0, i)) for x in lefts]
            + [pl.BlockSpec(x.shape, lambda i, s: (0, 0)) for x in rights]
            + [pl.BlockSpec(memory_space=pl.ANY)] * given,
            out_specs=[pl.BlockSpec((1, rows, wide), lambda i, s: ((s[0] >> 1) ^ i, 0, column))] * 2,
        ),
        out_shape=[shape] * 2,
        input_output_aliases={1 + 2 * count: 0, 2 + 2 * count: 1} if given else {},
        compiler_params=params(),
        cost_estimate=cost(2 * depth * high * wide, 2 * depth * (high + wide) + 2 * high * wide),
        name="shard_grad",
    )(low, *lefts, *rights, *(before or ()))


def pack_shards(shards, turned, up, down):
    rows, cols = shards[0].shape
    flat = [*shards, up, down]
    part = up.shape[1] // 8

    def kernel(*refs):
        up_ref, down_ref, out_ref, lift_ref = refs[len(shards) :]
        for i, ref in enumerate(refs[: len(shards)]):
            out_ref[:, i * cols : (i + 1) * cols] = ref[...].T if i in turned else ref[...]
        for d in range(8):
            span = slice(d * part, (d + 1) * part)
            lift_ref[d, 0] = up_ref[:, span]
            lift_ref[d, 1] = down_ref[span, :].T

    return pl.pallas_call(
        kernel,
        out_shape=[
            jax.ShapeDtypeStruct((rows, len(shards) * cols), bf16),
            jax.ShapeDtypeStruct((8, 2, rows, part), bf16),
        ],
        compiler_params=params(),
        cost_estimate=cost(0, 4 * sum(x.size for x in flat)),
        name="pack_shards",
    )(*flat)


def sum_columns(place, pieces, count, size):
    rows, wide = pieces[0].shape
    cols = wide // count
    part = cols // size

    def kernel(place_ref, *refs):
        ins, outs, total = refs[: len(pieces)], refs[len(pieces) : -1], refs[-1]
        acc = ins[0][...].astype(f32)
        for ref in ins[1:]:
            acc = acc + ref[...].astype(f32)
        total[...] = acc
        for r in range(size):
            start = lax.rem(place_ref[0] + size - r, size) * part
            for w in range(count):
                span = pl.ds(pl.multiple_of(w * cols + start, part), part)
                outs[r][:, w * part : (w + 1) * part] = total[:, span].astype(outs[r].dtype)

    return pl.pallas_call(
        kernel,
        grid_spec=pltpu.PrefetchScalarGridSpec(
            num_scalar_prefetch=1,
            grid=(1,),
            in_specs=[pl.BlockSpec(x.shape, lambda i, s: (0, 0)) for x in pieces],
            out_specs=[pl.BlockSpec((rows, count * part), lambda i, s: (0, 0))] * size,
            scratch_shapes=[pltpu.VMEM((rows, wide), f32)],
        ),
        out_shape=[jax.ShapeDtypeStruct((rows, count * part), f32 if r == 0 else bf16) for r in range(size)],
        compiler_params=params(),
        cost_estimate=cost(0, 4 * sum(x.size for x in pieces)),
        name="sum_columns",
    )(place, *pieces)


def normed(rows, gain, shift):
    average = jnp.mean(rows, axis=-1, keepdims=True)
    centered = rows - average
    variance = jnp.mean(centered * centered, axis=-1, keepdims=True)
    return (centered * lax.rsqrt(variance + EPSILON) * gain + shift).astype(bf16)


def centered_rows(rows):
    average = jnp.mean(rows, axis=-1, keepdims=True)
    centered = rows - average
    scale = lax.rsqrt(jnp.mean(centered * centered, axis=-1, keepdims=True) + EPSILON)
    return centered * scale, scale


def norm_back(rows, gain, grad):
    xhat, scale = centered_rows(rows)
    scaled = grad * gain
    return scale * (
        scaled
        - jnp.mean(scaled, axis=-1, keepdims=True)
        - xhat * jnp.mean(scaled * xhat, axis=-1, keepdims=True)
    )


def norm_sums(rows, grad):
    return jnp.sum(grad * centered_rows(rows)[0], axis=0), jnp.sum(grad, axis=0)


def column_sums(matrix):
    return jnp.sum(matrix.astype(f32), axis=0)


def together(*values):
    return lax.optimization_barrier(values)


def flip(x, k):
    return lax.ppermute(x, "low", [(i, i ^ k) for i in range(8)])


def wrap(value, size):
    return value % size if isinstance(value, int) else lax.rem(value, size)


def turn(x, r, size):
    return lax.ppermute(x, "tensor", [(i, (i + r) % size) for i in range(size)])


def gather_chips(x):
    return [x] + [flip(x, k) for k in (2, 4, 6)]


def gather_cores(even):
    return [p for e in even for p in (e, flip(e, 1))]


def by_place(pieces, place):
    size = len(pieces)
    return jnp.stack(
        [
            sum(jnp.where(lax.rem(place + size - r, size) == z, pieces[r], 0.0) for r in range(size))
            for z in range(size)
        ]
    )


def stack_shards(scalars, pieces, first, count):
    rows, wide = pieces[0].shape
    cut = wide // count * first
    every = slice(None)
    return move(
        "stack_shards", scalars, pieces, [(len(pieces), rows, cut), (len(pieces), rows, wide - cut)],
        lambda s: [
            (r, (every, pl.ds(start, extent)), part, (r, every, every))
            for r in range(len(pieces))
            for part, (start, extent) in enumerate([(0, cut), (cut, wide - cut)])
        ],
    )


def unpack_weights(scalars, pieces, count, sizes):
    size, rows, cols = pieces[0].shape
    cols //= count
    every = slice(None)

    def plan(s):
        return [
            (
                k, (r, every, pl.ds(w * cols, cols)),
                w, (at((s[0] ^ k) * rows, rows), at(wrap(s[1] + size - r, size) * cols, cols)),
            )
            for w in range(count) for k in range(8) for r in range(size)
        ]

    matrices = move("unpack_weights", scalars, pieces, [(8 * rows, size * cols)] * count, plan)
    if sizes[0] > 1:
        matrices = [lax.all_gather(m, "high", axis=0, tiled=True) for m in matrices]
    return matrices


def add_pair(a, b):
    return (a.astype(f32) + b.astype(f32)).astype(bf16)


def scatter_low(pieces):
    even = [add_pair(pieces[k], flip(pieces[k + 1], 1)) for k in (6, 4, 2)]
    back = [flip(e, k).astype(f32) for e, k in zip(even, (6, 4, 2))]
    own = pieces[0].astype(f32) + flip(pieces[1], 1).astype(f32)
    return own + back[0] + back[1] + back[2]


def shard_grads(low, grads):
    before = None
    for i, (lefts, rights) in enumerate(grads):
        before = shard_grad(low, lefts, rights, i, len(grads), before)
    return before


def whole_shards(parts, turned, count):
    shard = parts[0] + sum(x.astype(f32) for x in turned)
    return jnp.split(shard, count, axis=1)


def sum_vector(vector, sizes):
    size = sizes[2]
    if sizes[0] > 1:
        vector = lax.psum(vector, "high")
    slices = lax.all_to_all(vector.reshape(8, -1), "low", split_axis=0, concat_axis=0, tiled=True)
    mine = jnp.sum(slices, axis=0)
    mine = mine + sum(turn(mine, r, size) for r in range(1, size))
    spread = jnp.broadcast_to(mine, (8, *mine.shape))
    return lax.all_to_all(spread, "low", split_axis=0, concat_axis=0, tiled=True).reshape(-1)


def path_bias(parents, place, own, blocks):
    count = parents.shape[0]
    labels = jnp.arange(count)
    table = (
        (labels[:, None] == labels[None, :])
        | ((parents[:, None] == labels[None, :]) & (labels[:, None] > 0))
    ).astype(f32)
    reach = 1
    while reach < count:
        table = jnp.minimum(jnp.dot(table, table), 1.0)
        reach *= 2
    slots = jnp.arange(blocks * own)
    segment = (place - slots // own) * own + slots % own
    pick = (labels[:, None] == segment[None, :]).astype(f32)
    lanes = jnp.arange(2 * own * SEG)
    query = place * own + (lanes // SEG) % own
    mine = (labels[:, None] == query[None, :]).astype(f32)
    seen = jnp.dot(pick.T, jnp.dot(table.T, mine))
    return jnp.where(seen > 0.5, 0.0, NEG)


def on_device(sizes, sure):
    size = sizes[2]

    def run(
        tokens,
        encoded,
        parents,
        source_lengths,
        cotangent,
        first_gain,
        first_shift,
        self_query,
        self_query_bias,
        self_key,
        self_value,
        self_value_bias,
        self_out,
        self_out_bias,
        second_gain,
        second_shift,
        cross_query,
        cross_query_bias,
        cross_key,
        cross_value,
        cross_value_bias,
        cross_out,
        cross_out_bias,
        third_gain,
        third_shift,
        up_weight,
        up_bias,
        down_weight,
        down_bias,
    ):
        low = lax.axis_index("low")
        place = lax.axis_index("tensor")
        scalars = jnp.stack([low, place]).astype(jnp.int32)
        low_1, place_1 = scalars[:1], scalars[1:]
        rows, width = tokens.shape
        up_chain = [(i, i + 1) for i in range(size - 1)]
        down_chain = [(i + 1, i) for i in range(size - 1)]

        a, lift = pack_shards(
            [
                self_query, self_key, self_value,
                self_out, cross_query, cross_key, cross_value, cross_out,
            ],
            (3, 7), up_weight, down_weight,
        )
        z = [turn(a, r, size) for r in range(1, size)]
        blocks = [tokens, lax.ppermute(tokens, "tensor", up_chain)]
        ones = [normed(tokens.astype(f32), first_gain, first_shift)]
        bias = path_bias(parents[0], place, rows // SEG, size)
        part = width // size
        hidden = up_weight.shape[1] // 8
        biases = jnp.concatenate(
            [
                self_query_bias, self_value_bias, cross_query_bias, cross_value_bias,
                lax.dynamic_slice_in_dim(up_bias, low * hidden, hidden, 0),
            ]
        )
        biases = [biases] + [turn(biases, r, size) for r in range(1, size)]
        ub = jnp.concatenate([x[4 * part :] for x in biases])[None]
        placed = by_place([x[: 4 * part] for x in biases], place).reshape(size, 4, part)
        q_bias, v_bias, xq_bias, xv_bias = [placed[:, i].reshape(width) for i in range(4)]
        lift = lax.all_to_all(lift, "low", split_axis=0, concat_axis=0, tiled=True)
        if sizes[0] > 1:
            lift = lax.all_gather(lift, "high", axis=0, tiled=True)
        cots = lax.all_gather(cotangent, "low", axis=0, tiled=True)
        a, lift, z, blocks, ones, bias, ub, q_bias, v_bias, xq_bias, xv_bias = together(
            a, lift, z, blocks, ones, bias, ub, q_bias, v_bias, xq_bias, xv_bias
        )

        packed_a, packed_b = stack_shards(scalars, [a, *z], 3, 8)
        even_a = gather_chips(packed_a)
        blocks = blocks + [lax.ppermute(blocks[-1], "tensor", up_chain)]
        ones = ones + [normed(blocks[1].astype(f32), first_gain, first_shift)]
        even_a, packed_b, blocks, ones, encoded = together(even_a, packed_b, blocks, ones, encoded)

        all_a = gather_cores(even_a)
        even_b = gather_chips(packed_b)
        blocks = blocks + [lax.ppermute(blocks[-1], "tensor", up_chain)]
        source = lax.all_gather(encoded, "tensor", axis=0, tiled=True)
        wq, wk, wv = unpack_weights(scalars, all_a, 3, sizes)
        ones = ones + [normed(blocks[2].astype(f32), first_gain, first_shift)]
        q1 = (dot(ones[0], wq) + q_bias).astype(bf16)
        ks = [dot(n, wk).astype(bf16) for n in ones]
        vs = [(dot(n, wv) + v_bias).astype(bf16) for n in ones]
        state = self_forward(place_1, q1, ks, vs, bias, range(size - 1), None, False)
        even_b, blocks, state, lift = together(even_b, blocks, state, lift)

        lifts = [lift, turn(lift, 1, size)]
        all_b = gather_cores(even_b)
        ones = ones + [normed(blocks[size - 1].astype(f32), first_gain, first_shift)]
        ks = ks + [dot(ones[-1], wk).astype(bf16)]
        vs = vs + [(dot(ones[-1], wv) + v_bias).astype(bf16)]
        mixed_one, lse_one = self_forward(
            place_1, q1, ks, vs, bias, (size - 1,), state, True
        )
        mixed_one, all_b, lifts, source = together(mixed_one, all_b, lifts, source)

        lifts = lifts + [turn(lifts[-1], 1, size)]
        wo, xq, xk, xv, xo = unpack_weights(scalars, all_b, 5, sizes)
        hidden_one = tokens.astype(f32) + dot(mixed_one, wo, 1, 1) + self_out_bias
        two = normed(hidden_one, second_gain, second_shift)
        q2 = (dot(two, xq) + xq_bias).astype(bf16)
        k2 = dot(source, xk).astype(bf16)
        v2 = (dot(source, xv) + xv_bias).astype(bf16)
        q2, k2, v2, lifts = together(q2, k2, v2, lifts)

        lifts = lifts + [turn(lifts[-1], 1, size)]
        mixed_two, lse_two = cross_forward(source_lengths, q2, k2, v2, sure)
        hidden_two = hidden_one + dot(mixed_two, xo, 1, 1) + cross_out_bias
        three = normed(hidden_two, third_gain, third_shift)
        three, lifts = together(three, lifts)

        x2, x4 = flip(three, 2), flip(three, 4)
        c0 = flip(three, 1)
        outs, firsts, lasts, inners, grads, up_sums, threes = None, [], [], [], [], [], []
        evens = [three, x2, x4, None]
        for n, k in enumerate(range(0, 8, 2)):
            if n == 0:
                pair = (three, c0)
            elif n == 1:
                three_sent, x2, x4, firsts[0] = together(three, x2, x4, firsts[0])
                evens = [three, x2, x4, flip(three_sent, 6)]
                pair = (x2, flip(x2, 1))
            else:
                pair = (evens[n], flip(evens[n], 1))
                pair, firsts[n - 2], lasts[n - 2] = together(pair, firsts[n - 2], lasts[n - 2])
            threes += pair
            outs, back0, back1, inner, grad, sums = feed_forward(
                low_1, k, *pair, cots, lifts, ub, outs
            )
            firsts.append(back0)
            lasts.append(flip(back1, 1))
            inners.append(inner)
            grads.append(grad)
            up_sums.append(sums)
        own = firsts[0].astype(f32) + lasts[0].astype(f32)
        back = [add_pair(firsts[n], lasts[n]) for n in (1, 2)]
        grads, back = together(grads, back)
        back = [flip(back[0], 2), flip(back[1], 4)]
        lift_shares = lift_grad(low_1, grads, threes, 0, None)
        inners, lift_shares, firsts[3], lasts[3], back = together(
            inners, lift_shares, firsts[3], lasts[3], back
        )
        back.append(flip(add_pair(firsts[3], lasts[3]), 6))
        lift_shares = lift_grad(low_1, inners, cots, 1, lift_shares)
        lift_shares, back, own = together(lift_shares, back, own)
        grad_three = own + sum(x.astype(f32) for x in back)

        grad_hidden_two = cotangent.astype(f32) + norm_back(hidden_two, third_gain, grad_three)
        grad_two = grad_hidden_two.astype(bf16)
        do2 = dot(grad_two, xo).astype(bf16)
        do2, outs, lift_shares = together(do2, outs, lift_shares)

        out_sum = lax.psum_scatter(outs, "low", scatter_dimension=0, tiled=True)
        lift_got = turn(lift_shares[size - 1], size - 1, size)
        dq2, dk2, dv2 = cross_backward(source_lengths, q2, k2, v2, mixed_two, do2, lse_two, sure)
        dq2, dk2, dv2, lift_got = together(dq2, dk2, dv2, lift_got)

        lift_got = turn(add_pair(lift_shares[size - 2], lift_got), size - 1, size)
        grad_two_normed = dot(dq2, xq, 1, 1)
        grad_hidden_one = grad_hidden_two + norm_back(hidden_one, second_gain, grad_two_normed)
        grad_one = grad_hidden_one.astype(bf16)
        do1 = dot(grad_one, wo).astype(bf16)
        b_even, b_odd = shard_grads(
            low_1,
            [
                ([grad_one], [mixed_one]),
                ([two], [dq2]),
                ([source], [dk2]),
                ([source], [dv2]),
                ([grad_two], [mixed_two]),
            ],
        )
        encoded_part = (dot(dk2, xk, 1, 1) + dot(dv2, xv, 1, 1)).astype(bf16)
        spread = by_place([sum(up_sums)[0, r * hidden : (r + 1) * hidden] for r in range(size)], place)
        spread = lax.dynamic_update_slice(
            jnp.zeros((size, up_bias.shape[0]), f32), spread, (0, low * hidden)
        )
        early = jnp.concatenate(
            [
                *norm_sums(hidden_one, grad_two_normed),
                *norm_sums(hidden_two, grad_three),
                column_sums(grad_one),
                column_sums(grad_two),
                column_sums(cotangent),
                column_sums(dq2),
                column_sums(dv2),
                spread.reshape(-1),
            ]
        )
        do1, b_even, b_odd, lift_got, encoded_part, early = together(
            do1, b_even, b_odd, lift_got, encoded_part, early
        )

        lift_got = turn(add_pair(lift_shares[size - 3], lift_got), size - 1, size)
        if sizes[0] > 1:
            b_even, b_odd = [
                lax.psum_scatter(x, "high", scatter_dimension=1, tiled=True) for x in (b_even, b_odd)
            ]
        b_got = flip(b_odd, 1)
        early = sum_vector(early, sizes)
        dq, dks, dvs, shares = None, [None] * size, [None] * size, [None] * size
        share = None
        for group in [(r,) for r in range(size - 1, 1, -1)] + [(1, 0)]:
            dq, dk, dv = self_backward(
                place_1, q1, ks, vs, mixed_one, do1, lse_one, bias, group, dq
            )
            for n, r in enumerate(group):
                dks[r], dvs[r] = dk[n], dv[n]
                shares[r] = dot(dk[n], wk, 1, 1) + dot(dv[n], wv, 1, 1)
            r = group[0]
            if share is None:
                share, b_even, b_got, lift_got, do1 = together(shares[r], b_even, b_got, lift_got, do1)
                b_sums = [add_pair(b_even[p], b_got[p]) for p in range(4)]
                b_back = [flip(b_sums[p], 2 * p) for p in (1, 2, 3)]
                share = lax.ppermute(share.astype(bf16), "tensor", down_chain)
            elif r > 1:
                share, shares[r], do1 = together(share, shares[r], do1)
                share = lax.ppermute(add_pair(shares[r], share), "tensor", down_chain)
            else:
                share, shares, dq, dks, dvs, b_back, early = together(
                    share, shares, dq, dks, dvs, b_back, early
                )
                share = lax.ppermute(add_pair(shares[r], share), "tensor", down_chain)
        shares[0] = shares[0] + dot(dq, wq, 1, 1)
        b_parts = sum_columns(place_1, [b_sums[0], *b_back], 5, size)
        b_turned = [turn(b_parts[r], size - r, size) for r in range(1, size)]
        lift_sums = add_pair(lift_shares[0], lift_got)
        if sizes[0] > 1:
            lift_sums = lax.psum_scatter(lift_sums, "high", scatter_dimension=2, tiled=True)
        lift_sums = lax.all_to_all(lift_sums, "low", split_axis=2, concat_axis=1, tiled=True)
        a_even, a_odd = shard_grads(low_1, [([ones[0]], [dq]), (ones, dks), (ones, dvs)])
        own_sums = [norm_sums(x.astype(f32), s) for x, s in zip(blocks, shares)]
        late = jnp.concatenate(
            [
                sum(f[0] for f in own_sums),
                sum(f[1] for f in own_sums),
                column_sums(dq),
                sum(column_sums(v) for v in dvs),
            ]
        )
        a_even, a_odd, b_turned, share, shares, late, encoded_part = together(
            a_even, a_odd, b_turned, share, shares, late, encoded_part
        )

        if sizes[0] > 1:
            a_even, a_odd = [
                lax.psum_scatter(x, "high", scatter_dimension=1, tiled=True) for x in (a_even, a_odd)
            ]
        a_got = flip(a_odd, 1)
        a_sums = [add_pair(a_even[p], a_got[p]) for p in range(4)]
        a_back = [flip(a_sums[p], 2 * p) for p in (1, 2, 3)]
        encoded_grad = lax.psum_scatter(
            encoded_part, "tensor", scatter_dimension=0, tiled=True
        ).astype(f32)
        share = shares[0] + share.astype(f32)
        tokens_grad = grad_hidden_one + norm_back(tokens.astype(f32), first_gain, share)
        a_parts = sum_columns(place_1, [a_sums[0], *a_back], 3, size)
        a_turned = [turn(a_parts[r], size - r, size) for r in range(1, size)]
        wo_g, xq_g, xk_g, xv_g, xo_g = whole_shards(b_parts, b_turned, 5)
        wq_g, wk_g, wv_g = whole_shards(a_parts, a_turned, 3)
        block_out = hidden_two + out_sum.astype(f32) + down_bias
        up_weight_grad = lift_sums[0].T.astype(f32)
        down_weight_grad = lift_sums[1].astype(f32)

        late = sum_vector(late, sizes)
        small = [early[i * width : (i + 1) * width] for i in range(9)]
        small = [late[:width], late[width : 2 * width]] + small + [late[2 * width : 3 * width], late[3 * width :]]
        split = [lax.dynamic_slice_in_dim(s, place * part, part, 0) for s in (small[11], small[12], small[9], small[10])]
        up_bias_grad = lax.dynamic_slice_in_dim(
            early[9 * width :], place * up_bias.shape[0], up_bias.shape[0], 0
        )
        return (
            block_out.astype(bf16),
            tokens_grad,
            encoded_grad,
            small[0],
            small[1],
            wq_g,
            split[0],
            wk_g,
            wv_g,
            split[1],
            wo_g.T,
            small[6],
            small[2],
            small[3],
            xq_g,
            split[2],
            xk_g,
            xv_g,
            split[3],
            xo_g.T,
            small[7],
            small[4],
            small[5],
            up_weight_grad,
            up_bias_grad,
            down_weight_grad,
            small[8],
        )

    return run


def solution(mesh):
    dp, size = mesh.shape["dp"], mesh.shape["tensor"]
    sizes = (dp // 8, 8, size)
    fine = Mesh(mesh.devices.reshape(sizes), ("high", "low", "tensor"))
    depth = ("high", "low")
    rows = P((*depth, "tensor"), None)
    block, turned = P(depth, "tensor"), P("tensor", depth)
    part, whole = P("tensor"), P()
    placed = (
        rows, rows, P(depth, None), P(depth), rows, whole, whole,
        block, part, block, block, part, turned, whole, whole, whole,
        block, part, block, block, part, turned, whole, whole, whole,
        block, part, turned, whole,
    )
    out = (
        rows, rows, rows, whole, whole,
        block, part, block, block, part, turned, whole, whole, whole,
        block, part, block, block, part, turned, whole, whole, whole,
        block, part, turned, whole,
    )
    return jax.shard_map(
        on_device(sizes, 768), mesh=fine, in_specs=placed, out_specs=out, check_vma=False
    )
```

time: 1170 us -> 827 us (0.71)
  waiting for transfers between devices: 375 us -> 183 us
  local copies, waits for them, and re-layouts: 200 us -> 43.2 us
  Pallas kernels: 129 us -> 280 us
  matrix products: 163 us -> 81.9 us
  blocking collectives: 60.2 us -> 0 us
  starting transfers between devices: 121 us -> 138 us
  other arithmetic: 93.7 us -> 77.8 us
    pallas_call x8 -> x27, Pallas kernels: 129 us -> 280 us  [the longest x4 71.8 us: feed_forward(): pl.pallas_call(kernel, grid_spec=pltpu.PrefetchScalarGridSpec(num_scalar_...]
    ppermute x80 -> x66, waiting for transfers between devices: 273 us -> 159 us  [the longest x36 78.2 us: flip(): return lax.ppermute(x, 'low', [(i, i ^ k) for i in range(8)])]
    dot_general x32 -> x28, matrix products: 162 us -> 80.4 us  [dot(): lax.dot_general(a, b, (((ca,), (cb,)), ((), ())), preferred_element_type=...]
    all_gather x2 -> x0, blocking collectives: 60.2 us -> none  [the longest x1 39.8 us: run(): lax.all_gather(jnp.stack([self_query_bias, self_value_bias, cross_query_b...]
    psum x1 -> x0, waiting for transfers between devices: 55.8 us -> none  [run(): summed = lax.psum(jnp.concatenate(vectors), ('high', 'low', 'tensor'))]
    ppermute x80 -> x66, starting transfers between devices: 70.9 us -> 114 us  [the longest x24 53.6 us: turn(): return lax.ppermute(x, 'tensor', [(i, (i + r) % size) for i in range(size)])]
    reduce_scatter x1 -> x2, waiting for transfers between devices: 42.8 us -> 0.01 us  [the longest x1 0.01 us: run(): out_sum = lax.psum_scatter(outs, 'low', scatter_dimension=0, tiled=True)]
    dynamic_update_slice x24 -> x0, local copies, waits for them, and re-layouts: 34.3 us -> none  [the longest x16 29.3 us: arrange(): lax.dynamic_update_slice_in_dim(whole, piece, (low ^ k) * extent, axis)]
  transfers between devices with their start and end apart: 89 -> 76, of which waited for: 28 -> 29; matrix products, arithmetic and copies ran while one was open for 37% -> 20% of each run, Pallas kernels for 9% -> 32%
where the time goes in v2:
time: 827 us; the launch traced here: 820 us
  Pallas kernels  280 us (34%)
  waiting for transfers between devices  183 us (22%)
  starting transfers between devices  138 us (17%)
  matrix products  81.9 us (10%)
  other arithmetic  77.8 us (9%)
  local copies, waits for them, and re-layouts  43.2 us (5%)
  between operations  16 us (2%)
    dot_general x28, matrix products, dot(): lax.dot_general(a, b, (((ca,), (cb,)), ((), ())), preferred_element_type=...  80.4 us
    ppermute x36, waiting for transfers between devices, flip(): return lax.ppermute(x, 'low', [(i, i ^ k) for i in range(8)])  78.2 us
    pallas_call x4, Pallas kernels, feed_forward(): pl.pallas_call(kernel, grid_spec=pltpu.PrefetchScalarGridSpec(num_scalar_...  71.8 us
    ppermute x24, waiting for transfers between devices, turn(): return lax.ppermute(x, 'tensor', [(i, (i + r) % size) for i in range(size)])  66.5 us
    ppermute x24, starting transfers between devices, turn(): return lax.ppermute(x, 'tensor', [(i, (i + r) % size) for i in range(size)])  53.6 us
    pallas_call x8, Pallas kernels, shard_grad(): pl.pallas_call(kernel, grid_spec=pltpu.PrefetchScalarGridSpec(num_scalar_...  51.2 us
    pallas_call x3, Pallas kernels, self_backward(): pl.pallas_call(kernel, grid_spec=pltpu.PrefetchScalarGridSpec(num_scalar_...  33.1 us
    pallas_call x2, Pallas kernels, lift_grad(): pl.pallas_call(kernel, grid_spec=pltpu.PrefetchScalarGridSpec(num_scalar_...  30.9 us
  transfers between devices with their start and end apart: 76, of which 29 were waited for; matrix products, arithmetic and copies ran while one was open for 20% of the time, Pallas kernels for 32%

profile of v2, /device:TPU:0, one launch (start us, length us, event | category | flops | bytes accessed | tf_op | source)
XLA Modules:
  0.0 819.6 jit_solution(15166201689362534801)
XLA Ops:
  36.0 20.5 %collective-permute-done.2.refs_3_ = bf16[128,2048]{1,0:T(8,128)(2,1)} collective-permute-done((bf16[128,2048]{1,0:T(8,128)(2,1)}, bf16[128,2048]{1,0:T(8,128)(2,1)}, u32[]{:S(2)}, u32[]{:S(2)}) %collective-permute-start.2) | collective-permute-done | bytes 524320 | tf_op jit(solution)/shard_map/ppermute | solution.py:633
  56.5 19.3 %collective-permute-done.1.refs_2_ = bf16[128,2048]{1,0:T(8,128)(2,1)} collective-permute-done((bf16[128,2048]{1,0:T(8,128)(2,1)}, bf16[128,2048]{1,0:T(8,128)(2,1)}, u32[]{:S(2)}, u32[]{:S(2)}) %collective-permute-start.1) | collective-permute-done | bytes 524320 | tf_op jit(solution)/shard_map/ppermute | solution.py:633
  84.2 13.4 %collective-permute-start.10 = (bf16[512,1024]{1,0:T(8,128)(2,1)S(1)}, bf16[512,1024]{1,0:T(8,128)(2,1)S(1)}, u32[]{:S(2)}, u32[]{:S(2)}) collective-permute-start(bf16[512,1024]{1,0:T(8,128)(2,1)S(1)} %collective-permute-done.3), channel_id=1, source_target_pairs={{0,1},{1,2},{2,3},{4,5},{5,6},{6,7},{8,9},{9,10},{10,11},{12,13},{... | collective-permute-start | bytes 3145736 | tf_op jit(solution)/shard_map/ppermute | solution.py:818
  102.3 14.3 %collective-permute-done.8.refs_4_ = bf16[4,128,768]{2,1,0:T(8,128)(2,1)S(1)} collective-permute-done((bf16[4,128,768]{2,1,0:T(8,128)(2,1)}, bf16[4,128,768]{2,1,0:T(8,128)(2,1)S(1)}, u32[]{:S(2)}, u32[]{:S(2)}) %collective-permute-start.8) | collective-permute-done | bytes 786464 | tf_op jit(solution)/shard_map/ppermute | solution.py:625
  120.3 13.7 %collective-permute-start.18 = (bf16[512,1024]{1,0:T(8,128)(2,1)S(1)}, bf16[512,1024]{1,0:T(8,128)(2,1)S(1)}, u32[]{:S(2)}, u32[]{:S(2)}) collective-permute-start(bf16[512,1024]{1,0:T(8,128)(2,1)S(1)} %collective-permute-done.10), channel_id=1, source_target_pairs={{0,1},{1,2},{2,3},{4,5},{5,6},{6,7},{8,9},{9,10},{10,11},{12,13},{... | collective-permute-start | bytes 3145736 | tf_op jit(solution)/shard_map/ppermute | solution.py:824
  163.8 10.8 %self_forward.2 = (f32[8,1,1024]{2,1,0:T(1,128)}, f32[8,1,1024]{2,1,0:T(1,128)}, f32[8,128,1024]{2,1,0:T(8,128)}) custom-call(s32[1]{0:T(128)} %bitcast.place_ref, bf16[512,1024]{1,0:T(8,128)(2,1)} %add_convert_fusion.22.q_ref, bf16[512,1024]{1,0:T(8,128)(2,1)} %convolution_convert_fusion.6.refs_0_.refs_1_, ...), custom_call_target="tpu_custom_call" | custom-call | flops 12884901888 | bytes 8388608 | tf_op jit(solution)/shard_map/self_forward/pallas_call | solution.py:157
  176.7 19.0 %collective-permute-done.16.refs_4_ = bf16[4,128,1280]{2,1,0:T(8,128)(2,1)S(1)} collective-permute-done((bf16[4,128,1280]{2,1,0:T(8,128)(2,1)S(1)}, bf16[4,128,1280]{2,1,0:T(8,128)(2,1)S(1)}, u32[]{:S(2)}, u32[]{:S(2)}) %collective-permute-start.16) | collective-permute-done | bytes 1310752 | tf_op jit(solution)/shard_map/ppermute | solution.py:625
  212.5 10.7 %collective-permute-done.23.refs_1_ = bf16[8,2,128,256]{3,2,1,0:T(8,128)(2,1)} collective-permute-done((bf16[8,2,128,256]{3,2,1,0:T(8,128)(2,1)}, bf16[8,2,128,256]{3,2,1,0:T(8,128)(2,1)}, u32[]{:S(2)}, u32[]{:S(2)}) %collective-permute-start.23) | collective-permute-done | bytes 1048608 | tf_op jit(solution)/shard_map/ppermute | solution.py:633
  224.3 9.4 %unpack_weights.3 = (bf16[1024,1024]{1,0:T(8,128)(2,1)}, bf16[1024,1024]{1,0:T(8,128)(2,1)}, bf16[1024,1024]{1,0:T(8,128)(2,1)}, bf16[1024,1024]{1,0:T(8,128)(2,1)}, bf16[1024,1024]{1,0:T(8,128)(2,1)}) custom-call(s32[2]{0:T(128)} %pad_add_fusion.scalars_ref, bf16[4,128,1280]{2,1,0:T(8,128)(2,1)} %get-tuple-element.308.refs_0_, ...), custom_call_target="tpu_custom_call" | custom-call | bytes 20971520 | tf_op jit(solution)/shard_map/unpack_weights/pallas_call | solution.py:50
  252.0 19.1 %cross_forward.1 = (bf16[512,1024]{1,0:T(8,128)(2,1)}, f32[8,1,1024]{2,1,0:T(1,128)}) custom-call(s32[1]{0:T(128)S(6)} %copy.156.length_ref, bf16[512,1024]{1,0:T(8,128)(2,1)} %add_convert_fusion.16.q_ref, bf16[1024,1024]{1,0:T(8,128)(2,1)} %convolution_convert_fusion.k_ref, bf16[1024,1024]{1,0:T(8,128)(2,1)} %add_convert_fusion.1.v_ref), custom_call_target="tpu_custom_call" | custom-call | flops 8589934592 | bytes 6291456 | tf_op jit(solution)/shard_map/cross_forward/pallas_call | solution.py:192
  280.7 17.8 %feed_forward.4 = (bf16[4096,1024]{1,0:T(8,128)(2,1)}, bf16[512,1024]{1,0:T(8,128)(2,1)}, bf16[512,1024]{1,0:T(8,128)(2,1)}, bf16[1024,1024]{1,0:T(8,128)(2,1)},...) custom-call(s32[1]{0:T(128)} %bitcast.1.low_ref, bf16[512,1024]{1,0:T(8,128)(2,1)} %add_convert_fusion.15.r0_ref.refs_4_, ...), custom_call_target="tpu_custom_call" | custom-call | flops 8589934592 | bytes 16777216 | tf_op jit(solution)/shard_map/feed_forward/pallas_call | solution.py:419
  311.6 18.3 %feed_forward.5 = (bf16[4096,1024]{1,0:T(8,128)(2,1)}, bf16[512,1024]{1,0:T(8,128)(2,1)}, bf16[512,1024]{1,0:T(8,128)(2,1)}, bf16[1024,1024]{1,0:T(8,128)(2,1)},...) custom-call(s32[1]{0:T(128)} %bitcast.1.low_ref, ...), custom_call_target="tpu_custom_call", output_to_operand_aliasing={{0}: (9, {})} | custom-call | flops 8589934592 | bytes 16777216 | tf_op jit(solution)/shard_map/feed_forward/pallas_call | solution.py:419
  332.0 17.9 %feed_forward.6 = (bf16[4096,1024]{1,0:T(8,128)(2,1)}, bf16[512,1024]{1,0:T(8,128)(2,1)}, bf16[512,1024]{1,0:T(8,128)(2,1)}, bf16[1024,1024]{1,0:T(8,128)(2,1)},...) custom-call(s32[1]{0:T(128)} %bitcast.1.low_ref, ...), custom_call_target="tpu_custom_call", output_to_operand_aliasing={{0}: (9, {})} | custom-call | flops 8589934592 | bytes 16777216 | tf_op jit(solution)/shard_map/feed_forward/pallas_call | solution.py:419
  355.4 17.9 %feed_forward.7 = (bf16[4096,1024]{1,0:T(8,128)(2,1)}, bf16[512,1024]{1,0:T(8,128)(2,1)}, bf16[512,1024]{1,0:T(8,128)(2,1)}, bf16[1024,1024]{1,0:T(8,128)(2,1)},...) custom-call(s32[1]{0:T(128)} %bitcast.1.low_ref, ...), custom_call_target="tpu_custom_call", output_to_operand_aliasing={{0}: (9, {})} | custom-call | flops 8589934592 | bytes 16777216 | tf_op jit(solution)/shard_map/feed_forward/pallas_call | solution.py:419
  375.9 15.4 %lift_grad.2 = (bf16[2,256,1024]{2,1,0:T(8,128)(2,1)}, bf16[2,256,1024]{2,1,0:T(8,128)(2,1)}, bf16[2,256,1024]{2,1,0:T(8,128)(2,1)}, bf16[2,256,1024]{2,1,0:T(8,128)(2,1)}) custom-call(s32[1]{0:T(128)} %bitcast.1.low_ref, bf16[1024,1024]{1,0:T(8,128)(2,1)} %get-tuple-element.366.refs_0_, bf16[1024,1024]{1,0:T(8,128)(2,1)} %get-tuple-element.367.refs_1_, ...), custom_call_target="tpu_custom_call" | custom-call | flops 8589934592 | bytes 18874368 | tf_op jit(solution)/shard_map/lift_grad/pallas_call | solution.py:467
  403.8 15.5 %lift_grad.3 = (bf16[2,256,1024]{2,1,0:T(8,128)(2,1)}, bf16[2,256,1024]{2,1,0:T(8,128)(2,1)}, bf16[2,256,1024]{2,1,0:T(8,128)(2,1)}, bf16[2,256,1024]{2,1,0:T(8,128)(2,1)}) custom-call(s32[1]{0:T(128)} %bitcast.1.low_ref, bf16[1024,1024]{1,0:T(8,128)(2,1)} %get-tuple-element.378.refs_0_, ...), custom_call_target="tpu_custom_call", output_to_operand_aliasing={{0}: (6, {}), {1}: (7, {}), {2}: (8, {}), {3}: (9, {})} | custom-call | flops 8589934592 | bytes 18874368 | tf_op jit(solution)/shard_map/lift_grad/pallas_call | solution.py:467
  437.3 24.5 %cross_backward.1 = (bf16[512,1024]{1,0:T(8,128)(2,1)}, bf16[1024,1024]{1,0:T(8,128)(2,1)}, bf16[1024,1024]{1,0:T(8,128)(2,1)}) custom-call(s32[1]{0:T(128)S(6)} %copy.156.length_ref, bf16[512,1024]{1,0:T(8,128)(2,1)} %add_convert_fusion.16.q_ref, bf16[1024,1024]{1,0:T(8,128)(2,1)} %convolution_convert_fusion.k_ref, ...), custom_call_target="tpu_custom_call" | custom-call | flops 21474836480 | bytes 12582912 | tf_op jit(solution)/shard_map/cross_backward/pallas_call | solution.py:334
  542.8 11.9 %collective-permute-start.51 = (f32[2176]{0:T(1024)S(1)}, f32[2176]{0:T(1024)S(1)}, u32[]{:S(2)}, u32[]{:S(2)}) collective-permute-start(f32[2176]{0:T(1024)S(1)} %reduce_sum.505), channel_id=1, source_target_pairs={{0,3},{1,0},{2,1},{3,2},{4,7},{5,4},{6,5},{7,6},{8,11},{9,8},{10,9... | collective-permute-start | bytes 26120 | tf_op jit(solution)/shard_map/ppermute | solution.py:633
  605.7 17.1 %self_backward.5 = (bf16[512,1024]{1,0:T(8,128)(2,1)}, bf16[512,1024]{1,0:T(8,128)(2,1)}, bf16[512,1024]{1,0:T(8,128)(2,1)}, bf16[512,1024]{1,0:T(8,128)(2,1)}, bf16[512,1024]{1,0:T(8,128)(2,1)}) custom-call(s32[1]{0:T(128)} %bitcast.place_ref, bf16[512,1024]{1,0:T(8,128)(2,1)} %add_convert_fusion.22.q_ref, ...), custom_call_target="tpu_custom_call" | custom-call | flops 21474836480 | bytes 16777216 | tf_op jit(solution)/shard_map/self_backward/pallas_call | solution.py:295
  636.3 12.4 %collective-permute-done.47.refs_2_ = bf16[128,5120]{1,0:T(8,128)(2,1)} collective-permute-done((bf16[128,5120]{1,0:T(8,128)(2,1)}, bf16[128,5120]{1,0:T(8,128)(2,1)}, u32[]{:S(2)}, u32[]{:S(2)}) %collective-permute-start.47) | collective-permute-done | bytes 1310752 | tf_op jit(solution)/shard_map/ppermute | solution.py:625
  654.0 12.1 %collective-permute-start.52 = (bf16[128,1280]{1,0:T(8,128)(2,1)}, bf16[128,1280]{1,0:T(8,128)(2,1)S(1)}, u32[]{:S(2)}, u32[]{:S(2)}) collective-permute-start(bf16[128,1280]{1,0:T(8,128)(2,1)} %get-tuple-element.474), channel_id=1, source_target_pairs={{0,3},{1,0},{2,1},{3,2},{4,7},{5,4},{6,5},{7,6},{8,11},{9,8},{10,9... | collective-permute-start | bytes 983048 | tf_op jit(solution)/shard_map/ppermute | solution.py:633
  683.3 9.0 %shard_grad.14 = (bf16[4,128,3072]{2,1,0:T(8,128)(2,1)}, bf16[4,128,3072]{2,1,0:T(8,128)(2,1)}) custom-call(s32[1]{0:T(128)} %bitcast.1.low_ref, bf16[512,1024]{1,0:T(8,128)(2,1)} %fusion.23.refs_0_, bf16[512,1024]{1,0:T(8,128)(2,1)} %fusion.46.refs_1_, bf16[512,1024]{1,0:T(8,128)(2,1)} %fusion.42.refs_2_, ...), custom_call_target="tpu_custom_call", output_to_operand_aliasing={{0}: (9, {}), {1}: (10, {})} | custom-call | flops 4294967296 | bytes 10485760 | tf_op jit(solution)/shard_map/shard_grad/pallas_call | solution.py:511
  761.8 22.7 %all-to-all-done.4 = f32[8,1,512]{2,1,0:T(1,128)S(1)} async-done(((f32[8,1,512]{2,1,0:T(1,128)}), f32[8,1,512]{2,1,0:T(1,128)S(1)}, u32[]{:S(2)}, u32[]{:S(2)}) %all-to-all-start.4) | async-done | bytes 16416 | tf_op jit(solution)/shard_map/all_to_all | solution.py:719
  799.3 10.5 %collective-permute-done.64 = bf16[128,768]{1,0:T(8,128)(2,1)S(1)} collective-permute-done((bf16[128,768]{1,0:T(8,128)(2,1)}, bf16[128,768]{1,0:T(8,128)(2,1)S(1)}, u32[]{:S(2)}, u32[]{:S(2)}) %collective-permute-start.64) | collective-permute-done | bytes 196640 | tf_op jit(solution)/shard_map/ppermute | solution.py:633
  (535 shorter events, 430.4 us)
Async XLA Ops:
  16.9 60.0 %collective-permute-start.3 = (bf16[512,1024]{1,0:T(8,128)(2,1)}, bf16[512,1024]{1,0:T(8,128)(2,1)S(1)}, u32[]{:S(2)}, u32[]{:S(2)}) collective-permute-start(bf16[512,1024]{1,0:T(8,128)(2,1)} %param.29), channel_id=1, source_target_pairs={{0,1},{1,2},{2,3},{4,5},{5,6},{6,7},{8,9},{9,10},{10,11},{12,13},{... | collective-permute-start | bytes 3145736 | tf_op jit(solution)/shard_map/ppermute | solution.py:793
  24.2 52.8 %all-to-all-start = ((bf16[8,2,128,256]{3,2,1,0:T(8,128)(2,1)}), bf16[8,2,128,256]{3,2,1,0:T(8,128)(2,1)S(1)}, u32[]{:S(2)}, u32[]{:S(2)}) async-start(bf16[8,2,128,256]{3,2,1,0:T(8,128)(2,1)} %get-tuple-element.266), calls=%async_computation | async-start | bytes 2097152 | tf_op jit(solution)/shard_map/all_to_all | solution.py:808
  28.0 195.2 %all-gather.3.cloned.1.call-start = ((), (), s32[]{:S(2)}) async-start(), calls=%async_computation.8 | async-start | bytes 2621440 | tf_op jit(solution)/shard_map/all_gather | solution.py:825
  32.4 43.4 %collective-permute-start.1 = (bf16[128,2048]{1,0:T(8,128)(2,1)}, bf16[128,2048]{1,0:T(8,128)(2,1)}, u32[]{:S(2)}, u32[]{:S(2)}) collective-permute-start(bf16[128,2048]{1,0:T(8,128)(2,1)} %get-tuple-element.267.refs_0_), channel_id=1, source_target_pairs={{0,2},{1,3},{2,0},{3,1},{4,6},{5,7},{6,4},{7,5},{8,10},{9,11},{10,... | collective-permute-start | bytes 1572872 | tf_op jit(solution)/shard_map/ppermute | solution.py:633
  33.7 43.2 %collective-permute-start = (bf16[128,2048]{1,0:T(8,128)(2,1)}, bf16[128,2048]{1,0:T(8,128)(2,1)}, u32[]{:S(2)}, u32[]{:S(2)}) collective-permute-start(bf16[128,2048]{1,0:T(8,128)(2,1)} %get-tuple-element.267.refs_0_), channel_id=1, source_target_pairs={{0,1},{1,2},{2,3},{3,0},{4,5},{5,6},{6,7},{7,4},{8,9},{9,10},{10,1... | collective-permute-start | bytes 1572872 | tf_op jit(solution)/shard_map/ppermute | solution.py:633
  117.8 162.9 %all-gather.5.cloned.1.call-start = ((), (), s32[]{:S(2)}) async-start(), calls=%async_computation.9 | async-start | bytes 9437184 | tf_op jit(solution)/shard_map/all_gather | solution.py:811
  118.5 675.6 %reduce-scatter.3.cloned.1.call-start = ((), (), s32[]{:S(2)}) async-start(), calls=%async_computation.10 | async-start | bytes 9437184 | tf_op jit(solution)/shard_map/reduce_scatter | solution.py:900
  120.3 56.4 %collective-permute-start.18 = (bf16[512,1024]{1,0:T(8,128)(2,1)S(1)}, bf16[512,1024]{1,0:T(8,128)(2,1)S(1)}, u32[]{:S(2)}, u32[]{:S(2)}) collective-permute-start(bf16[512,1024]{1,0:T(8,128)(2,1)S(1)} %collective-permute-done.10), channel_id=1, source_target_pairs={{0,1},{1,2},{2,3},{4,5},{5,6},{6,7},{8,9},{9,10},{10,11},{12,13},{... | collective-permute-start | bytes 3145736 | tf_op jit(solution)/shard_map/ppermute | solution.py:824
  136.1 40.6 %collective-permute-start.17 = (bf16[4,128,1280]{2,1,0:T(8,128)(2,1)S(1)}, bf16[4,128,1280]{2,1,0:T(8,128)(2,1)S(1)}, u32[]{:S(2)}, u32[]{:S(2)}) collective-permute-start(bf16[4,128,1280]{2,1,0:T(8,128)(2,1)S(1)} %copy-done.24), channel_id=1, source_target_pairs={{0,24},{4,28},{8,16},{12,20},{16,8},{20,12},{24,0},{28,4},{1,25},{... | collective-permute-start | bytes 3932168 | tf_op jit(solution)/shard_map/ppermute | solution.py:625
  138.0 57.7 %collective-permute-start.16 = (bf16[4,128,1280]{2,1,0:T(8,128)(2,1)S(1)}, bf16[4,128,1280]{2,1,0:T(8,128)(2,1)S(1)}, u32[]{:S(2)}, u32[]{:S(2)}) collective-permute-start(bf16[4,128,1280]{2,1,0:T(8,128)(2,1)S(1)} %copy-done.24), channel_id=1, source_target_pairs={{0,16},{4,20},{8,24},{12,28},{16,0},{20,4},{24,8},{28,12},{1,17},{... | collective-permute-start | bytes 3932168 | tf_op jit(solution)/shard_map/ppermute | solution.py:625
  139.2 56.7 %collective-permute-start.15 = (bf16[4,128,1280]{2,1,0:T(8,128)(2,1)S(1)}, bf16[4,128,1280]{2,1,0:T(8,128)(2,1)}, u32[]{:S(2)}, u32[]{:S(2)}) collective-permute-start(bf16[4,128,1280]{2,1,0:T(8,128)(2,1)S(1)} %copy-done.24), channel_id=1, source_target_pairs={{0,8},{4,12},{8,0},{12,4},{16,24},{20,28},{24,16},{28,20},{1,9},{5... | collective-permute-start | bytes 3932168 | tf_op jit(solution)/shard_map/ppermute | solution.py:625
  474.4 45.5 %collective-permute-start.41 = (bf16[2,256,1024]{2,1,0:T(8,128)(2,1)}, bf16[2,256,1024]{2,1,0:T(8,128)(2,1)}, u32[]{:S(2)}, u32[]{:S(2)}) collective-permute-start(bf16[2,256,1024]{2,1,0:T(8,128)(2,1)} %add_convert_fusion.10), channel_id=1, source_target_pairs={{0,3},{1,0},{2,1},{3,2},{4,7},{5,4},{6,5},{7,6},{8,11},{9,8},{10,9... | collective-permute-start | bytes 3145736 | tf_op jit(solution)/shard_map/ppermute | solution.py:633
  519.9 46.0 %collective-permute-start.42 = (bf16[4,128,5120]{2,1,0:T(8,128)(2,1)}, bf16[4,128,5120]{2,1,0:T(8,128)(2,1)}, u32[]{:S(2)}, u32[]{:S(2)}) collective-permute-start(bf16[4,128,5120]{2,1,0:T(8,128)(2,1)} %get-tuple-element.436), channel_id=1, source_target_pairs={{0,4},{4,0},{8,12},{12,8},{16,20},{20,16},{24,28},{28,24},{1,5},{5... | collective-permute-start | bytes 15728648 | tf_op jit(solution)/shard_map/ppermute | solution.py:625
  561.5 70.4 %all-to-all-start.2 = ((f32[8,1,2176]{2,1,0:T(1,128)}), f32[8,1,2176]{2,1,0:T(1,128)S(1)}, u32[]{:S(2)}, u32[]{:S(2)}) async-start(f32[8,1,2176]{2,1,0:T(1,128)} %broadcast_in_dim.59), calls=%async_computation.3 | async-start | bytes 139264 | tf_op jit(solution)/shard_map/all_to_all | solution.py:719
  583.0 53.3 %collective-permute-start.48 = (bf16[128,5120]{1,0:T(8,128)(2,1)}, bf16[128,5120]{1,0:T(8,128)(2,1)}, u32[]{:S(2)}, u32[]{:S(2)}) collective-permute-start(bf16[128,5120]{1,0:T(8,128)(2,1)} %get-tuple-element.694), channel_id=1, source_target_pairs={{0,24},{4,28},{8,16},{12,20},{16,8},{20,12},{24,0},{28,4},{1,25},{... | collective-permute-start | bytes 3932168 | tf_op jit(solution)/shard_map/ppermute | solution.py:625
  585.9 62.7 %collective-permute-start.47 = (bf16[128,5120]{1,0:T(8,128)(2,1)}, bf16[128,5120]{1,0:T(8,128)(2,1)}, u32[]{:S(2)}, u32[]{:S(2)}) collective-permute-start(bf16[128,5120]{1,0:T(8,128)(2,1)} %get-tuple-element.695), channel_id=1, source_target_pairs={{0,16},{4,20},{8,24},{12,28},{16,0},{20,4},{24,8},{28,12},{1,17},{... | collective-permute-start | bytes 3932168 | tf_op jit(solution)/shard_map/ppermute | solution.py:625
  586.7 62.2 %collective-permute-start.46 = (bf16[128,5120]{1,0:T(8,128)(2,1)}, bf16[128,5120]{1,0:T(8,128)(2,1)}, u32[]{:S(2)}, u32[]{:S(2)}) collective-permute-start(bf16[128,5120]{1,0:T(8,128)(2,1)} %get-tuple-element.696), channel_id=1, source_target_pairs={{0,8},{4,12},{8,0},{12,4},{16,24},{20,28},{24,16},{28,20},{1,9},{5... | collective-permute-start | bytes 3932168 | tf_op jit(solution)/shard_map/ppermute | solution.py:625
  604.2 44.7 %collective-permute-start.45 = (bf16[512,1024]{1,0:T(8,128)(2,1)}, bf16[512,1024]{1,0:T(8,128)(2,1)}, u32[]{:S(2)}, u32[]{:S(2)}) collective-permute-start(bf16[512,1024]{1,0:T(8,128)(2,1)} %add_convert_fusion.8), channel_id=1, source_target_pairs={{1,0},{2,1},{3,2},{5,4},{6,5},{7,6},{9,8},{10,9},{11,10},{13,12},{... | collective-permute-start | bytes 3145736 | tf_op jit(solution)/shard_map/ppermute | solution.py:965
  632.0 77.3 %all-to-all-start.5 = ((bf16[2,256,1024]{1,0,2:T(2,128)(2,1)}), bf16[2,256,1024]{1,0,2:T(2,128)(2,1)}, u32[]{:S(2)}, u32[]{:S(2)}) async-start(bf16[2,256,1024]{1,0,2:T(2,128)(2,1)} %copy.104), calls=%async_computation.7 | async-start | bytes 2097152 | tf_op jit(solution)/shard_map/all_to_all | solution.py:977
  636.2 174.4 %reduce-scatter.5.cloned.1.call-start = ((), (), s32[]{:S(2)}) async-start(), calls=%async_computation.11 | async-start | bytes 2621440 | tf_op jit(solution)/shard_map/reduce_scatter | solution.py:999
  654.0 47.9 %collective-permute-start.52 = (bf16[128,1280]{1,0:T(8,128)(2,1)}, bf16[128,1280]{1,0:T(8,128)(2,1)S(1)}, u32[]{:S(2)}, u32[]{:S(2)}) collective-permute-start(bf16[128,1280]{1,0:T(8,128)(2,1)} %get-tuple-element.474), channel_id=1, source_target_pairs={{0,3},{1,0},{2,1},{3,2},{4,7},{5,4},{6,5},{7,6},{8,11},{9,8},{10,9... | collective-permute-start | bytes 983048 | tf_op jit(solution)/shard_map/ppermute | solution.py:633
  669.5 39.7 %collective-permute-start.55 = (bf16[512,1024]{1,0:T(8,128)(2,1)}, bf16[512,1024]{1,0:T(8,128)(2,1)}, u32[]{:S(2)}, u32[]{:S(2)}) collective-permute-start(bf16[512,1024]{1,0:T(8,128)(2,1)} %get-tuple-element.701), channel_id=1, source_target_pairs={{1,0},{2,1},{3,2},{5,4},{6,5},{7,6},{9,8},{10,9},{11,10},{13,12},{... | collective-permute-start | bytes 3145736 | tf_op jit(solution)/shard_map/ppermute | solution.py:970
  747.2 39.1 %collective-permute-start.62 = (bf16[128,3072]{1,0:T(8,128)(2,1)}, bf16[128,3072]{1,0:T(8,128)(2,1)}, u32[]{:S(2)}, u32[]{:S(2)}) collective-permute-start(bf16[128,3072]{1,0:T(8,128)(2,1)} %get-tuple-element.697), channel_id=1, source_target_pairs={{0,24},{4,28},{8,16},{12,20},{16,8},{20,12},{24,0},{28,4},{1,25},{... | collective-permute-start | bytes 2359304 | tf_op jit(solution)/shard_map/ppermute | solution.py:625
  749.6 36.7 %collective-permute-start.61 = (bf16[128,3072]{1,0:T(8,128)(2,1)}, bf16[128,3072]{1,0:T(8,128)(2,1)}, u32[]{:S(2)}, u32[]{:S(2)}) collective-permute-start(bf16[128,3072]{1,0:T(8,128)(2,1)} %get-tuple-element.698), channel_id=1, source_target_pairs={{0,16},{4,20},{8,24},{12,28},{16,0},{20,4},{24,8},{28,12},{1,17},{... | collective-permute-start | bytes 2359304 | tf_op jit(solution)/shard_map/ppermute | solution.py:625
  (152 other events, 2173.2 us)
Sparse Core Ops, SparseCore 0:
  117.9 72.2 all-gather.2
  192.1 55.1 all-gather.4
  524.3 101.7 reduce-scatter.2
  721.5 49.0 reduce-scatter.4

commit v3 on v2

--- a/solution.py
+++ b/solution.py
@@ -15,7 +15,6 @@
 SCALE = HEAD_DIM ** -0.5
 NEG = -1e30
 CHUNK = 512
-VMEM_LIMIT = 56 * 1024 * 1024
 f32, bf16 = jnp.float32, jnp.bfloat16
 
 
@@ -27,8 +26,8 @@
     return pl.CostEstimate(flops=int(flops), bytes_accessed=int(moved), transcendentals=0)
 
 
-def params():
-    return pltpu.CompilerParams(vmem_limit_bytes=VMEM_LIMIT)
+def params(mib):
+    return pltpu.CompilerParams(vmem_limit_bytes=mib * 1024 * 1024)
 
 
 def move(name, scalars, sources, outs, plan):
@@ -54,7 +53,7 @@
         out_specs=[anywhere] * len(outs),
         out_shape=[jax.ShapeDtypeStruct(s, bf16) for s in outs],
         scratch_shapes=[pltpu.SemaphoreType.DMA((count,))],
-        compiler_params=params(),
+        compiler_params=params(56),
         cost_estimate=cost(0, 4 * sum(x.size for x in sources)),
         name=name,
     )(scalars, *sources)
@@ -166,7 +165,7 @@
             scratch_shapes=[stat, stat, pltpu.VMEM((PAIR, 2 * rows), f32)],
         ),
         out_shape=[jax.ShapeDtypeStruct(q.shape, bf16), lines] if final else [lines, lines, slabs],
-        compiler_params=params(),
+        compiler_params=params(56),
         cost_estimate=cost(16 * count * rows * q.size, 4 * q.size * (1 + count)),
         name="self_forward",
     )(place, q, *[ks[r] for r in blocks], *[vs[r] for r in blocks], bias, *(state or ()))
@@ -202,7 +201,7 @@
             jax.ShapeDtypeStruct(q.shape, bf16),
             jax.ShapeDtypeStruct((pairs, 1, 2 * rows), f32),
         ],
-        compiler_params=params(),
+        compiler_params=params(56),
         cost_estimate=cost(16 * total * q.size, 4 * q.size + 4 * k.size),
         name="cross_forward",
     )(length, q, k, v)
@@ -302,7 +301,7 @@
             scratch_shapes=[pltpu.VMEM((PAIR, 2 * rows), f32)],
         ),
         out_shape=[jax.ShapeDtypeStruct(q.shape, bf16 if last else f32)] + [shape] * (2 * count),
-        compiler_params=params(),
+        compiler_params=params(56),
         cost_estimate=cost(40 * count * rows * q.size, 8 * q.size * (2 + count)),
         name="self_backward",
     )(place, *args)
@@ -345,7 +344,7 @@
             jax.ShapeDtypeStruct(k.shape, bf16),
             jax.ShapeDtypeStruct(k.shape, bf16),
         ],
-        compiler_params=params(),
+        compiler_params=params(56),
         cost_estimate=cost(40 * total * q.size, 8 * q.size + 8 * k.size),
         name="cross_backward",
     )(length, q, k, v, o, do, lse)
@@ -371,7 +370,7 @@
 
     def kernel(low_ref, r0_ref, r1_ref, g_ref, *refs):
         w_refs, ub_ref = refs[:count], refs[count]
-        out_ref, back0, back1, inner_ref, grad_ref, sums_ref, r_ref, back_s = refs[count + 1 + given :]
+        out_ref, back0, back1, inner_ref, grad_ref, sums_ref, r_ref, back_s, inner_s, grad_s = refs[count + 1 + given :]
         i = pl.program_id(0)
 
         @pl.when(i == 0)
@@ -391,14 +390,15 @@
             lifted = dot(r_ref[...], ups[n]) + ub_ref[:, cols]
             grad_inner = dot(g_ref[...], downs[n])
             value, slope = gelu_pair(lifted)
-            inner_ref[:, cols] = value.astype(bf16)
+            inner = value.astype(bf16)
             grad = (grad_inner * slope).astype(bf16)
-            grad_ref[:, cols] = grad
+            inner_s[:, cols], grad_s[:, cols] = inner, grad
+            inner_ref[cols, :], grad_ref[cols, :] = inner.T, grad.T
             sums_ref[:, cols] += jnp.sum(grad.astype(f32), axis=0, keepdims=True)
         for n in range(count):
             cols = slice(n * part, (n + 1) * part)
-            o = dot(inner_ref[:, cols], downs[n], 1, 1)
-            b = dot(grad_ref[:, cols], ups[n], 1, 1)
+            o = dot(inner_s[:, cols], downs[n], 1, 1)
+            b = dot(grad_s[:, cols], ups[n], 1, 1)
             out, back = (o, b) if n == 0 else (out + o, back + b)
         out_ref[...] = out.astype(bf16)
         back_s[...] = back.astype(bf16)
@@ -413,9 +413,9 @@
 
     whole = lambda x: pl.BlockSpec(x.shape, lambda i, s: (0,) * x.ndim)
     row = jax.ShapeDtypeStruct((rows, width), bf16)
-    tall = jax.ShapeDtypeStruct((2 * rows, hidden), bf16)
-    tall_spec = pl.BlockSpec((rows, hidden), lambda i, s: (i, 0))
-    by_device = pl.BlockSpec((rows, width), lambda i, s: (s[0] ^ (pair + i), 0))
+    tall = jax.ShapeDtypeStruct((hidden, 2 * rows), bf16)
+    tall_spec = pl.BlockSpec((hidden, rows), lambda i, s: (0, i))
+    by_device = pl.BlockSpec((rows, width), lambda i, s: (s[0] ^ (pair[0] + (pair[1] - pair[0]) * i), 0))
     return pl.pallas_call(
         kernel,
         grid_spec=pltpu.PrefetchScalarGridSpec(
@@ -425,128 +425,164 @@
             + [whole(x) for x in lifts] + [whole(ub)]
             + [pl.BlockSpec(memory_space=pl.ANY)] * given,
             out_specs=[by_device] + [whole(r0)] * 2 + [tall_spec] * 2 + [whole(ub)],
-            scratch_shapes=[pltpu.VMEM((rows, width), bf16)] * 2,
+            scratch_shapes=[pltpu.VMEM((rows, width), bf16)] * 2
+            + [pltpu.VMEM((rows, hidden), bf16)] * 2,
         ),
         out_shape=[jax.ShapeDtypeStruct(cots.shape, bf16)] + [row] * 2 + [tall] * 2
         + [jax.ShapeDtypeStruct(ub.shape, f32)],
         input_output_aliases={5 + count: 0} if given else {},
-        compiler_params=params(),
+        compiler_params=params(56),
         cost_estimate=cost(16 * rows * width * hidden, 24 * rows * width + 4 * hidden * width),
         name="feed_forward",
     )(low, r0, r1, cots, *lifts, ub, *([outs] if given else []))
 
 
-def lift_grad(low, lefts, rights, place, before):
+def lift_grad(scalars, lefts, rights, order, half, before):
     ordered = not isinstance(rights, list)
     ins = [rights] if ordered else rights
-    hidden, wide = lefts[0].shape[1], ins[0].shape[1]
+    hidden, wide = lefts[0].shape[0], ins[0].shape[1]
     count = len(lefts)
-    piece = lefts[0].shape[0] // 2
+    piece = lefts[0].shape[1] // 2
     tiles, given = 4, 0 if before is None else 4
     tile = hidden // tiles
 
-    def kernel(low_ref, *refs):
-        l_refs, r_refs = refs[:count], refs[count : count + len(ins)]
-        out_refs = refs[count + len(ins) + given :]
+    def kernel(scalars_ref, *refs):
+        l_refs, r_refs = refs[: 2 * count], refs[2 * count : 2 * count + len(ins)]
+        out_refs = refs[2 * count + len(ins) + given :]
         total = None
-        for k in range(2 * count):
-            if ordered:
-                right = r_refs[0][pl.ds(pl.multiple_of((low_ref[0] ^ k) * piece, piece), piece), :]
-            else:
-                right = r_refs[k][...]
-            start = (k % 2) * piece
-            part = dot(l_refs[k // 2][start : start + piece, :], right, 0, 0)
-            total = part if total is None else total + part
+        for n in range(count):
+            both = jnp.concatenate([l_refs[2 * n][...], l_refs[2 * n + 1][...]], axis=0)
+            for h in range(2):
+                if ordered:
+                    start = (scalars_ref[0] ^ order[2 * n + h]) * piece
+                    right = r_refs[0][pl.ds(pl.multiple_of(start, piece), piece), :]
+                else:
+                    right = r_refs[2 * n + h][...]
+                part = dot(both[:, h * piece : (h + 1) * piece], right)
+                total = part if total is None else total + part
         total = total.astype(bf16)
         for n in range(tiles):
-            @pl.when(pl.program_id(0) == n)
+            @pl.when(pl.program_id(0) == n // 2)
             def _(n=n):
-                out_refs[n][0] = total
+                out_refs[n][0] = total[(n % 2) * tile : (n % 2 + 1) * tile]
+
+    def quarter(h):
+        return pl.BlockSpec((tile, 2 * piece), lambda i, s: (2 * i + h, 0))
 
     depth = 2 * count * piece
     return pl.pallas_call(
         kernel,
         grid_spec=pltpu.PrefetchScalarGridSpec(
             num_scalar_prefetch=1,
-            grid=(tiles,),
-            in_specs=[pl.BlockSpec((2 * piece, tile), lambda i, s: (0, i))] * count
+            grid=(2,),
+            in_specs=[quarter(0), quarter(1)] * count
             + [pl.BlockSpec(x.shape, lambda i, s: (0, 0)) for x in ins]
             + [pl.BlockSpec(memory_space=pl.ANY)] * given,
-            out_specs=[pl.BlockSpec((1, tile, wide), lambda i, s: (place, 0, 0))] * tiles,
+            out_specs=[pl.BlockSpec((1, tile, wide), lambda i, s: (half, 0, 0))] * tiles,
         ),
         out_shape=[jax.ShapeDtypeStruct((2, tile, wide), bf16)] * tiles,
-        input_output_aliases={1 + count + len(ins) + n: n for n in range(given)},
-        compiler_params=params(),
+        input_output_aliases={1 + 2 * count + len(ins) + n: n for n in range(given)},
+        compiler_params=params(56),
         cost_estimate=cost(2 * depth * hidden * wide, 2 * depth * (hidden + wide) + 2 * hidden * wide),
         name="lift_grad",
-    )(low, *lefts, *ins, *(before or ()))
-
-
-def shard_grad(low, lefts, rights, column, columns, before):
-    high, wide = lefts[0].shape[1], rights[0].shape[1]
-    count = len(lefts)
-    rows = high // 8
-    given = 0 if before is None else 2
+    )(scalars, *[x for left in lefts for x in (left, left)], *ins, *(before or ()))
+
+
+def shard_grads(low, products):
+    lefts = [x for p in products for x in p[0]]
+    rights = [x for p in products for x in p[1]]
+    spans = []
+    for p in products:
+        start = spans[-1][1] if spans else 0
+        spans.append((start, start + len(p[0])))
+    count, wide = len(lefts), rights[0].shape[1]
+    rows = lefts[0].shape[1] // 8
 
     def kernel(low_ref, *refs):
-        even_ref, odd_ref = refs[2 * count + given :]
-        total = None
-        for l_ref, r_ref in zip(refs[:count], refs[count : 2 * count]):
-            part = dot(l_ref[...], r_ref[...], 0, 0)
-            total = part if total is None else total + part
-        total = total.astype(bf16)
-
-        @pl.when((low_ref[0] & 1) == 0)
+        l_refs, r_refs = refs[:count], refs[count : 2 * count]
+        even_ref, odd_ref = refs[2 * count : 2 * count + 2]
+        bufs, sems = refs[2 * count + 2 : -1], refs[-1]
+        step = pl.program_id(0)
+        copies = [pltpu.make_async_copy(r_refs[n], bufs[n], sems.at[n]) for n in range(count)]
+
+        @pl.when(step == 0)
         def _():
-            even_ref[0] = total[:rows]
-            odd_ref[0] = total[rows:]
-
-        @pl.when((low_ref[0] & 1) == 1)
-        def _():
-            even_ref[0] = total[rows:]
-            odd_ref[0] = total[:rows]
-
+            for copy in copies:
+                copy.start()
+
+        for p, (start, stop) in enumerate(spans):
+            @pl.when(step == 2 * p)
+            def _(start=start, stop=stop):
+                for n in range(start, stop):
+                    copies[n].wait()
+
+            @pl.when(step // 2 == p)
+            def _(start=start, stop=stop):
+                total = None
+                for n in range(start, stop):
+                    part = dot(l_refs[n][...], bufs[n][...], 0, 0)
+                    total = part if total is None else total + part
+                total = total.astype(bf16)
+                swap = (low_ref[0] & 1) == 1
+                for h in range(2):
+                    first = total[2 * h * rows : (2 * h + 1) * rows]
+                    second = total[(2 * h + 1) * rows : (2 * h + 2) * rows]
+                    spot = ((low_ref[0] >> 1) & 1) ^ h
+                    even_ref[spot] = jnp.where(swap, second, first)
+                    odd_ref[spot] = jnp.where(swap, first, second)
+
+    def tile(p):
+        return lambda i, s: (0, jnp.clip(i - 2 * p, 0, 1))
+
+    specs = [
+        pl.BlockSpec((lefts[n].shape[0], 4 * rows), tile(p))
+        for p, (start, stop) in enumerate(spans)
+        for n in range(start, stop)
+    ]
     depth = sum(x.shape[0] for x in lefts)
-    shape = jax.ShapeDtypeStruct((4, rows, columns * wide), bf16)
+    shape = jax.ShapeDtypeStruct((4, rows, len(products) * wide), bf16)
     return pl.pallas_call(
         kernel,
         grid_spec=pltpu.PrefetchScalarGridSpec(
             num_scalar_prefetch=1,
-            grid=(4,),
-            in_specs=[pl.BlockSpec((x.shape[0], 2 * rows), lambda i, s: (0, i)) for x in lefts]
-            + [pl.BlockSpec(x.shape, lambda i, s: (0, 0)) for x in rights]
-            + [pl.BlockSpec(memory_space=pl.ANY)] * given,
-            out_specs=[pl.BlockSpec((1, rows, wide), lambda i, s: ((s[0] >> 1) ^ i, 0, column))] * 2,
+            grid=(2 * len(products),),
+            in_specs=specs + [pl.BlockSpec(memory_space=pl.ANY)] * count,
+            out_specs=[pl.BlockSpec((2, rows, wide), lambda i, s: ((s[0] >> 2) ^ (i % 2), 0, i // 2))] * 2,
+            scratch_shapes=[pltpu.VMEM(x.shape, bf16) for x in rights] + [pltpu.SemaphoreType.DMA((count,))],
         ),
         out_shape=[shape] * 2,
-        input_output_aliases={1 + 2 * count: 0, 2 + 2 * count: 1} if given else {},
-        compiler_params=params(),
-        cost_estimate=cost(2 * depth * high * wide, 2 * depth * (high + wide) + 2 * high * wide),
-        name="shard_grad",
-    )(low, *lefts, *rights, *(before or ()))
-
-
-def pack_shards(shards, turned, up, down):
-    rows, cols = shards[0].shape
-    flat = [*shards, up, down]
+        compiler_params=params(56),
+        cost_estimate=cost(16 * depth * rows * wide, 2 * depth * (8 * rows + wide)),
+        name="shard_grads",
+    )(low, *lefts, *rights)
+
+
+def pack_shards(ones, twos, up, down):
+    rows, cols = ones[0].shape
+    flat = [*ones, *twos, up, down]
     part = up.shape[1] // 8
 
     def kernel(*refs):
-        up_ref, down_ref, out_ref, lift_ref = refs[len(shards) :]
-        for i, ref in enumerate(refs[: len(shards)]):
-            out_ref[:, i * cols : (i + 1) * cols] = ref[...].T if i in turned else ref[...]
+        one_refs, two_refs = refs[: len(ones)], refs[len(ones) : len(ones) + len(twos)]
+        up_ref, down_ref, out_one, out_two, out_lift = refs[len(flat) - 2 :]
+        for i, ref in enumerate(one_refs):
+            out_one[:, i * cols : (i + 1) * cols] = ref[...]
+        for i, ref in enumerate(two_refs):
+            x = ref[...].T if i in (0, len(twos) - 1) else ref[...]
+            out_two[:, i * cols : (i + 1) * cols] = x
         for d in range(8):
             span = slice(d * part, (d + 1) * part)
-            lift_ref[d, 0] = up_ref[:, span]
-            lift_ref[d, 1] = down_ref[span, :].T
+            out_lift[d, 0] = up_ref[:, span]
+            out_lift[d, 1] = down_ref[span, :].T
 
     return pl.pallas_call(
         kernel,
         out_shape=[
-            jax.ShapeDtypeStruct((rows, len(shards) * cols), bf16),
+            jax.ShapeDtypeStruct((rows, len(ones) * cols), bf16),
+            jax.ShapeDtypeStruct((rows, len(twos) * cols), bf16),
             jax.ShapeDtypeStruct((8, 2, rows, part), bf16),
         ],
-        compiler_params=params(),
+        compiler_params=params(56),
         cost_estimate=cost(0, 4 * sum(x.size for x in flat)),
         name="pack_shards",
     )(*flat)
@@ -579,10 +615,101 @@
             scratch_shapes=[pltpu.VMEM((rows, wide), f32)],
         ),
         out_shape=[jax.ShapeDtypeStruct((rows, count * part), f32 if r == 0 else bf16) for r in range(size)],
-        compiler_params=params(),
+        compiler_params=params(56),
         cost_estimate=cost(0, 4 * sum(x.size for x in pieces)),
         name="sum_columns",
     )(place, *pieces)
+
+
+def row_sums(x):
+    return jnp.mean(x, axis=-1, keepdims=True)
+
+
+def norm_backward(rows, gain, pieces, residual, sums, tile=128):
+    count, width = rows.shape
+
+    def kernel(rows_ref, gain_ref, residual_ref, *refs):
+        grads, outs = refs[: len(pieces)], refs[len(pieces) :]
+        x = rows_ref[...].astype(f32)
+        centered = x - row_sums(x)
+        scale = lax.rsqrt(row_sums(centered * centered) + EPSILON)
+        xhat = centered * scale
+        grad = grads[0][...].astype(f32)
+        for g in grads[1:]:
+            grad = grad + g[...].astype(f32)
+        scaled = grad * gain_ref[...]
+        back = scale * (scaled - row_sums(scaled) - xhat * row_sums(scaled * xhat))
+        out = residual_ref[...].astype(f32) + back
+        outs[0][...] = out
+        if sums:
+            short = out.astype(bf16)
+            outs[1][...] = short
+
+            @pl.when(pl.program_id(0) == 0)
+            def _():
+                outs[2][...] = jnp.zeros_like(outs[2])
+
+            for n, v in enumerate((grad * xhat, grad, short.astype(f32))):
+                outs[2][n : n + 1, :] += jnp.sum(v, axis=0, keepdims=True)
+
+    row = pl.BlockSpec((tile, width), lambda i: (i, 0))
+    shape = jax.ShapeDtypeStruct((count, width), f32)
+    return pl.pallas_call(
+        kernel,
+        grid=(count // tile,),
+        in_specs=[row, pl.BlockSpec((1, width), lambda i: (0, 0)), row] + [row] * len(pieces),
+        out_specs=[row, row, pl.BlockSpec((3, width), lambda i: (0, 0))] if sums else [row],
+        out_shape=[
+            shape,
+            jax.ShapeDtypeStruct((count, width), bf16),
+            jax.ShapeDtypeStruct((3, width), f32),
+        ]
+        if sums
+        else [shape],
+        compiler_params=params(56),
+        cost_estimate=cost(0, 12 * rows.size),
+        name="norm_backward",
+    )(rows, gain[None], residual, *pieces)
+
+
+def share_grad(grads, weights, rows, before, final):
+    count, width = rows.shape
+    tile = count
+    given = 0 if before is None else 1
+
+    def kernel(*refs):
+        g_refs, w_refs = refs[: len(grads)], refs[len(grads) : 2 * len(grads)]
+        rows_ref, rest = refs[2 * len(grads)], refs[2 * len(grads) + 1 :]
+        out_ref, sums_ref = rest[given:]
+        share = dot(g_refs[0][...], w_refs[0][...], 1, 1)
+        for g, w in zip(g_refs[1:], w_refs[1:]):
+            share = share + dot(g[...], w[...], 1, 1)
+        x = rows_ref[...].astype(f32)
+        centered = x - row_sums(x)
+        xhat = centered * lax.rsqrt(row_sums(centered * centered) + EPSILON)
+
+        sums_ref[0:1, :] = jnp.sum(share * xhat, axis=0, keepdims=True)
+        sums_ref[1:2, :] = jnp.sum(share, axis=0, keepdims=True)
+        if given:
+            share = share + rest[0][...].astype(f32)
+        out_ref[...] = share.astype(out_ref.dtype)
+
+    row = pl.BlockSpec((tile, width), lambda i: (i, 0))
+    return pl.pallas_call(
+        kernel,
+        grid=(1,),
+        in_specs=[row] * len(grads)
+        + [pl.BlockSpec(w.shape, lambda i: (0, 0)) for w in weights]
+        + [row] * (1 + given),
+        out_specs=[row, pl.BlockSpec((2, width), lambda i: (0, 0))],
+        out_shape=[
+            jax.ShapeDtypeStruct((count, width), f32 if final else bf16),
+            jax.ShapeDtypeStruct((2, width), f32),
+        ],
+        compiler_params=params(56),
+        cost_estimate=cost(2 * len(grads) * count * width * width, 6 * rows.size),
+        name="share_grad",
+    )(*grads, *weights, rows, *([before] if given else []))
 
 
 def normed(rows, gain, shift):
@@ -651,18 +778,12 @@
     )
 
 
-def stack_shards(scalars, pieces, first, count):
-    rows, wide = pieces[0].shape
-    cut = wide // count * first
-    every = slice(None)
-    return move(
-        "stack_shards", scalars, pieces, [(len(pieces), rows, cut), (len(pieces), rows, wide - cut)],
-        lambda s: [
-            (r, (every, pl.ds(start, extent)), part, (r, every, every))
-            for r in range(len(pieces))
-            for part, (start, extent) in enumerate([(0, cut), (cut, wide - cut)])
-        ],
+def stack_shards(scalars, pieces):
+    (stacked,) = move(
+        "stack_shards", scalars, pieces, [(len(pieces), *pieces[0].shape)],
+        lambda s: [(r, (slice(None), slice(None)), 0, (r,)) for r in range(len(pieces))],
     )
+    return stacked
 
 
 def unpack_weights(scalars, pieces, count, sizes):
@@ -696,27 +817,20 @@
     return own + back[0] + back[1] + back[2]
 
 
-def shard_grads(low, grads):
-    before = None
-    for i, (lefts, rights) in enumerate(grads):
-        before = shard_grad(low, lefts, rights, i, len(grads), before)
-    return before
-
-
 def whole_shards(parts, turned, count):
     shard = parts[0] + sum(x.astype(f32) for x in turned)
     return jnp.split(shard, count, axis=1)
 
 
-def sum_vector(vector, sizes):
-    size = sizes[2]
+def sum_tensor(vector, sizes):
     if sizes[0] > 1:
         vector = lax.psum(vector, "high")
-    slices = lax.all_to_all(vector.reshape(8, -1), "low", split_axis=0, concat_axis=0, tiled=True)
-    mine = jnp.sum(slices, axis=0)
-    mine = mine + sum(turn(mine, r, size) for r in range(1, size))
-    spread = jnp.broadcast_to(mine, (8, *mine.shape))
-    return lax.all_to_all(spread, "low", split_axis=0, concat_axis=0, tiled=True).reshape(-1)
+    return vector + sum(turn(vector, r, sizes[2]) for r in range(1, sizes[2]))
+
+
+def sum_low(vector):
+    spread = jnp.broadcast_to(vector, (8, *vector.shape))
+    return jnp.sum(lax.all_to_all(spread, "low", split_axis=0, concat_axis=0, tiled=True), axis=0)
 
 
 def path_bias(parents, place, own, blocks):
@@ -782,19 +896,24 @@
         up_chain = [(i, i + 1) for i in range(size - 1)]
         down_chain = [(i + 1, i) for i in range(size - 1)]
 
-        a, lift = pack_shards(
-            [
-                self_query, self_key, self_value,
-                self_out, cross_query, cross_key, cross_value, cross_out,
-            ],
-            (3, 7), up_weight, down_weight,
-        )
-        z = [turn(a, r, size) for r in range(1, size)]
-        blocks = [tokens, lax.ppermute(tokens, "tensor", up_chain)]
+        first, second, lift = pack_shards(
+            [self_query, self_key, self_value],
+            [self_out, cross_query, cross_key, cross_value, cross_out],
+            up_weight, down_weight,
+        )
+        part = width // size
+        hidden = up_weight.shape[1] // 8
+        z = [turn(first, r, size) for r in range(1, size)]
         ones = [normed(tokens.astype(f32), first_gain, first_shift)]
         bias = path_bias(parents[0], place, rows // SEG, size)
-        part = width // size
-        hidden = up_weight.shape[1] // 8
+        lift = lax.all_to_all(lift, "low", split_axis=0, concat_axis=0, tiled=True)
+        if sizes[0] > 1:
+            lift = lax.all_gather(lift, "high", axis=0, tiled=True)
+        first, second, z, ones, bias, tokens_sent = together(first, second, z, ones, bias, tokens)
+
+        even_a = gather_chips(stack_shards(scalars, [first, *z]))
+        blocks = [tokens, lax.ppermute(tokens_sent, "tensor", up_chain)]
+        z = [turn(second, 1, size)]
         biases = jnp.concatenate(
             [
                 self_query_bias, self_value_bias, cross_query_bias, cross_value_bias,
@@ -805,43 +924,49 @@
         ub = jnp.concatenate([x[4 * part :] for x in biases])[None]
         placed = by_place([x[: 4 * part] for x in biases], place).reshape(size, 4, part)
         q_bias, v_bias, xq_bias, xv_bias = [placed[:, i].reshape(width) for i in range(4)]
-        lift = lax.all_to_all(lift, "low", split_axis=0, concat_axis=0, tiled=True)
-        if sizes[0] > 1:
-            lift = lax.all_gather(lift, "high", axis=0, tiled=True)
-        cots = lax.all_gather(cotangent, "low", axis=0, tiled=True)
-        a, lift, z, blocks, ones, bias, ub, q_bias, v_bias, xq_bias, xv_bias = together(
-            a, lift, z, blocks, ones, bias, ub, q_bias, v_bias, xq_bias, xv_bias
-        )
-
-        packed_a, packed_b = stack_shards(scalars, [a, *z], 3, 8)
-        even_a = gather_chips(packed_a)
-        blocks = blocks + [lax.ppermute(blocks[-1], "tensor", up_chain)]
-        ones = ones + [normed(blocks[1].astype(f32), first_gain, first_shift)]
-        even_a, packed_b, blocks, ones, encoded = together(even_a, packed_b, blocks, ones, encoded)
+        even_a, second, z[0], blocks, ub, q_bias, v_bias, xq_bias, xv_bias, encoded, lift = together(
+            even_a, second, z[0], blocks, ub, q_bias, v_bias, xq_bias, xv_bias, encoded, lift
+        )
 
         all_a = gather_cores(even_a)
-        even_b = gather_chips(packed_b)
-        blocks = blocks + [lax.ppermute(blocks[-1], "tensor", up_chain)]
+        blocks.append(lax.ppermute(blocks[-1], "tensor", up_chain))
         source = lax.all_gather(encoded, "tensor", axis=0, tiled=True)
+        z = z + [turn(second, r, size) for r in range(2, size)]
         wq, wk, wv = unpack_weights(scalars, all_a, 3, sizes)
-        ones = ones + [normed(blocks[2].astype(f32), first_gain, first_shift)]
         q1 = (dot(ones[0], wq) + q_bias).astype(bf16)
-        ks = [dot(n, wk).astype(bf16) for n in ones]
-        vs = [(dot(n, wv) + v_bias).astype(bf16) for n in ones]
-        state = self_forward(place_1, q1, ks, vs, bias, range(size - 1), None, False)
-        even_b, blocks, state, lift = together(even_b, blocks, state, lift)
-
-        lifts = [lift, turn(lift, 1, size)]
-        all_b = gather_cores(even_b)
-        ones = ones + [normed(blocks[size - 1].astype(f32), first_gain, first_shift)]
-        ks = ks + [dot(ones[-1], wk).astype(bf16)]
-        vs = vs + [(dot(ones[-1], wv) + v_bias).astype(bf16)]
-        mixed_one, lse_one = self_forward(
-            place_1, q1, ks, vs, bias, (size - 1,), state, True
-        )
-        mixed_one, all_b, lifts, source = together(mixed_one, all_b, lifts, source)
-
+        ks, vs, state, mixed_one = [], [], None, None
+        for r in range(size):
+            if r:
+                ones.append(normed(blocks[r].astype(f32), first_gain, first_shift))
+            ks.append(dot(ones[r], wk).astype(bf16))
+            vs.append((dot(ones[r], wv) + v_bias).astype(bf16))
+            if r == 0:
+                continue
+            if r == 1:
+                q1, ks, vs, second, z = together(q1, ks, vs, second, z)
+                packed_b = stack_shards(scalars, [second, *z])
+                even_b = [packed_b, flip(packed_b, 2), flip(packed_b, 4)]
+            seen = (0, 1) if r == 1 else (r,)
+            if r < size - 1:
+                state = self_forward(place_1, q1, ks, vs, bias, seen, state, False)
+            else:
+                mixed_one, lse_one = self_forward(place_1, q1, ks, vs, bias, seen, state, True)
+            if r == 1:
+                state, blocks, even_b = together(state, blocks, even_b)
+                even_b.append(flip(even_b[0], 6))
+                blocks.append(lax.ppermute(blocks[-1], "tensor", up_chain))
+            elif r < size - 1:
+                if r < size - 2:
+                    blocks.append(lax.ppermute(blocks[-1], "tensor", up_chain))
+                state, blocks, even_b, cots_sent, lift = together(
+                    state, blocks, even_b, cotangent, lift
+                )
+                cots = lax.all_gather(cots_sent, "low", axis=0, tiled=True)
+                all_b = gather_cores(even_b)
+                lifts = [lift, turn(lift, 1, size)]
+        mixed_one, all_b, lifts = together(mixed_one, all_b, lifts)
         lifts = lifts + [turn(lifts[-1], 1, size)]
+
         wo, xq, xk, xv, xo = unpack_weights(scalars, all_b, 5, sizes)
         hidden_one = tokens.astype(f32) + dot(mixed_one, wo, 1, 1) + self_out_bias
         two = normed(hidden_one, second_gain, second_shift)
@@ -856,44 +981,40 @@
         three = normed(hidden_two, third_gain, third_shift)
         three, lifts = together(three, lifts)
 
-        x2, x4 = flip(three, 2), flip(three, 4)
-        c0 = flip(three, 1)
-        outs, firsts, lasts, inners, grads, up_sums, threes = None, [], [], [], [], [], []
-        evens = [three, x2, x4, None]
-        for n, k in enumerate(range(0, 8, 2)):
-            if n == 0:
-                pair = (three, c0)
-            elif n == 1:
-                three_sent, x2, x4, firsts[0] = together(three, x2, x4, firsts[0])
-                evens = [three, x2, x4, flip(three_sent, 6)]
-                pair = (x2, flip(x2, 1))
-            else:
-                pair = (evens[n], flip(evens[n], 1))
-                pair, firsts[n - 2], lasts[n - 2] = together(pair, firsts[n - 2], lasts[n - 2])
-            threes += pair
-            outs, back0, back1, inner, grad, sums = feed_forward(
-                low_1, k, *pair, cots, lifts, ub, outs
-            )
-            firsts.append(back0)
-            lasts.append(flip(back1, 1))
-            inners.append(inner)
-            grads.append(grad)
-            up_sums.append(sums)
-        own = firsts[0].astype(f32) + lasts[0].astype(f32)
-        back = [add_pair(firsts[n], lasts[n]) for n in (1, 2)]
-        grads, back = together(grads, back)
-        back = [flip(back[0], 2), flip(back[1], 4)]
-        lift_shares = lift_grad(low_1, grads, threes, 0, None)
-        inners, lift_shares, firsts[3], lasts[3], back = together(
-            inners, lift_shares, firsts[3], lasts[3], back
-        )
-        back.append(flip(add_pair(firsts[3], lasts[3]), 6))
-        lift_shares = lift_grad(low_1, inners, cots, 1, lift_shares)
-        lift_shares, back, own = together(lift_shares, back, own)
-        grad_three = own + sum(x.astype(f32) for x in back)
-
-        grad_hidden_two = cotangent.astype(f32) + norm_back(hidden_two, third_gain, grad_three)
-        grad_two = grad_hidden_two.astype(bf16)
+        x2, x4, c0 = flip(three, 2), flip(three, 4), flip(three, 1)
+
+        def lift_pair(pair, r0, r1, outs):
+            return feed_forward(low_1, pair, r0, r1, cots, lifts, ub, outs)
+
+        outs, own, got, inner_0, grad_0, sums_0 = lift_pair((0, 1), three, c0, None)
+        own_got = flip(got, 1)
+        three_sent, x2, x4, own = together(three, x2, x4, own)
+        c2, c4, x6 = flip(x2, 1), flip(x4, 1), flip(three_sent, 6)
+        outs, back_2, back_4, inner_1, grad_1, sums_1 = lift_pair((2, 4), x2, x4, outs)
+        c2, c4, back_2, own_got = together(c2, c4, back_2, own_got)
+        outs, got_2, got_4, inner_2, grad_2, sums_2 = lift_pair((3, 5), c2, c4, outs)
+        x6, got_2 = together(x6, got_2)
+        got_2, got_4, c6 = flip(got_2, 1), flip(got_4, 1), flip(x6, 1)
+        outs, back_6, got_6, inner_3, grad_3, sums_3 = lift_pair((6, 7), x6, c6, outs)
+        back_6, got_2, got_4 = together(back_6, got_2, got_4)
+        back_2, back_4 = flip(add_pair(back_2, got_2), 2), flip(add_pair(back_4, got_4), 4)
+        got_6 = flip(got_6, 1)
+        order = (0, 1, 2, 4, 3, 5, 6, 7)
+        lift_shares = lift_grad(
+            scalars, [grad_0, grad_1, grad_2, grad_3], [three, c0, x2, x4, c2, c4, x6, c6], order, 0, None
+        )
+        back_6, got_6, back_2, back_4, lift_shares = together(
+            back_6, got_6, back_2, back_4, lift_shares
+        )
+        back_6 = flip(add_pair(back_6, got_6), 6)
+        lift_shares = lift_grad(
+            scalars, [inner_0, inner_1, inner_2, inner_3], cots, order, 1, lift_shares
+        )
+        up_sums = [sums_0, sums_1, sums_2, sums_3]
+        lift_shares, back_6 = together(lift_shares, back_6)
+        grad_hidden_two, grad_two, sums_three = norm_backward(
+            hidden_two, third_gain, [own, own_got, back_2, back_4, back_6], cotangent, True
+        )
         do2 = dot(grad_two, xo).astype(bf16)
         do2, outs, lift_shares = together(do2, outs, lift_shares)
 
@@ -903,11 +1024,16 @@
         dq2, dk2, dv2, lift_got = together(dq2, dk2, dv2, lift_got)
 
         lift_got = turn(add_pair(lift_shares[size - 2], lift_got), size - 1, size)
-        grad_two_normed = dot(dq2, xq, 1, 1)
-        grad_hidden_one = grad_hidden_two + norm_back(hidden_one, second_gain, grad_two_normed)
-        grad_one = grad_hidden_one.astype(bf16)
+        grad_hidden_one, grad_one, sums_two = norm_backward(
+            hidden_one, second_gain, [dot(dq2, xq, 1, 1)], grad_hidden_two, True
+        )
         do1 = dot(grad_one, wo).astype(bf16)
-        b_even, b_odd = shard_grads(
+        encoded_part = (dot(dk2, xk, 1, 1) + dot(dv2, xv, 1, 1)).astype(bf16)
+        early = column_sums(cotangent), column_sums(dq2), column_sums(dv2)
+        do1, lift_got, encoded_part, early = together(do1, lift_got, encoded_part, early)
+
+        lift_got = turn(add_pair(lift_shares[size - 3], lift_got), size - 1, size)
+        b_laid = shard_grads(
             low_1,
             [
                 ([grad_one], [mixed_one]),
@@ -917,101 +1043,102 @@
                 ([grad_two], [mixed_two]),
             ],
         )
-        encoded_part = (dot(dk2, xk, 1, 1) + dot(dv2, xv, 1, 1)).astype(bf16)
         spread = by_place([sum(up_sums)[0, r * hidden : (r + 1) * hidden] for r in range(size)], place)
         spread = lax.dynamic_update_slice(
             jnp.zeros((size, up_bias.shape[0]), f32), spread, (0, low * hidden)
         )
         early = jnp.concatenate(
             [
-                *norm_sums(hidden_one, grad_two_normed),
-                *norm_sums(hidden_two, grad_three),
-                column_sums(grad_one),
-                column_sums(grad_two),
-                column_sums(cotangent),
-                column_sums(dq2),
-                column_sums(dv2),
+                sums_two.reshape(-1),
+                sums_three.reshape(-1),
+                *early,
                 spread.reshape(-1),
             ]
         )
-        do1, b_even, b_odd, lift_got, encoded_part, early = together(
-            do1, b_even, b_odd, lift_got, encoded_part, early
-        )
-
-        lift_got = turn(add_pair(lift_shares[size - 3], lift_got), size - 1, size)
+        (b_even, b_odd), do1, lift_got, encoded_part, early = together(
+            b_laid, do1, lift_got, encoded_part, early
+        )
+
         if sizes[0] > 1:
             b_even, b_odd = [
                 lax.psum_scatter(x, "high", scatter_dimension=1, tiled=True) for x in (b_even, b_odd)
             ]
         b_got = flip(b_odd, 1)
-        early = sum_vector(early, sizes)
-        dq, dks, dvs, shares = None, [None] * size, [None] * size, [None] * size
-        share = None
-        for group in [(r,) for r in range(size - 1, 1, -1)] + [(1, 0)]:
-            dq, dk, dv = self_backward(
-                place_1, q1, ks, vs, mixed_one, do1, lse_one, bias, group, dq
-            )
-            for n, r in enumerate(group):
-                dks[r], dvs[r] = dk[n], dv[n]
-                shares[r] = dot(dk[n], wk, 1, 1) + dot(dv[n], wv, 1, 1)
-            r = group[0]
-            if share is None:
-                share, b_even, b_got, lift_got, do1 = together(shares[r], b_even, b_got, lift_got, do1)
-                b_sums = [add_pair(b_even[p], b_got[p]) for p in range(4)]
-                b_back = [flip(b_sums[p], 2 * p) for p in (1, 2, 3)]
-                share = lax.ppermute(share.astype(bf16), "tensor", down_chain)
-            elif r > 1:
-                share, shares[r], do1 = together(share, shares[r], do1)
-                share = lax.ppermute(add_pair(shares[r], share), "tensor", down_chain)
-            else:
-                share, shares, dq, dks, dvs, b_back, early = together(
-                    share, shares, dq, dks, dvs, b_back, early
-                )
-                share = lax.ppermute(add_pair(shares[r], share), "tensor", down_chain)
-        shares[0] = shares[0] + dot(dq, wq, 1, 1)
-        b_parts = sum_columns(place_1, [b_sums[0], *b_back], 5, size)
-        b_turned = [turn(b_parts[r], size - r, size) for r in range(1, size)]
+        early = sum_tensor(early, sizes)
         lift_sums = add_pair(lift_shares[0], lift_got)
         if sizes[0] > 1:
             lift_sums = lax.psum_scatter(lift_sums, "high", scatter_dimension=2, tiled=True)
         lift_sums = lax.all_to_all(lift_sums, "low", split_axis=2, concat_axis=1, tiled=True)
+        encoded_sum = lax.psum_scatter(encoded_part, "tensor", scatter_dimension=0, tiled=True)
+        dq, dks, dvs, own_sums, share = None, [None] * size, [None] * size, [], None
+        for group in [(r,) for r in range(size - 1, 1, -1)] + [(1, 0)]:
+            r = group[0]
+            dq, dk, dv = self_backward(
+                place_1, q1, ks, vs, mixed_one, do1, lse_one, bias, group, dq
+            )
+            for n, s in enumerate(group):
+                dks[s], dvs[s] = dk[n], dv[n]
+            if r > 1:
+                share, sums = share_grad([dk[0], dv[0]], [wk, wv], blocks[r], share, False)
+                own_sums.append(sums)
+            if r == size - 1:
+                share, do1, b_even, b_got, early, out_sum, lift_sums = together(
+                    share, do1, b_even, b_got, early, out_sum, lift_sums
+                )
+                share = lax.ppermute(share, "tensor", down_chain)
+                b_sums = [add_pair(b_even[p], b_got[p]) for p in range(4)]
+                b_back = [flip(b_sums[p], 2 * p) for p in (1, 2, 3)]
+            elif r > 1:
+                share, do1, encoded_sum = together(share, do1, encoded_sum)
+                share = lax.ppermute(share, "tensor", down_chain)
+        share, sums = share_grad([dk[0], dv[0]], [wk, wv], blocks[1], share, False)
+        own_sums.append(sums)
+        share, dq, dks, dvs, b_back, early = together(share, dq, dks, dvs, b_back, early)
+        share = lax.ppermute(share, "tensor", down_chain)
         a_even, a_odd = shard_grads(low_1, [([ones[0]], [dq]), (ones, dks), (ones, dvs)])
-        own_sums = [norm_sums(x.astype(f32), s) for x, s in zip(blocks, shares)]
-        late = jnp.concatenate(
-            [
-                sum(f[0] for f in own_sums),
-                sum(f[1] for f in own_sums),
-                column_sums(dq),
-                sum(column_sums(v) for v in dvs),
-            ]
-        )
-        a_even, a_odd, b_turned, share, shares, late, encoded_part = together(
-            a_even, a_odd, b_turned, share, shares, late, encoded_part
-        )
-
         if sizes[0] > 1:
             a_even, a_odd = [
                 lax.psum_scatter(x, "high", scatter_dimension=1, tiled=True) for x in (a_even, a_odd)
             ]
+        a_even, a_odd, share, dq, dks, dvs, b_sums, b_back = together(
+            a_even, a_odd, share, dq, dks, dvs, b_sums, b_back
+        )
+
         a_got = flip(a_odd, 1)
+        own_share, sums = share_grad([dks[0], dvs[0], dq], [wk, wv, wq], tokens, None, True)
+        own_sums.append(sums)
+        a_even, a_got, own_share, own_sums, share, b_sums, b_back = together(
+            a_even, a_got, own_share, own_sums, share, b_sums, b_back
+        )
         a_sums = [add_pair(a_even[p], a_got[p]) for p in range(4)]
+        a_sums, own_sums, own_share, share, b_sums, b_back, dq, dvs = together(
+            a_sums, own_sums, own_share, share, b_sums, b_back, dq, dvs
+        )
         a_back = [flip(a_sums[p], 2 * p) for p in (1, 2, 3)]
-        encoded_grad = lax.psum_scatter(
-            encoded_part, "tensor", scatter_dimension=0, tiled=True
-        ).astype(f32)
-        share = shares[0] + share.astype(f32)
-        tokens_grad = grad_hidden_one + norm_back(tokens.astype(f32), first_gain, share)
+        b_parts = sum_columns(place_1, [b_sums[0], *b_back], 5, size)
+        b_turned = [turn(b_parts[r], size - r, size) for r in range(1, size)]
+        (tokens_grad,) = norm_backward(tokens, first_gain, [own_share, share], grad_hidden_one, False)
+        late = jnp.concatenate(
+            [sum(own_sums).reshape(-1), column_sums(dq), sum(column_sums(v) for v in dvs)]
+        )
+        late = sum_tensor(late, sizes)
+        a_back, b_turned, late, tokens_grad, out_sum, lift_sums = together(
+            a_back, b_turned, late, tokens_grad, out_sum, lift_sums
+        )
         a_parts = sum_columns(place_1, [a_sums[0], *a_back], 3, size)
         a_turned = [turn(a_parts[r], size - r, size) for r in range(1, size)]
+        vectors = sum_low(jnp.concatenate([early, late]))
+        early, late = vectors[: early.shape[0]], vectors[early.shape[0] :]
+        encoded_grad = encoded_sum.astype(f32)
         wo_g, xq_g, xk_g, xv_g, xo_g = whole_shards(b_parts, b_turned, 5)
         wq_g, wk_g, wv_g = whole_shards(a_parts, a_turned, 3)
         block_out = hidden_two + out_sum.astype(f32) + down_bias
         up_weight_grad = lift_sums[0].T.astype(f32)
         down_weight_grad = lift_sums[1].astype(f32)
 
-        late = sum_vector(late, sizes)
         small = [early[i * width : (i + 1) * width] for i in range(9)]
-        small = [late[:width], late[width : 2 * width]] + small + [late[2 * width : 3 * width], late[3 * width :]]
+        small = [late[:width], late[width : 2 * width]] + [small[i] for i in (0, 1, 3, 4, 2, 5, 6, 7, 8)]
+        small = small + [late[2 * width : 3 * width], late[3 * width :]]
         split = [lax.dynamic_slice_in_dim(s, place * part, part, 0) for s in (small[11], small[12], small[9], small[10])]
         up_bias_grad = lax.dynamic_slice_in_dim(
             early[9 * width :], place * up_bias.shape[0], up_bias.shape[0], 0

time: 827 us -> 771 us (0.932)
  other arithmetic: 77.8 us -> 30.9 us
  Pallas kernels: 280 us -> 322 us
  starting transfers between devices: 138 us -> 112 us
  matrix products: 81.9 us -> 56.2 us
  local copies, waits for them, and re-layouts: 43.2 us -> 32.1 us
    ppermute x6, waiting for transfers between devices: 14.1 us -> 88.3 us  [the longest x3 53.9 us: run(): share = lax.ppermute(share, 'tensor', down_chain)]
    ppermute x36, waiting for transfers between devices: 78.2 us -> 34.1 us  [flip(): return lax.ppermute(x, 'low', [(i, i ^ k) for i in range(8)])]
    pallas_call x9 -> x10, Pallas kernels: 54 us -> 85.9 us  [the longest x2 33.3 us: shard_grads(): pl.pallas_call(kernel, grid_spec=pltpu.PrefetchScalarGridSpec(num_scalar_...]
    dot_general x28 -> x19, matrix products: 80.4 us -> 54.7 us  [dot(): lax.dot_general(a, b, (((ca,), (cb,)), ((), ())), preferred_element_type=...]
    all_to_all x4 -> x1, waiting for transfers between devices: 23.2 us -> 0.01 us  [sum_low(): lax.all_to_all(spread, 'low', split_axis=0, concat_axis=0, tiled=True)]
    convert_element_type x9 -> x8, other arithmetic: 27.4 us -> 14.2 us  [add_pair(): return (a.astype(f32) + b.astype(f32)).astype(bf16)]
    all_to_all x4 -> x1, starting transfers between devices: 15.4 us -> 3.65 us  [sum_low(): lax.all_to_all(spread, 'low', split_axis=0, concat_axis=0, tiled=True)]
    reduce_sum x14 -> x1, other arithmetic: 11.8 us -> 0.5 us  [sum_low(): jnp.sum(lax.all_to_all(spread, 'low', split_axis=0, concat_axis=0, tiled=...]
  transfers between devices with their start and end apart: 76 -> 76, of which waited for: 29 -> 26; matrix products, arithmetic and copies ran while one was open for 20% -> 12% of each run, Pallas kernels for 32% -> 41%
where the time goes in v3:
time: 771 us; the launch traced here: 760 us
  Pallas kernels  322 us (42%)
  waiting for transfers between devices  191 us (25%)
  starting transfers between devices  112 us (15%)
  matrix products  56.2 us (7%)
  local copies, waits for them, and re-layouts  32.1 us (4%)
  other arithmetic  30.9 us (4%)
  between operations  16.2 us (2%)
    pallas_call x4, Pallas kernels, feed_forward(): pl.pallas_call(kernel, grid_spec=pltpu.PrefetchScalarGridSpec(num_scalar_...  71.4 us
    ppermute x27, waiting for transfers between devices, turn(): return lax.ppermute(x, 'tensor', [(i, (i + r) % size) for i in range(size)])  68.2 us
    dot_general x19, matrix products, dot(): lax.dot_general(a, b, (((ca,), (cb,)), ((), ())), preferred_element_type=...  54.7 us
    ppermute x3, waiting for transfers between devices, run(): share = lax.ppermute(share, 'tensor', down_chain)  53.9 us
    ppermute x27, starting transfers between devices, turn(): return lax.ppermute(x, 'tensor', [(i, (i + r) % size) for i in range(size)])  45.6 us
    ppermute x2, waiting for transfers between devices, run(): blocks.append(lax.ppermute(blocks[-1], 'tensor', up_chain))  34.4 us
    ppermute x36, waiting for transfers between devices, flip(): return lax.ppermute(x, 'low', [(i, i ^ k) for i in range(8)])  34.1 us
    pallas_call x2, Pallas kernels, lift_grad(): pl.pallas_call(kernel, grid_spec=pltpu.PrefetchScalarGridSpec(num_scalar_...  33.3 us
  transfers between devices with their start and end apart: 76, of which 26 were waited for; matrix products, arithmetic and copies ran while one was open for 12% of the time, Pallas kernels for 41%

profile of v3, /device:TPU:0, one launch (start us, length us, event | category | flops | bytes accessed | tf_op | source)
XLA Modules:
  0.0 759.8 jit_solution(11944580033545586741)
XLA Ops:
  43.6 22.3 %collective-permute-done.6.refs_1_ = bf16[128,1280]{1,0:T(8,128)(2,1)} collective-permute-done((bf16[128,1280]{1,0:T(8,128)(2,1)S(1)}, bf16[128,1280]{1,0:T(8,128)(2,1)}, u32[]{:S(2)}, u32[]{:S(2)}) %collective-permute-start.6) | collective-permute-done | bytes 327712 | tf_op jit(solution)/shard_map/ppermute | solution.py:760
  66.0 9.3 %collective-permute-done.4.refs_4_ = bf16[4,128,768]{2,1,0:T(8,128)(2,1)} collective-permute-done((bf16[4,128,768]{2,1,0:T(8,128)(2,1)}, bf16[4,128,768]{2,1,0:T(8,128)(2,1)}, u32[]{:S(2)}, u32[]{:S(2)}) %collective-permute-start.4) | collective-permute-done | bytes 786464 | tf_op jit(solution)/shard_map/ppermute | solution.py:752
  111.3 10.6 %self_forward.3 = (f32[8,1,1024]{2,1,0:T(1,128)}, f32[8,1,1024]{2,1,0:T(1,128)}, f32[8,128,1024]{2,1,0:T(8,128)}) custom-call(s32[1]{0:T(128)} %bitcast.place_ref, bf16[512,1024]{1,0:T(8,128)(2,1)} %add_convert_fusion.20.q_ref, bf16[512,1024]{1,0:T(8,128)(2,1)} %convolution_convert_fusion.6.refs_0_.refs_1_, ...), custom_call_target="tpu_custom_call" | custom-call | flops 8589934592 | bytes 6291456 | tf_op jit(solution)/shard_map/self_forward/pallas_call | solution.py:156
  121.9 27.8 %collective-permute-done.17.refs_4_ = bf16[512,1024]{1,0:T(8,128)(2,1)S(1)} collective-permute-done((bf16[512,1024]{1,0:T(8,128)(2,1)S(1)}, bf16[512,1024]{1,0:T(8,128)(2,1)S(1)}, u32[]{:S(2)}, u32[]{:S(2)}) %collective-permute-start.17) | collective-permute-done | bytes 1048608 | tf_op jit(solution)/shard_map/ppermute | solution.py:932
  149.7 18.9 %collective-permute-start.20 = (bf16[512,1024]{1,0:T(8,128)(2,1)S(1)}, bf16[512,1024]{1,0:T(8,128)(2,1)S(1)}, u32[]{:S(2)}, u32[]{:S(2)}) collective-permute-start(bf16[512,1024]{1,0:T(8,128)(2,1)S(1)} %collective-permute-done.17.refs_4_), channel_id=1, source_target_pairs={{0,1},{1,2},{2,3},{4,5},{5,6},{6,7},{8,9},{9,10},{10,11},{12,13},{... | collective-permute-start | bytes 3145736 | tf_op jit(solution)/shard_map/ppermute | solution.py:957
  174.4 7.9 %self_forward.4 = (f32[8,1,1024]{2,1,0:T(1,128)}, f32[8,1,1024]{2,1,0:T(1,128)}, f32[8,128,1024]{2,1,0:T(8,128)}) custom-call(s32[1]{0:T(128)} %bitcast.place_ref, bf16[512,1024]{1,0:T(8,128)(2,1)} %add_convert_fusion.20.q_ref, bf16[512,1024]{1,0:T(8,128)(2,1)} %convolution_convert_fusion.4.refs_0_, bf16[512,1024]{1,0:T(8,128)(2,1)} %add_convert_fusion.17.refs_1_, ...), custom_call_target="tpu_custom_call" | custom-call | flops 4294967296 | bytes 4194304 | tf_op jit(solution)/shard_map/self_forward/pallas_call | solution.py:156
  210.7 10.0 %collective-permute-done.26.refs_1_ = bf16[8,2,128,256]{3,2,1,0:T(8,128)(2,1)} collective-permute-done((bf16[8,2,128,256]{3,2,1,0:T(8,128)(2,1)}, bf16[8,2,128,256]{3,2,1,0:T(8,128)(2,1)}, u32[]{:S(2)}, u32[]{:S(2)}) %collective-permute-start.26) | collective-permute-done | bytes 1048608 | tf_op jit(solution)/shard_map/ppermute | solution.py:760
  223.5 9.5 %unpack_weights.3 = (bf16[1024,1024]{1,0:T(8,128)(2,1)}, bf16[1024,1024]{1,0:T(8,128)(2,1)}, bf16[1024,1024]{1,0:T(8,128)(2,1)}, bf16[1024,1024]{1,0:T(8,128)(2,1)}, bf16[1024,1024]{1,0:T(8,128)(2,1)}) custom-call(s32[2]{0:T(128)} %pad_add_fusion.scalars_ref, bf16[4,128,1280]{2,1,0:T(8,128)(2,1)} %stack_shards.3.refs_0_, bf16[4,128,1280]{2,1,0:T(8,128)(2,1)} %copy-done.22, ...), custom_call_target="tpu_custom_call" | custom-call | bytes 20971520 | tf_op jit(solution)/shard_map/unpack_weights/pallas_call | solution.py:49
  253.6 19.0 %cross_forward.1 = (bf16[512,1024]{1,0:T(8,128)(2,1)}, f32[8,1,1024]{2,1,0:T(1,128)}) custom-call(s32[1]{0:T(128)S(6)} %copy.132.length_ref, bf16[512,1024]{1,0:T(8,128)(2,1)} %add_convert_fusion.14.q_ref, bf16[1024,1024]{1,0:T(8,128)(2,1)} %convolution_convert_fusion.k_ref, bf16[1024,1024]{1,0:T(8,128)(2,1)} %add_convert_fusion.1.v_ref), custom_call_target="tpu_custom_call" | custom-call | flops 8589934592 | bytes 6291456 | tf_op jit(solution)/shard_map/cross_forward/pallas_call | solution.py:191
  282.1 17.8 %feed_forward.4 = (bf16[4096,1024]{1,0:T(8,128)(2,1)}, bf16[512,1024]{1,0:T(8,128)(2,1)}, bf16[512,1024]{1,0:T(8,128)(2,1)}, bf16[1024,1024]{1,0:T(8,128)(2,1)},...) custom-call(s32[1]{0:T(128)} %bitcast.2.low_ref, bf16[512,1024]{1,0:T(8,128)(2,1)} %copy-done.39, ...), custom_call_target="tpu_custom_call" | custom-call | flops 8589934592 | bytes 16777216 | tf_op jit(solution)/shard_map/feed_forward/pallas_call | solution.py:419
  307.0 17.9 %feed_forward.5 = (bf16[4096,1024]{1,0:T(8,128)(2,1)}, bf16[512,1024]{1,0:T(8,128)(2,1)}, bf16[512,1024]{1,0:T(8,128)(2,1)}, bf16[1024,1024]{1,0:T(8,128)(2,1)},...) custom-call(s32[1]{0:T(128)} %bitcast.2.low_ref, ...), custom_call_target="tpu_custom_call", output_to_operand_aliasing={{0}: (9, {})} | custom-call | flops 8589934592 | bytes 16777216 | tf_op jit(solution)/shard_map/feed_forward/pallas_call | solution.py:419
  326.2 17.8 %feed_forward.6 = (bf16[4096,1024]{1,0:T(8,128)(2,1)}, bf16[512,1024]{1,0:T(8,128)(2,1)}, bf16[512,1024]{1,0:T(8,128)(2,1)}, bf16[1024,1024]{1,0:T(8,128)(2,1)},...) custom-call(s32[1]{0:T(128)} %bitcast.2.low_ref, bf16[512,1024]{1,0:T(8,128)(2,1)} %copy-done.89, ...), custom_call_target="tpu_custom_call", output_to_operand_aliasing={{0}: (9, {})} | custom-call | flops 8589934592 | bytes 16777216 | tf_op jit(solution)/shard_map/feed_forward/pallas_call | solution.py:419
  347.7 18.0 %feed_forward.7 = (bf16[4096,1024]{1,0:T(8,128)(2,1)}, bf16[512,1024]{1,0:T(8,128)(2,1)}, bf16[512,1024]{1,0:T(8,128)(2,1)}, bf16[1024,1024]{1,0:T(8,128)(2,1)},...) custom-call(s32[1]{0:T(128)} %bitcast.2.low_ref, bf16[512,1024]{1,0:T(8,128)(2,1)} %copy-done.91, ...), custom_call_target="tpu_custom_call", output_to_operand_aliasing={{0}: (9, {})} | custom-call | flops 8589934592 | bytes 16777216 | tf_op jit(solution)/shard_map/feed_forward/pallas_call | solution.py:419
  369.4 16.5 %lift_grad.2 = (bf16[2,256,1024]{2,1,0:T(8,128)(2,1)}, bf16[2,256,1024]{2,1,0:T(8,128)(2,1)}, bf16[2,256,1024]{2,1,0:T(8,128)(2,1)}, bf16[2,256,1024]{2,1,0:T(8,128)(2,1)}) custom-call(s32[2]{0:T(128)} %pad_add_fusion.scalars_ref, bf16[1024,1024]{1,0:T(8,128)(2,1)} %get-tuple-element.433.refs_0_.refs_1_, ...), custom_call_target="tpu_custom_call" | custom-call | flops 8589934592 | bytes 18874368 | tf_op jit(solution)/shard_map/lift_grad/pallas_call | solution.py:473
  395.0 16.8 %lift_grad.3 = (bf16[2,256,1024]{2,1,0:T(8,128)(2,1)}, bf16[2,256,1024]{2,1,0:T(8,128)(2,1)}, bf16[2,256,1024]{2,1,0:T(8,128)(2,1)}, bf16[2,256,1024]{2,1,0:T(8,128)(2,1)}) custom-call(s32[2]{0:T(128)} %pad_add_fusion.scalars_ref, ...), custom_call_target="tpu_custom_call", output_to_operand_aliasing={{0}: (10, {}), {1}: (11, {}), {2}: (12, {}), {3}: (13, {})} | custom-call | flops 8589934592 | bytes 18874368 | tf_op jit(solution)/shard_map/lift_grad/pallas_call | solution.py:473
  431.8 24.8 %cross_backward.1 = (bf16[512,1024]{1,0:T(8,128)(2,1)}, bf16[1024,1024]{1,0:T(8,128)(2,1)}, bf16[1024,1024]{1,0:T(8,128)(2,1)}) custom-call(s32[1]{0:T(128)S(6)} %copy.132.length_ref, bf16[512,1024]{1,0:T(8,128)(2,1)} %add_convert_fusion.14.q_ref, bf16[1024,1024]{1,0:T(8,128)(2,1)} %convolution_convert_fusion.k_ref, ...), custom_call_target="tpu_custom_call" | custom-call | flops 21474836480 | bytes 12582912 | tf_op jit(solution)/shard_map/cross_backward/pallas_call | solution.py:333
  485.1 16.4 %shard_grads.2 = (bf16[4,128,5120]{2,1,0:T(8,128)(2,1)}, bf16[4,128,5120]{2,1,0:T(8,128)(2,1)}) custom-call(s32[1]{0:T(128)} %bitcast.2.low_ref, bf16[512,1024]{1,0:T(8,128)(2,1)} %get-tuple-element.472.refs_0_, bf16[512,1024]{1,0:T(8,128)(2,1)} %copy-done.37, bf16[1024,1024]{1,0:T(8,128)(2,1)} %all-gather.3.cloned.1.call-done.refs_2_.refs_3_, ...), custom_call_target="tpu_custom_call" | custom-call | flops 7516192768 | bytes 14680064 | tf_op jit(solution)/shard_map/shard_grads/pallas_call | solution.py:544
  551.9 32.9 %collective-permute-done.50.refs_5_ = bf16[512,1024]{1,0:T(8,128)(2,1)S(1)} collective-permute-done((bf16[512,1024]{1,0:T(8,128)(2,1)S(1)}, bf16[512,1024]{1,0:T(8,128)(2,1)S(1)}, u32[]{:S(2)}, u32[]{:S(2)}) %collective-permute-start.50) | collective-permute-done | bytes 1048608 | tf_op jit(solution)/shard_map/ppermute | solution.py:1088
  594.4 17.0 %self_backward.5 = (bf16[512,1024]{1,0:T(8,128)(2,1)}, bf16[512,1024]{1,0:T(8,128)(2,1)}, bf16[512,1024]{1,0:T(8,128)(2,1)}, bf16[512,1024]{1,0:T(8,128)(2,1)}, bf16[512,1024]{1,0:T(8,128)(2,1)}) custom-call(s32[1]{0:T(128)} %bitcast.place_ref, bf16[512,1024]{1,0:T(8,128)(2,1)} %add_convert_fusion.20.q_ref, ...), custom_call_target="tpu_custom_call" | custom-call | flops 21474836480 | bytes 16777216 | tf_op jit(solution)/shard_map/self_backward/pallas_call | solution.py:294
  611.3 9.1 %collective-permute-done.51.refs_5_ = bf16[512,1024]{1,0:T(8,128)(2,1)S(1)} collective-permute-done((bf16[512,1024]{1,0:T(8,128)(2,1)}, bf16[512,1024]{1,0:T(8,128)(2,1)S(1)}, u32[]{:S(2)}, u32[]{:S(2)}) %collective-permute-start.51) | collective-permute-done | bytes 1048608 | tf_op jit(solution)/shard_map/ppermute | solution.py:1093
  630.0 16.8 %shard_grads.3 = (bf16[4,128,3072]{2,1,0:T(8,128)(2,1)}, bf16[4,128,3072]{2,1,0:T(8,128)(2,1)}) custom-call(s32[1]{0:T(128)} %bitcast.2.low_ref, bf16[512,1024]{1,0:T(8,128)(2,1)} %copy-done.33, bf16[512,1024]{1,0:T(8,128)(2,1)} %copy-done.33, bf16[512,1024]{1,0:T(8,128)(2,1)} %copy-done.34, bf16[512,1024]{1,0:T(8,128)(2,1)} %copy-done.35, ...), custom_call_target="tpu_custom_call" | custom-call | flops 9663676416 | bytes 18874368 | tf_op jit(solution)/shard_map/shard_grads/pallas_call | solution.py:544
  646.9 11.8 %collective-permute-done.55.refs_1_ = bf16[512,1024]{1,0:T(8,128)(2,1)S(1)} collective-permute-done((bf16[512,1024]{1,0:T(8,128)(2,1)}, bf16[512,1024]{1,0:T(8,128)(2,1)S(1)}, u32[]{:S(2)}, u32[]{:S(2)}) %collective-permute-start.55) | collective-permute-done | bytes 1048608 | tf_op jit(solution)/shard_map/ppermute | solution.py:1097
  658.7 9.6 %share_grad.7 = (f32[512,1024]{1,0:T(8,128)}, f32[2,1024]{1,0:T(2,128)}) custom-call(bf16[512,1024]{1,0:T(8,128)(2,1)} %get-tuple-element.541.refs_10_.refs_0_, bf16[512,1024]{1,0:T(8,128)(2,1)} %get-tuple-element.584.refs_14_.refs_1_, bf16[512,1024]{1,0:T(8,128)(2,1)} %get-tuple-element.583.refs_9_.refs_2_, ...), custom_call_target="tpu_custom_call" | custom-call | flops 3221225472 | bytes 3145728 | tf_op jit(solution)/shard_map/share_grad/pallas_call | solution.py:698
  710.8 11.2 %collective-permute-done.61 = bf16[128,1280]{1,0:T(8,128)(2,1)} collective-permute-done((bf16[128,1280]{1,0:T(8,128)(2,1)}, bf16[128,1280]{1,0:T(8,128)(2,1)}, u32[]{:S(2)}, u32[]{:S(2)}) %collective-permute-start.61) | collective-permute-done | bytes 327712 | tf_op jit(solution)/shard_map/ppermute | solution.py:760
  (494 shorter events, 353.9 us)
Async XLA Ops:
  22.7 43.3 %all-to-all-start = ((bf16[8,2,128,256]{3,2,1,0:T(8,128)(2,1)}), bf16[8,2,128,256]{3,2,1,0:T(8,128)(2,1)}, u32[]{:S(2)}, u32[]{:S(2)}) async-start(bf16[8,2,128,256]{3,2,1,0:T(8,128)(2,1)} %get-tuple-element.328), calls=%async_computation | async-start | bytes 2097152 | tf_op jit(solution)/shard_map/all_to_all | solution.py:909
  27.1 209.6 %all-gather.3.cloned.1.call-start = ((), (), s32[]{:S(2)}) async-start(), calls=%async_computation.5 | async-start | bytes 2621440 | tf_op jit(solution)/shard_map/all_gather | solution.py:933
  31.8 44.5 %collective-permute-start.7 = (bf16[512,1024]{1,0:T(8,128)(2,1)S(1)}, bf16[512,1024]{1,0:T(8,128)(2,1)S(1)}, u32[]{:S(2)}, u32[]{:S(2)}) collective-permute-start(bf16[512,1024]{1,0:T(8,128)(2,1)S(1)} %copy-done.4), channel_id=1, source_target_pairs={{0,1},{1,2},{2,3},{4,5},{5,6},{6,7},{8,9},{9,10},{10,11},{12,13},{... | collective-permute-start | bytes 3145736 | tf_op jit(solution)/shard_map/ppermute | solution.py:915
  40.1 35.1 %collective-permute-start.4 = (bf16[4,128,768]{2,1,0:T(8,128)(2,1)}, bf16[4,128,768]{2,1,0:T(8,128)(2,1)}, u32[]{:S(2)}, u32[]{:S(2)}) collective-permute-start(bf16[4,128,768]{2,1,0:T(8,128)(2,1)} %stack_shards.2.refs_0_), channel_id=1, source_target_pairs={{0,16},{4,20},{8,24},{12,28},{16,0},{20,4},{24,8},{28,12},{1,17},{... | collective-permute-start | bytes 2359304 | tf_op jit(solution)/shard_map/ppermute | solution.py:752
  41.7 34.6 %collective-permute-start.5 = (bf16[4,128,768]{2,1,0:T(8,128)(2,1)}, bf16[4,128,768]{2,1,0:T(8,128)(2,1)}, u32[]{:S(2)}, u32[]{:S(2)}) collective-permute-start(bf16[4,128,768]{2,1,0:T(8,128)(2,1)} %stack_shards.2.refs_0_), channel_id=1, source_target_pairs={{0,24},{4,28},{8,16},{12,20},{16,8},{20,12},{24,0},{28,4},{1,25},{... | collective-permute-start | bytes 2359304 | tf_op jit(solution)/shard_map/ppermute | solution.py:752
  106.3 43.4 %collective-permute-start.18 = (bf16[4,128,1280]{2,1,0:T(8,128)(2,1)}, bf16[4,128,1280]{2,1,0:T(8,128)(2,1)}, u32[]{:S(2)}, u32[]{:S(2)}) collective-permute-start(bf16[4,128,1280]{2,1,0:T(8,128)(2,1)} %stack_shards.3.refs_0_), channel_id=1, source_target_pairs={{0,8},{4,12},{8,0},{12,4},{16,24},{20,28},{24,16},{28,20},{1,9},{5... | collective-permute-start | bytes 3932168 | tf_op jit(solution)/shard_map/ppermute | solution.py:752
  107.5 42.2 %collective-permute-start.19 = (bf16[4,128,1280]{2,1,0:T(8,128)(2,1)}, bf16[4,128,1280]{2,1,0:T(8,128)(2,1)}, u32[]{:S(2)}, u32[]{:S(2)}) collective-permute-start(bf16[4,128,1280]{2,1,0:T(8,128)(2,1)} %stack_shards.3.refs_0_), channel_id=1, source_target_pairs={{0,16},{4,20},{8,24},{12,28},{16,0},{20,4},{24,8},{28,12},{1,17},{... | collective-permute-start | bytes 3932168 | tf_op jit(solution)/shard_map/ppermute | solution.py:752
  108.4 41.3 %collective-permute-start.17 = (bf16[512,1024]{1,0:T(8,128)(2,1)S(1)}, bf16[512,1024]{1,0:T(8,128)(2,1)S(1)}, u32[]{:S(2)}, u32[]{:S(2)}) collective-permute-start(bf16[512,1024]{1,0:T(8,128)(2,1)S(1)} %collective-permute-done.7.refs_4_), channel_id=1, source_target_pairs={{0,1},{1,2},{2,3},{4,5},{5,6},{6,7},{8,9},{9,10},{10,11},{12,13},{... | collective-permute-start | bytes 3145736 | tf_op jit(solution)/shard_map/ppermute | solution.py:932
  111.1 170.0 %all-gather.5.cloned.1.call-start = ((), (), s32[]{:S(2)}) async-start(), calls=%async_computation.6 | async-start | bytes 9437184 | tf_op jit(solution)/shard_map/all_gather | solution.py:964
  149.7 39.2 %collective-permute-start.20 = (bf16[512,1024]{1,0:T(8,128)(2,1)S(1)}, bf16[512,1024]{1,0:T(8,128)(2,1)S(1)}, u32[]{:S(2)}, u32[]{:S(2)}) collective-permute-start(bf16[512,1024]{1,0:T(8,128)(2,1)S(1)} %collective-permute-done.17.refs_4_), channel_id=1, source_target_pairs={{0,1},{1,2},{2,3},{4,5},{5,6},{6,7},{8,9},{9,10},{10,11},{12,13},{... | collective-permute-start | bytes 3145736 | tf_op jit(solution)/shard_map/ppermute | solution.py:957
  191.6 340.8 %reduce-scatter.3.cloned.1.call-start = ((), (), s32[]{:S(2)}) async-start(), calls=%async_computation.7 | async-start | bytes 9437184 | tf_op jit(solution)/shard_map/reduce_scatter | solution.py:1021
  192.3 28.4 %collective-permute-start.22 = (bf16[4,128,1280]{2,1,0:T(8,128)(2,1)}, bf16[4,128,1280]{2,1,0:T(8,128)(2,1)S(1)}, u32[]{:S(2)}, u32[]{:S(2)}) collective-permute-start(bf16[4,128,1280]{2,1,0:T(8,128)(2,1)} %stack_shards.3.refs_0_), channel_id=1, source_target_pairs={{0,4},{4,0},{8,12},{12,8},{16,20},{20,16},{24,28},{28,24},{1,5},{5... | collective-permute-start | bytes 3932168 | tf_op jit(solution)/shard_map/ppermute | solution.py:752
  192.4 28.3 %collective-permute-start.23 = (bf16[4,128,1280]{2,1,0:T(8,128)(2,1)}, bf16[4,128,1280]{2,1,0:T(8,128)(2,1)S(1)}, u32[]{:S(2)}, u32[]{:S(2)}) collective-permute-start(bf16[4,128,1280]{2,1,0:T(8,128)(2,1)} %collective-permute-done.18.refs_2_), channel_id=1, source_target_pairs={{0,4},{4,0},{8,12},{12,8},{16,20},{20,16},{24,28},{28,24},{1,5},{5... | collective-permute-start | bytes 3932168 | tf_op jit(solution)/shard_map/ppermute | solution.py:752
  220.8 30.6 %collective-permute-start.27 = (bf16[8,2,128,256]{3,2,1,0:T(8,128)(2,1)}, bf16[8,2,128,256]{3,2,1,0:T(8,128)(2,1)}, u32[]{:S(2)}, u32[]{:S(2)}) collective-permute-start(bf16[8,2,128,256]{3,2,1,0:T(8,128)(2,1)} %collective-permute-done.26.refs_1_), channel_id=1, source_target_pairs={{0,1},{1,2},{2,3},{3,0},{4,5},{5,6},{6,7},{7,4},{8,9},{9,10},{10,1... | collective-permute-start | bytes 3145736 | tf_op jit(solution)/shard_map/ppermute | solution.py:760
  305.8 38.3 %collective-permute-start.35 = (bf16[512,1024]{1,0:T(8,128)(2,1)}, bf16[512,1024]{1,0:T(8,128)(2,1)S(1)}, u32[]{:S(2)}, u32[]{:S(2)}) collective-permute-start(bf16[512,1024]{1,0:T(8,128)(2,1)} %copy-done.39), channel_id=1, source_target_pairs={{0,24},{4,28},{8,16},{12,20},{16,8},{20,12},{24,0},{28,4},{1,25},{... | collective-permute-start | bytes 3145736 | tf_op jit(solution)/shard_map/ppermute | solution.py:752
  515.8 77.2 %reduce-scatter.5.cloned.1.call-start = ((), (), s32[]{:S(2)}) async-start(), calls=%async_computation.8 | async-start | bytes 2621440 | tf_op jit(solution)/shard_map/reduce_scatter | solution.py:1072
  532.6 52.2 %collective-permute-start.50 = (bf16[512,1024]{1,0:T(8,128)(2,1)S(1)}, bf16[512,1024]{1,0:T(8,128)(2,1)S(1)}, u32[]{:S(2)}, u32[]{:S(2)}) collective-permute-start(bf16[512,1024]{1,0:T(8,128)(2,1)S(1)} %copy-done.93), channel_id=1, source_target_pairs={{1,0},{2,1},{3,2},{5,4},{6,5},{7,6},{9,8},{10,9},{11,10},{13,12},{... | collective-permute-start | bytes 3145736 | tf_op jit(solution)/shard_map/ppermute | solution.py:1088
  540.5 88.1 %collective-permute-start.52 = (bf16[128,5120]{1,0:T(8,128)(2,1)}, bf16[128,5120]{1,0:T(8,128)(2,1)S(1)}, u32[]{:S(2)}, u32[]{:S(2)}) collective-permute-start(bf16[128,5120]{1,0:T(8,128)(2,1)} %get-tuple-element.724), channel_id=1, source_target_pairs={{0,8},{4,12},{8,0},{12,4},{16,24},{20,28},{24,16},{28,20},{1,9},{5... | collective-permute-start | bytes 3932168 | tf_op jit(solution)/shard_map/ppermute | solution.py:752
  542.5 86.2 %collective-permute-start.53 = (bf16[128,5120]{1,0:T(8,128)(2,1)}, bf16[128,5120]{1,0:T(8,128)(2,1)}, u32[]{:S(2)}, u32[]{:S(2)}) collective-permute-start(bf16[128,5120]{1,0:T(8,128)(2,1)} %get-tuple-element.723), channel_id=1, source_target_pairs={{0,16},{4,20},{8,24},{12,28},{16,0},{20,4},{24,8},{28,12},{1,17},{... | collective-permute-start | bytes 3932168 | tf_op jit(solution)/shard_map/ppermute | solution.py:752
  543.9 84.7 %collective-permute-start.54 = (bf16[128,5120]{1,0:T(8,128)(2,1)}, bf16[128,5120]{1,0:T(8,128)(2,1)}, u32[]{:S(2)}, u32[]{:S(2)}) collective-permute-start(bf16[128,5120]{1,0:T(8,128)(2,1)} %get-tuple-element.722), channel_id=1, source_target_pairs={{0,24},{4,28},{8,16},{12,20},{16,8},{20,12},{24,0},{28,4},{1,25},{... | collective-permute-start | bytes 3932168 | tf_op jit(solution)/shard_map/ppermute | solution.py:752
  628.7 30.0 %collective-permute-start.55 = (bf16[512,1024]{1,0:T(8,128)(2,1)}, bf16[512,1024]{1,0:T(8,128)(2,1)S(1)}, u32[]{:S(2)}, u32[]{:S(2)}) collective-permute-start(bf16[512,1024]{1,0:T(8,128)(2,1)} %get-tuple-element.535), channel_id=1, source_target_pairs={{1,0},{2,1},{3,2},{5,4},{6,5},{7,6},{9,8},{10,9},{11,10},{13,12},{... | collective-permute-start | bytes 3145736 | tf_op jit(solution)/shard_map/ppermute | solution.py:1097
  672.3 49.7 %collective-permute-start.57 = (bf16[128,3072]{1,0:T(8,128)(2,1)S(1)}, bf16[128,3072]{1,0:T(8,128)(2,1)}, u32[]{:S(2)}, u32[]{:S(2)}) collective-permute-start(bf16[128,3072]{1,0:T(8,128)(2,1)S(1)} %get-tuple-element.569), channel_id=1, source_target_pairs={{0,8},{4,12},{8,0},{12,4},{16,24},{20,28},{24,16},{28,20},{1,9},{5... | collective-permute-start | bytes 2359304 | tf_op jit(solution)/shard_map/ppermute | solution.py:752
  673.7 48.2 %collective-permute-start.58 = (bf16[128,3072]{1,0:T(8,128)(2,1)S(1)}, bf16[128,3072]{1,0:T(8,128)(2,1)}, u32[]{:S(2)}, u32[]{:S(2)}) collective-permute-start(bf16[128,3072]{1,0:T(8,128)(2,1)S(1)} %get-tuple-element.570), channel_id=1, source_target_pairs={{0,16},{4,20},{8,24},{12,28},{16,0},{20,4},{24,8},{28,12},{1,17},{... | collective-permute-start | bytes 2359304 | tf_op jit(solution)/shard_map/ppermute | solution.py:752
  675.2 46.8 %collective-permute-start.59 = (bf16[128,3072]{1,0:T(8,128)(2,1)S(1)}, bf16[128,3072]{1,0:T(8,128)(2,1)}, u32[]{:S(2)}, u32[]{:S(2)}) collective-permute-start(bf16[128,3072]{1,0:T(8,128)(2,1)S(1)} %get-tuple-element.571), channel_id=1, source_target_pairs={{0,24},{4,28},{8,16},{12,20},{16,8},{20,12},{24,0},{28,4},{1,25},{... | collective-permute-start | bytes 2359304 | tf_op jit(solution)/shard_map/ppermute | solution.py:752
  (152 other events, 1722.5 us)
Sparse Core Ops, SparseCore 0:
  111.2 59.0 all-gather.2
  191.7 55.2 all-gather.4
  429.9 68.7 reduce-scatter.2
  518.8 60.6 reduce-scatter.4

commit v4 on v3

--- a/solution.py
+++ b/solution.py
@@ -437,7 +437,7 @@
     )(low, r0, r1, cots, *lifts, ub, *([outs] if given else []))
 
 
-def lift_grad(scalars, lefts, rights, order, half, before):
+def lift_grad(low, lefts, rights, order, place, before):
     ordered = not isinstance(rights, list)
     ins = [rights] if ordered else rights
     hidden, wide = lefts[0].shape[0], ins[0].shape[1]
@@ -446,46 +446,41 @@
     tiles, given = 4, 0 if before is None else 4
     tile = hidden // tiles
 
-    def kernel(scalars_ref, *refs):
-        l_refs, r_refs = refs[: 2 * count], refs[2 * count : 2 * count + len(ins)]
-        out_refs = refs[2 * count + len(ins) + given :]
+    def kernel(low_ref, *refs):
+        l_refs, r_refs = refs[:count], refs[count : count + len(ins)]
+        out_refs = refs[count + len(ins) + given :]
         total = None
-        for n in range(count):
-            both = jnp.concatenate([l_refs[2 * n][...], l_refs[2 * n + 1][...]], axis=0)
-            for h in range(2):
-                if ordered:
-                    start = (scalars_ref[0] ^ order[2 * n + h]) * piece
-                    right = r_refs[0][pl.ds(pl.multiple_of(start, piece), piece), :]
-                else:
-                    right = r_refs[2 * n + h][...]
-                part = dot(both[:, h * piece : (h + 1) * piece], right)
-                total = part if total is None else total + part
+        for k in range(2 * count):
+            if ordered:
+                right = r_refs[0][pl.ds(pl.multiple_of((low_ref[0] ^ order[k]) * piece, piece), piece), :]
+            else:
+                right = r_refs[k][...]
+            start = (k % 2) * piece
+            part = dot(l_refs[k // 2][:, start : start + piece], right)
+            total = part if total is None else total + part
         total = total.astype(bf16)
         for n in range(tiles):
-            @pl.when(pl.program_id(0) == n // 2)
+            @pl.when(pl.program_id(0) == n)
             def _(n=n):
-                out_refs[n][0] = total[(n % 2) * tile : (n % 2 + 1) * tile]
-
-    def quarter(h):
-        return pl.BlockSpec((tile, 2 * piece), lambda i, s: (2 * i + h, 0))
+                out_refs[n][0] = total
 
     depth = 2 * count * piece
     return pl.pallas_call(
         kernel,
         grid_spec=pltpu.PrefetchScalarGridSpec(
             num_scalar_prefetch=1,
-            grid=(2,),
-            in_specs=[quarter(0), quarter(1)] * count
+            grid=(tiles,),
+            in_specs=[pl.BlockSpec((tile, 2 * piece), lambda i, s: (i, 0))] * count
             + [pl.BlockSpec(x.shape, lambda i, s: (0, 0)) for x in ins]
             + [pl.BlockSpec(memory_space=pl.ANY)] * given,
-            out_specs=[pl.BlockSpec((1, tile, wide), lambda i, s: (half, 0, 0))] * tiles,
+            out_specs=[pl.BlockSpec((1, tile, wide), lambda i, s: (place, 0, 0))] * tiles,
         ),
         out_shape=[jax.ShapeDtypeStruct((2, tile, wide), bf16)] * tiles,
-        input_output_aliases={1 + 2 * count + len(ins) + n: n for n in range(given)},
+        input_output_aliases={1 + count + len(ins) + n: n for n in range(given)},
         compiler_params=params(56),
         cost_estimate=cost(2 * depth * hidden * wide, 2 * depth * (hidden + wide) + 2 * hidden * wide),
         name="lift_grad",
-    )(scalars, *[x for left in lefts for x in (left, left)], *ins, *(before or ()))
+    )(low, *lefts, *ins, *(before or ()))
 
 
 def shard_grads(low, products):
@@ -625,7 +620,7 @@
     return jnp.mean(x, axis=-1, keepdims=True)
 
 
-def norm_backward(rows, gain, pieces, residual, sums, tile=128):
+def norm_backward(rows, gain, pieces, residual, sums, tile=256):
     count, width = rows.shape
 
     def kernel(rows_ref, gain_ref, residual_ref, *refs):
@@ -1001,14 +996,14 @@
         got_6 = flip(got_6, 1)
         order = (0, 1, 2, 4, 3, 5, 6, 7)
         lift_shares = lift_grad(
-            scalars, [grad_0, grad_1, grad_2, grad_3], [three, c0, x2, x4, c2, c4, x6, c6], order, 0, None
+            low_1, [grad_0, grad_1, grad_2, grad_3], [three, c0, x2, x4, c2, c4, x6, c6], order, 0, None
         )
         back_6, got_6, back_2, back_4, lift_shares = together(
             back_6, got_6, back_2, back_4, lift_shares
         )
         back_6 = flip(add_pair(back_6, got_6), 6)
         lift_shares = lift_grad(
-            scalars, [inner_0, inner_1, inner_2, inner_3], cots, order, 1, lift_shares
+            low_1, [inner_0, inner_1, inner_2, inner_3], cots, order, 1, lift_shares
         )
         up_sums = [sums_0, sums_1, sums_2, sums_3]
         lift_shares, back_6 = together(lift_shares, back_6)
@@ -1047,16 +1042,10 @@
         spread = lax.dynamic_update_slice(
             jnp.zeros((size, up_bias.shape[0]), f32), spread, (0, low * hidden)
         )
-        early = jnp.concatenate(
-            [
-                sums_two.reshape(-1),
-                sums_three.reshape(-1),
-                *early,
-                spread.reshape(-1),
-            ]
-        )
-        (b_even, b_odd), do1, lift_got, encoded_part, early = together(
-            b_laid, do1, lift_got, encoded_part, early
+        whole_sums = [sums_two.reshape(-1), sums_three.reshape(-1), early[0]]
+        place_sums = [spread, early[1].reshape(size, part), early[2].reshape(size, part)]
+        (b_even, b_odd), do1, lift_got, encoded_part, whole_sums, place_sums = together(
+            b_laid, do1, lift_got, encoded_part, whole_sums, place_sums
         )
 
         if sizes[0] > 1:
@@ -1064,7 +1053,6 @@
                 lax.psum_scatter(x, "high", scatter_dimension=1, tiled=True) for x in (b_even, b_odd)
             ]
         b_got = flip(b_odd, 1)
-        early = sum_tensor(early, sizes)
         lift_sums = add_pair(lift_shares[0], lift_got)
         if sizes[0] > 1:
             lift_sums = lax.psum_scatter(lift_sums, "high", scatter_dimension=2, tiled=True)
@@ -1082,8 +1070,8 @@
                 share, sums = share_grad([dk[0], dv[0]], [wk, wv], blocks[r], share, False)
                 own_sums.append(sums)
             if r == size - 1:
-                share, do1, b_even, b_got, early, out_sum, lift_sums = together(
-                    share, do1, b_even, b_got, early, out_sum, lift_sums
+                share, do1, b_even, b_got, out_sum, lift_sums = together(
+                    share, do1, b_even, b_got, out_sum, lift_sums
                 )
                 share = lax.ppermute(share, "tensor", down_chain)
                 b_sums = [add_pair(b_even[p], b_got[p]) for p in range(4)]
@@ -1093,7 +1081,7 @@
                 share = lax.ppermute(share, "tensor", down_chain)
         share, sums = share_grad([dk[0], dv[0]], [wk, wv], blocks[1], share, False)
         own_sums.append(sums)
-        share, dq, dks, dvs, b_back, early = together(share, dq, dks, dvs, b_back, early)
+        share, dq, dks, dvs, b_back = together(share, dq, dks, dvs, b_back)
         share = lax.ppermute(share, "tensor", down_chain)
         a_even, a_odd = shard_grads(low_1, [([ones[0]], [dq]), (ones, dks), (ones, dvs)])
         if sizes[0] > 1:
@@ -1105,30 +1093,33 @@
         )
 
         a_got = flip(a_odd, 1)
+        b_parts = sum_columns(place_1, [b_sums[0], *b_back], 5, size)
+        a_even, a_got, b_parts = together(a_even, a_got, b_parts)
+        a_sums = [add_pair(a_even[p], a_got[p]) for p in range(4)]
+        a_sums, b_parts, dq, dks, dvs, share = together(a_sums, b_parts, dq, dks, dvs, share)
+        a_back = [flip(a_sums[p], 2 * p) for p in (1, 2, 3)]
+        b_turned = [turn(b_parts[r], size - r, size) for r in range(1, size)]
         own_share, sums = share_grad([dks[0], dvs[0], dq], [wk, wv, wq], tokens, None, True)
         own_sums.append(sums)
-        a_even, a_got, own_share, own_sums, share, b_sums, b_back = together(
-            a_even, a_got, own_share, own_sums, share, b_sums, b_back
-        )
-        a_sums = [add_pair(a_even[p], a_got[p]) for p in range(4)]
-        a_sums, own_sums, own_share, share, b_sums, b_back, dq, dvs = together(
-            a_sums, own_sums, own_share, share, b_sums, b_back, dq, dvs
-        )
-        a_back = [flip(a_sums[p], 2 * p) for p in (1, 2, 3)]
-        b_parts = sum_columns(place_1, [b_sums[0], *b_back], 5, size)
-        b_turned = [turn(b_parts[r], size - r, size) for r in range(1, size)]
         (tokens_grad,) = norm_backward(tokens, first_gain, [own_share, share], grad_hidden_one, False)
-        late = jnp.concatenate(
-            [sum(own_sums).reshape(-1), column_sums(dq), sum(column_sums(v) for v in dvs)]
-        )
-        late = sum_tensor(late, sizes)
-        a_back, b_turned, late, tokens_grad, out_sum, lift_sums = together(
-            a_back, b_turned, late, tokens_grad, out_sum, lift_sums
+        whole_sums = jnp.concatenate([*whole_sums, sum(own_sums).reshape(-1)])
+        place_sums += [
+            column_sums(dq).reshape(size, part),
+            sum(column_sums(v) for v in dvs).reshape(size, part),
+        ]
+        vectors = jnp.concatenate([whole_sums, jnp.concatenate(place_sums, axis=1).reshape(-1)])
+        a_back, b_turned, vectors, tokens_grad, out_sum, lift_sums = together(
+            a_back, b_turned, vectors, tokens_grad, out_sum, lift_sums
         )
         a_parts = sum_columns(place_1, [a_sums[0], *a_back], 3, size)
         a_turned = [turn(a_parts[r], size - r, size) for r in range(1, size)]
-        vectors = sum_low(jnp.concatenate([early, late]))
-        early, late = vectors[: early.shape[0]], vectors[early.shape[0] :]
+        vectors, a_parts = together(vectors, a_parts)
+        vectors = sum_low(sum_tensor(vectors, sizes))
+        small = [vectors[i * width : (i + 1) * width] for i in range(9)]
+        small = [small[i] for i in (7, 8, 0, 1, 3, 4, 2, 5, 6)]
+        mine = lax.dynamic_index_in_dim(vectors[9 * width :].reshape(size, -1), place, 0, keepdims=False)
+        up_bias_grad, mine = mine[: up_bias.shape[0]], mine[up_bias.shape[0] :]
+        split = [mine[i * part : (i + 1) * part] for i in (2, 3, 0, 1)]
         encoded_grad = encoded_sum.astype(f32)
         wo_g, xq_g, xk_g, xv_g, xo_g = whole_shards(b_parts, b_turned, 5)
         wq_g, wk_g, wv_g = whole_shards(a_parts, a_turned, 3)
@@ -1136,13 +1127,6 @@
         up_weight_grad = lift_sums[0].T.astype(f32)
         down_weight_grad = lift_sums[1].astype(f32)
 
-        small = [early[i * width : (i + 1) * width] for i in range(9)]
-        small = [late[:width], late[width : 2 * width]] + [small[i] for i in (0, 1, 3, 4, 2, 5, 6, 7, 8)]
-        small = small + [late[2 * width : 3 * width], late[3 * width :]]
-        split = [lax.dynamic_slice_in_dim(s, place * part, part, 0) for s in (small[11], small[12], small[9], small[10])]
-        up_bias_grad = lax.dynamic_slice_in_dim(
-            early[9 * width :], place * up_bias.shape[0], up_bias.shape[0], 0
-        )
         return (
             block_out.astype(bf16),
             tokens_grad,

time: 771 us -> 755 us (0.979)
  waiting for transfers between devices: 191 us -> 173 us
    ppermute x27 -> x24, waiting for transfers between devices: 68.2 us -> 48.5 us  [turn(): return lax.ppermute(x, 'tensor', [(i, (i + r) % size) for i in range(size)])]
    ppermute x3, waiting for transfers between devices: 53.9 us -> 43.7 us  [run(): share = lax.ppermute(share, 'tensor', down_chain)]
    ppermute x27 -> x24, starting transfers between devices: 45.6 us -> 52.2 us  [turn(): return lax.ppermute(x, 'tensor', [(i, (i + r) % size) for i in range(size)])]
    unnamed x216 -> x220, local copies, waits for them, and re-layouts: 20.4 us -> 24.4 us
  transfers between devices with their start and end apart: 76 -> 73, of which waited for: 26 -> 25; matrix products, arithmetic and copies ran while one was open for 12% -> 12% of each run, Pallas kernels for 41% -> 40%
where the time goes in v4:
time: 755 us; the launch traced here: 745 us
  Pallas kernels  317 us (42%)
  waiting for transfers between devices  173 us (23%)
  starting transfers between devices  118 us (16%)
  matrix products  56.2 us (7%)
  local copies, waits for them, and re-layouts  34.2 us (5%)
  other arithmetic  30.1 us (4%)
  between operations  16.3 us (2%)
    pallas_call x4, Pallas kernels, feed_forward(): pl.pallas_call(kernel, grid_spec=pltpu.PrefetchScalarGridSpec(num_scalar_...  71.7 us
    dot_general x19, matrix products, dot(): lax.dot_general(a, b, (((ca,), (cb,)), ((), ())), preferred_element_type=...  54.7 us
    ppermute x24, starting transfers between devices, turn(): return lax.ppermute(x, 'tensor', [(i, (i + r) % size) for i in range(size)])  52.2 us
    ppermute x24, waiting for transfers between devices, turn(): return lax.ppermute(x, 'tensor', [(i, (i + r) % size) for i in range(size)])  48.5 us
    ppermute x3, waiting for transfers between devices, run(): share = lax.ppermute(share, 'tensor', down_chain)  43.7 us
    ppermute x36, waiting for transfers between devices, flip(): return lax.ppermute(x, 'low', [(i, i ^ k) for i in range(8)])  39.5 us
    ppermute x2, waiting for transfers between devices, run(): blocks.append(lax.ppermute(blocks[-1], 'tensor', up_chain))  34.3 us
    pallas_call x2, Pallas kernels, shard_grads(): pl.pallas_call(kernel, grid_spec=pltpu.PrefetchScalarGridSpec(num_scalar_...  33.5 us
  transfers between devices with their start and end apart: 73, of which 25 were waited for; matrix products, arithmetic and copies ran while one was open for 12% of the time, Pallas kernels for 40%

profile of v4, /device:TPU:0, one launch (start us, length us, event | category | flops | bytes accessed | tf_op | source)
XLA Modules:
  0.0 745.0 jit_solution(2903726740558136687)
XLA Ops:
  43.6 22.4 %collective-permute-done.6.refs_1_ = bf16[128,1280]{1,0:T(8,128)(2,1)} collective-permute-done((bf16[128,1280]{1,0:T(8,128)(2,1)S(1)}, bf16[128,1280]{1,0:T(8,128)(2,1)}, u32[]{:S(2)}, u32[]{:S(2)}) %collective-permute-start.6) | collective-permute-done | bytes 327712 | tf_op jit(solution)/shard_map/ppermute | solution.py:755
  66.0 9.3 %collective-permute-done.4.refs_4_ = bf16[4,128,768]{2,1,0:T(8,128)(2,1)} collective-permute-done((bf16[4,128,768]{2,1,0:T(8,128)(2,1)}, bf16[4,128,768]{2,1,0:T(8,128)(2,1)}, u32[]{:S(2)}, u32[]{:S(2)}) %collective-permute-start.4) | collective-permute-done | bytes 786464 | tf_op jit(solution)/shard_map/ppermute | solution.py:747
  111.3 10.6 %self_forward.3 = (f32[8,1,1024]{2,1,0:T(1,128)}, f32[8,1,1024]{2,1,0:T(1,128)}, f32[8,128,1024]{2,1,0:T(8,128)}) custom-call(s32[1]{0:T(128)} %bitcast.place_ref, bf16[512,1024]{1,0:T(8,128)(2,1)} %add_convert_fusion.20.q_ref, bf16[512,1024]{1,0:T(8,128)(2,1)} %convolution_convert_fusion.6.refs_0_.refs_1_, ...), custom_call_target="tpu_custom_call" | custom-call | flops 8589934592 | bytes 6291456 | tf_op jit(solution)/shard_map/self_forward/pallas_call | solution.py:156
  121.9 27.7 %collective-permute-done.17.refs_4_ = bf16[512,1024]{1,0:T(8,128)(2,1)S(1)} collective-permute-done((bf16[512,1024]{1,0:T(8,128)(2,1)S(1)}, bf16[512,1024]{1,0:T(8,128)(2,1)S(1)}, u32[]{:S(2)}, u32[]{:S(2)}) %collective-permute-start.17) | collective-permute-done | bytes 1048608 | tf_op jit(solution)/shard_map/ppermute | solution.py:927
  149.7 18.9 %collective-permute-start.20 = (bf16[512,1024]{1,0:T(8,128)(2,1)S(1)}, bf16[512,1024]{1,0:T(8,128)(2,1)S(1)}, u32[]{:S(2)}, u32[]{:S(2)}) collective-permute-start(bf16[512,1024]{1,0:T(8,128)(2,1)S(1)} %collective-permute-done.17.refs_4_), channel_id=1, source_target_pairs={{0,1},{1,2},{2,3},{4,5},{5,6},{6,7},{8,9},{9,10},{10,11},{12,13},{... | collective-permute-start | bytes 3145736 | tf_op jit(solution)/shard_map/ppermute | solution.py:952
  210.8 10.0 %collective-permute-done.26.refs_1_ = bf16[8,2,128,256]{3,2,1,0:T(8,128)(2,1)} collective-permute-done((bf16[8,2,128,256]{3,2,1,0:T(8,128)(2,1)}, bf16[8,2,128,256]{3,2,1,0:T(8,128)(2,1)}, u32[]{:S(2)}, u32[]{:S(2)}) %collective-permute-start.26) | collective-permute-done | bytes 1048608 | tf_op jit(solution)/shard_map/ppermute | solution.py:755
  223.8 9.4 %unpack_weights.3 = (bf16[1024,1024]{1,0:T(8,128)(2,1)}, bf16[1024,1024]{1,0:T(8,128)(2,1)}, bf16[1024,1024]{1,0:T(8,128)(2,1)}, bf16[1024,1024]{1,0:T(8,128)(2,1)}, bf16[1024,1024]{1,0:T(8,128)(2,1)}) custom-call(s32[2]{0:T(128)} %pad_add_fusion.scalars_ref, bf16[4,128,1280]{2,1,0:T(8,128)(2,1)} %stack_shards.3.refs_0_, bf16[4,128,1280]{2,1,0:T(8,128)(2,1)} %copy-done.22, ...), custom_call_target="tpu_custom_call" | custom-call | bytes 20971520 | tf_op jit(solution)/shard_map/unpack_weights/pallas_call | solution.py:49
  253.5 19.0 %cross_forward.1 = (bf16[512,1024]{1,0:T(8,128)(2,1)}, f32[8,1,1024]{2,1,0:T(1,128)}) custom-call(s32[1]{0:T(128)S(6)} %copy.125.length_ref, bf16[512,1024]{1,0:T(8,128)(2,1)} %add_convert_fusion.14.q_ref, bf16[1024,1024]{1,0:T(8,128)(2,1)} %convolution_convert_fusion.k_ref, bf16[1024,1024]{1,0:T(8,128)(2,1)} %add_convert_fusion.1.v_ref), custom_call_target="tpu_custom_call" | custom-call | flops 8589934592 | bytes 6291456 | tf_op jit(solution)/shard_map/cross_forward/pallas_call | solution.py:191
  281.8 17.7 %feed_forward.4 = (bf16[4096,1024]{1,0:T(8,128)(2,1)}, bf16[512,1024]{1,0:T(8,128)(2,1)}, bf16[512,1024]{1,0:T(8,128)(2,1)}, bf16[1024,1024]{1,0:T(8,128)(2,1)},...) custom-call(s32[1]{0:T(128)} %bitcast.2.low_ref, bf16[512,1024]{1,0:T(8,128)(2,1)} %copy-done.41, ...), custom_call_target="tpu_custom_call" | custom-call | flops 8589934592 | bytes 16777216 | tf_op jit(solution)/shard_map/feed_forward/pallas_call | solution.py:419
  306.7 18.1 %feed_forward.5 = (bf16[4096,1024]{1,0:T(8,128)(2,1)}, bf16[512,1024]{1,0:T(8,128)(2,1)}, bf16[512,1024]{1,0:T(8,128)(2,1)}, bf16[1024,1024]{1,0:T(8,128)(2,1)},...) custom-call(s32[1]{0:T(128)} %bitcast.2.low_ref, ...), custom_call_target="tpu_custom_call", output_to_operand_aliasing={{0}: (9, {})} | custom-call | flops 8589934592 | bytes 16777216 | tf_op jit(solution)/shard_map/feed_forward/pallas_call | solution.py:419
  326.2 17.8 %feed_forward.6 = (bf16[4096,1024]{1,0:T(8,128)(2,1)}, bf16[512,1024]{1,0:T(8,128)(2,1)}, bf16[512,1024]{1,0:T(8,128)(2,1)}, bf16[1024,1024]{1,0:T(8,128)(2,1)},...) custom-call(s32[1]{0:T(128)} %bitcast.2.low_ref, bf16[512,1024]{1,0:T(8,128)(2,1)} %copy-done.90, ...), custom_call_target="tpu_custom_call", output_to_operand_aliasing={{0}: (9, {})} | custom-call | flops 8589934592 | bytes 16777216 | tf_op jit(solution)/shard_map/feed_forward/pallas_call | solution.py:419
  347.7 18.0 %feed_forward.7 = (bf16[4096,1024]{1,0:T(8,128)(2,1)}, bf16[512,1024]{1,0:T(8,128)(2,1)}, bf16[512,1024]{1,0:T(8,128)(2,1)}, bf16[1024,1024]{1,0:T(8,128)(2,1)},...) custom-call(s32[1]{0:T(128)} %bitcast.2.low_ref, bf16[512,1024]{1,0:T(8,128)(2,1)} %copy-done.92, ...), custom_call_target="tpu_custom_call", output_to_operand_aliasing={{0}: (9, {})} | custom-call | flops 8589934592 | bytes 16777216 | tf_op jit(solution)/shard_map/feed_forward/pallas_call | solution.py:419
  369.5 15.3 %lift_grad.2 = (bf16[2,256,1024]{2,1,0:T(8,128)(2,1)}, bf16[2,256,1024]{2,1,0:T(8,128)(2,1)}, bf16[2,256,1024]{2,1,0:T(8,128)(2,1)}, bf16[2,256,1024]{2,1,0:T(8,128)(2,1)}) custom-call(s32[1]{0:T(128)} %bitcast.2.low_ref, bf16[1024,1024]{1,0:T(8,128)(2,1)} %get-tuple-element.428.refs_0_, bf16[1024,1024]{1,0:T(8,128)(2,1)} %get-tuple-element.429.refs_1_, ...), custom_call_target="tpu_custom_call" | custom-call | flops 8589934592 | bytes 18874368 | tf_op jit(solution)/shard_map/lift_grad/pallas_call | solution.py:468
  395.1 15.2 %lift_grad.3 = (bf16[2,256,1024]{2,1,0:T(8,128)(2,1)}, bf16[2,256,1024]{2,1,0:T(8,128)(2,1)}, bf16[2,256,1024]{2,1,0:T(8,128)(2,1)}, bf16[2,256,1024]{2,1,0:T(8,128)(2,1)}) custom-call(s32[1]{0:T(128)} %bitcast.2.low_ref, bf16[1024,1024]{1,0:T(8,128)(2,1)} %get-tuple-element.438.refs_0_, ...), custom_call_target="tpu_custom_call", output_to_operand_aliasing={{0}: (6, {}), {1}: (7, {}), {2}: (8, {}), {3}: (9, {})} | custom-call | flops 8589934592 | bytes 18874368 | tf_op jit(solution)/shard_map/lift_grad/pallas_call | solution.py:468
  410.3 8.6 %collective-permute-done.42.refs_4_ = bf16[512,1024]{1,0:T(8,128)(2,1)S(1)} collective-permute-done((bf16[512,1024]{1,0:T(8,128)(2,1)S(1)}, bf16[512,1024]{1,0:T(8,128)(2,1)S(1)}, u32[]{:S(2)}, u32[]{:S(2)}) %collective-permute-start.42) | collective-permute-done | bytes 1048608 | tf_op jit(solution)/shard_map/ppermute | solution.py:747
  431.1 24.6 %cross_backward.1 = (bf16[512,1024]{1,0:T(8,128)(2,1)}, bf16[1024,1024]{1,0:T(8,128)(2,1)}, bf16[1024,1024]{1,0:T(8,128)(2,1)}) custom-call(s32[1]{0:T(128)S(6)} %copy.125.length_ref, bf16[512,1024]{1,0:T(8,128)(2,1)} %add_convert_fusion.14.q_ref, bf16[1024,1024]{1,0:T(8,128)(2,1)} %convolution_convert_fusion.k_ref, ...), custom_call_target="tpu_custom_call" | custom-call | flops 21474836480 | bytes 12582912 | tf_op jit(solution)/shard_map/cross_backward/pallas_call | solution.py:333
  484.2 16.6 %shard_grads.2 = (bf16[4,128,5120]{2,1,0:T(8,128)(2,1)}, bf16[4,128,5120]{2,1,0:T(8,128)(2,1)}) custom-call(s32[1]{0:T(128)} %bitcast.2.low_ref, bf16[512,1024]{1,0:T(8,128)(2,1)} %get-tuple-element.467.refs_0_, bf16[512,1024]{1,0:T(8,128)(2,1)} %copy-done.37, bf16[1024,1024]{1,0:T(8,128)(2,1)} %all-gather.3.cloned.1.call-done.refs_2_.refs_3_, ...), custom_call_target="tpu_custom_call" | custom-call | flops 7516192768 | bytes 14680064 | tf_op jit(solution)/shard_map/shard_grads/pallas_call | solution.py:539
  545.8 23.1 %collective-permute-done.47.refs_5_ = bf16[512,1024]{1,0:T(8,128)(2,1)S(1)} collective-permute-done((bf16[512,1024]{1,0:T(8,128)(2,1)S(1)}, bf16[512,1024]{1,0:T(8,128)(2,1)S(1)}, u32[]{:S(2)}, u32[]{:S(2)}) %collective-permute-start.47) | collective-permute-done | bytes 1048608 | tf_op jit(solution)/shard_map/ppermute | solution.py:1076
  578.4 17.0 %self_backward.5 = (bf16[512,1024]{1,0:T(8,128)(2,1)}, bf16[512,1024]{1,0:T(8,128)(2,1)}, bf16[512,1024]{1,0:T(8,128)(2,1)}, bf16[512,1024]{1,0:T(8,128)(2,1)}, bf16[512,1024]{1,0:T(8,128)(2,1)}) custom-call(s32[1]{0:T(128)} %bitcast.place_ref, bf16[512,1024]{1,0:T(8,128)(2,1)} %add_convert_fusion.20.q_ref, ...), custom_call_target="tpu_custom_call" | custom-call | flops 21474836480 | bytes 16777216 | tf_op jit(solution)/shard_map/self_backward/pallas_call | solution.py:294
  595.4 8.8 %collective-permute-done.48.refs_5_ = bf16[512,1024]{1,0:T(8,128)(2,1)S(1)} collective-permute-done((bf16[512,1024]{1,0:T(8,128)(2,1)}, bf16[512,1024]{1,0:T(8,128)(2,1)S(1)}, u32[]{:S(2)}, u32[]{:S(2)}) %collective-permute-start.48) | collective-permute-done | bytes 1048608 | tf_op jit(solution)/shard_map/ppermute | solution.py:1081
  613.8 16.9 %shard_grads.3 = (bf16[4,128,3072]{2,1,0:T(8,128)(2,1)}, bf16[4,128,3072]{2,1,0:T(8,128)(2,1)}) custom-call(s32[1]{0:T(128)} %bitcast.2.low_ref, bf16[512,1024]{1,0:T(8,128)(2,1)} %copy-done.33, bf16[512,1024]{1,0:T(8,128)(2,1)} %copy-done.33, bf16[512,1024]{1,0:T(8,128)(2,1)} %copy-done.34, bf16[512,1024]{1,0:T(8,128)(2,1)} %copy-done.35, ...), custom_call_target="tpu_custom_call" | custom-call | flops 9663676416 | bytes 18874368 | tf_op jit(solution)/shard_map/shard_grads/pallas_call | solution.py:539
  630.8 11.8 %collective-permute-done.52.refs_1_ = bf16[512,1024]{1,0:T(8,128)(2,1)S(1)} collective-permute-done((bf16[512,1024]{1,0:T(8,128)(2,1)}, bf16[512,1024]{1,0:T(8,128)(2,1)S(1)}, u32[]{:S(2)}, u32[]{:S(2)}) %collective-permute-start.52) | collective-permute-done | bytes 1048608 | tf_op jit(solution)/shard_map/ppermute | solution.py:1085
  663.0 9.2 %share_grad.7 = (f32[512,1024]{1,0:T(8,128)}, f32[2,1024]{1,0:T(2,128)}) custom-call(bf16[512,1024]{1,0:T(8,128)(2,1)} %get-tuple-element.567.refs_10_.refs_0_, bf16[512,1024]{1,0:T(8,128)(2,1)} %get-tuple-element.568.refs_14_.refs_1_, bf16[512,1024]{1,0:T(8,128)(2,1)} %get-tuple-element.569.refs_9_.refs_2_, ...), custom_call_target="tpu_custom_call" | custom-call | flops 3221225472 | bytes 3145728 | tf_op jit(solution)/shard_map/share_grad/pallas_call | solution.py:693
  674.4 11.8 %collective-permute-start.59 = (bf16[128,1280]{1,0:T(8,128)(2,1)}, bf16[128,1280]{1,0:T(8,128)(2,1)S(1)}, u32[]{:S(2)}, u32[]{:S(2)}) collective-permute-start(bf16[128,1280]{1,0:T(8,128)(2,1)} %get-tuple-element.560), channel_id=1, source_target_pairs={{0,1},{1,2},{2,3},{3,0},{4,5},{5,6},{6,7},{7,4},{8,9},{9,10},{10,1... | collective-permute-start | bytes 983048 | tf_op jit(solution)/shard_map/ppermute | solution.py:755
  (492 shorter events, 350.7 us)
Async XLA Ops:
  22.7 43.3 %all-to-all-start = ((bf16[8,2,128,256]{3,2,1,0:T(8,128)(2,1)}), bf16[8,2,128,256]{3,2,1,0:T(8,128)(2,1)}, u32[]{:S(2)}, u32[]{:S(2)}) async-start(bf16[8,2,128,256]{3,2,1,0:T(8,128)(2,1)} %get-tuple-element.323), calls=%async_computation | async-start | bytes 2097152 | tf_op jit(solution)/shard_map/all_to_all | solution.py:904
  27.1 209.9 %all-gather.3.cloned.1.call-start = ((), (), s32[]{:S(2)}) async-start(), calls=%async_computation.5 | async-start | bytes 2621440 | tf_op jit(solution)/shard_map/all_gather | solution.py:928
  31.8 44.5 %collective-permute-start.7 = (bf16[512,1024]{1,0:T(8,128)(2,1)S(1)}, bf16[512,1024]{1,0:T(8,128)(2,1)S(1)}, u32[]{:S(2)}, u32[]{:S(2)}) collective-permute-start(bf16[512,1024]{1,0:T(8,128)(2,1)S(1)} %copy-done.4), channel_id=1, source_target_pairs={{0,1},{1,2},{2,3},{4,5},{5,6},{6,7},{8,9},{9,10},{10,11},{12,13},{... | collective-permute-start | bytes 3145736 | tf_op jit(solution)/shard_map/ppermute | solution.py:910
  40.1 35.1 %collective-permute-start.4 = (bf16[4,128,768]{2,1,0:T(8,128)(2,1)}, bf16[4,128,768]{2,1,0:T(8,128)(2,1)}, u32[]{:S(2)}, u32[]{:S(2)}) collective-permute-start(bf16[4,128,768]{2,1,0:T(8,128)(2,1)} %stack_shards.2.refs_0_), channel_id=1, source_target_pairs={{0,16},{4,20},{8,24},{12,28},{16,0},{20,4},{24,8},{28,12},{1,17},{... | collective-permute-start | bytes 2359304 | tf_op jit(solution)/shard_map/ppermute | solution.py:747
  41.7 34.6 %collective-permute-start.5 = (bf16[4,128,768]{2,1,0:T(8,128)(2,1)}, bf16[4,128,768]{2,1,0:T(8,128)(2,1)}, u32[]{:S(2)}, u32[]{:S(2)}) collective-permute-start(bf16[4,128,768]{2,1,0:T(8,128)(2,1)} %stack_shards.2.refs_0_), channel_id=1, source_target_pairs={{0,24},{4,28},{8,16},{12,20},{16,8},{20,12},{24,0},{28,4},{1,25},{... | collective-permute-start | bytes 2359304 | tf_op jit(solution)/shard_map/ppermute | solution.py:747
  106.3 43.4 %collective-permute-start.18 = (bf16[4,128,1280]{2,1,0:T(8,128)(2,1)}, bf16[4,128,1280]{2,1,0:T(8,128)(2,1)}, u32[]{:S(2)}, u32[]{:S(2)}) collective-permute-start(bf16[4,128,1280]{2,1,0:T(8,128)(2,1)} %stack_shards.3.refs_0_), channel_id=1, source_target_pairs={{0,8},{4,12},{8,0},{12,4},{16,24},{20,28},{24,16},{28,20},{1,9},{5... | collective-permute-start | bytes 3932168 | tf_op jit(solution)/shard_map/ppermute | solution.py:747
  107.5 42.2 %collective-permute-start.19 = (bf16[4,128,1280]{2,1,0:T(8,128)(2,1)}, bf16[4,128,1280]{2,1,0:T(8,128)(2,1)}, u32[]{:S(2)}, u32[]{:S(2)}) collective-permute-start(bf16[4,128,1280]{2,1,0:T(8,128)(2,1)} %stack_shards.3.refs_0_), channel_id=1, source_target_pairs={{0,16},{4,20},{8,24},{12,28},{16,0},{20,4},{24,8},{28,12},{1,17},{... | collective-permute-start | bytes 3932168 | tf_op jit(solution)/shard_map/ppermute | solution.py:747
  108.4 41.3 %collective-permute-start.17 = (bf16[512,1024]{1,0:T(8,128)(2,1)S(1)}, bf16[512,1024]{1,0:T(8,128)(2,1)S(1)}, u32[]{:S(2)}, u32[]{:S(2)}) collective-permute-start(bf16[512,1024]{1,0:T(8,128)(2,1)S(1)} %collective-permute-done.7.refs_4_), channel_id=1, source_target_pairs={{0,1},{1,2},{2,3},{4,5},{5,6},{6,7},{8,9},{9,10},{10,11},{12,13},{... | collective-permute-start | bytes 3145736 | tf_op jit(solution)/shard_map/ppermute | solution.py:927
  111.1 169.8 %all-gather.5.cloned.1.call-start = ((), (), s32[]{:S(2)}) async-start(), calls=%async_computation.6 | async-start | bytes 9437184 | tf_op jit(solution)/shard_map/all_gather | solution.py:959
  149.7 39.2 %collective-permute-start.20 = (bf16[512,1024]{1,0:T(8,128)(2,1)S(1)}, bf16[512,1024]{1,0:T(8,128)(2,1)S(1)}, u32[]{:S(2)}, u32[]{:S(2)}) collective-permute-start(bf16[512,1024]{1,0:T(8,128)(2,1)S(1)} %collective-permute-done.17.refs_4_), channel_id=1, source_target_pairs={{0,1},{1,2},{2,3},{4,5},{5,6},{6,7},{8,9},{9,10},{10,11},{12,13},{... | collective-permute-start | bytes 3145736 | tf_op jit(solution)/shard_map/ppermute | solution.py:952
  191.6 335.1 %reduce-scatter.3.cloned.1.call-start = ((), (), s32[]{:S(2)}) async-start(), calls=%async_computation.7 | async-start | bytes 9437184 | tf_op jit(solution)/shard_map/reduce_scatter | solution.py:1016
  192.3 28.5 %collective-permute-start.22 = (bf16[4,128,1280]{2,1,0:T(8,128)(2,1)}, bf16[4,128,1280]{2,1,0:T(8,128)(2,1)S(1)}, u32[]{:S(2)}, u32[]{:S(2)}) collective-permute-start(bf16[4,128,1280]{2,1,0:T(8,128)(2,1)} %stack_shards.3.refs_0_), channel_id=1, source_target_pairs={{0,4},{4,0},{8,12},{12,8},{16,20},{20,16},{24,28},{28,24},{1,5},{5... | collective-permute-start | bytes 3932168 | tf_op jit(solution)/shard_map/ppermute | solution.py:747
  220.9 30.7 %collective-permute-start.27 = (bf16[8,2,128,256]{3,2,1,0:T(8,128)(2,1)}, bf16[8,2,128,256]{3,2,1,0:T(8,128)(2,1)}, u32[]{:S(2)}, u32[]{:S(2)}) collective-permute-start(bf16[8,2,128,256]{3,2,1,0:T(8,128)(2,1)} %collective-permute-done.26.refs_1_), channel_id=1, source_target_pairs={{0,1},{1,2},{2,3},{3,0},{4,5},{5,6},{6,7},{7,4},{8,9},{9,10},{10,1... | collective-permute-start | bytes 3145736 | tf_op jit(solution)/shard_map/ppermute | solution.py:755
  305.5 38.5 %collective-permute-start.35 = (bf16[512,1024]{1,0:T(8,128)(2,1)}, bf16[512,1024]{1,0:T(8,128)(2,1)S(1)}, u32[]{:S(2)}, u32[]{:S(2)}) collective-permute-start(bf16[512,1024]{1,0:T(8,128)(2,1)} %copy-done.41), channel_id=1, source_target_pairs={{0,24},{4,28},{8,16},{12,20},{16,8},{20,12},{24,0},{28,4},{1,25},{... | collective-permute-start | bytes 3145736 | tf_op jit(solution)/shard_map/ppermute | solution.py:747
  429.6 147.6 %reduce-scatter.5.cloned.1.call-start = ((), (), s32[]{:S(2)}) async-start(), calls=%async_computation.8 | async-start | bytes 2621440 | tf_op jit(solution)/shard_map/reduce_scatter | solution.py:1060
  526.7 42.2 %collective-permute-start.47 = (bf16[512,1024]{1,0:T(8,128)(2,1)S(1)}, bf16[512,1024]{1,0:T(8,128)(2,1)S(1)}, u32[]{:S(2)}, u32[]{:S(2)}) collective-permute-start(bf16[512,1024]{1,0:T(8,128)(2,1)S(1)} %copy-done.95), channel_id=1, source_target_pairs={{1,0},{2,1},{3,2},{5,4},{6,5},{7,6},{9,8},{10,9},{11,10},{13,12},{... | collective-permute-start | bytes 3145736 | tf_op jit(solution)/shard_map/ppermute | solution.py:1076
  534.6 77.9 %collective-permute-start.49 = (bf16[128,5120]{1,0:T(8,128)(2,1)}, bf16[128,5120]{1,0:T(8,128)(2,1)S(1)}, u32[]{:S(2)}, u32[]{:S(2)}) collective-permute-start(bf16[128,5120]{1,0:T(8,128)(2,1)} %get-tuple-element.714), channel_id=1, source_target_pairs={{0,8},{4,12},{8,0},{12,4},{16,24},{20,28},{24,16},{28,20},{1,9},{5... | collective-permute-start | bytes 3932168 | tf_op jit(solution)/shard_map/ppermute | solution.py:747
  535.7 76.8 %collective-permute-start.50 = (bf16[128,5120]{1,0:T(8,128)(2,1)}, bf16[128,5120]{1,0:T(8,128)(2,1)}, u32[]{:S(2)}, u32[]{:S(2)}) collective-permute-start(bf16[128,5120]{1,0:T(8,128)(2,1)} %get-tuple-element.713), channel_id=1, source_target_pairs={{0,16},{4,20},{8,24},{12,28},{16,0},{20,4},{24,8},{28,12},{1,17},{... | collective-permute-start | bytes 3932168 | tf_op jit(solution)/shard_map/ppermute | solution.py:747
  537.2 75.4 %collective-permute-start.51 = (bf16[128,5120]{1,0:T(8,128)(2,1)}, bf16[128,5120]{1,0:T(8,128)(2,1)}, u32[]{:S(2)}, u32[]{:S(2)}) collective-permute-start(bf16[128,5120]{1,0:T(8,128)(2,1)} %get-tuple-element.712), channel_id=1, source_target_pairs={{0,24},{4,28},{8,16},{12,20},{16,8},{20,12},{24,0},{28,4},{1,25},{... | collective-permute-start | bytes 3932168 | tf_op jit(solution)/shard_map/ppermute | solution.py:747
  612.5 30.0 %collective-permute-start.52 = (bf16[512,1024]{1,0:T(8,128)(2,1)}, bf16[512,1024]{1,0:T(8,128)(2,1)S(1)}, u32[]{:S(2)}, u32[]{:S(2)}) collective-permute-start(bf16[512,1024]{1,0:T(8,128)(2,1)} %get-tuple-element.528), channel_id=1, source_target_pairs={{1,0},{2,1},{3,2},{5,4},{6,5},{7,6},{9,8},{10,9},{11,10},{13,12},{... | collective-permute-start | bytes 3145736 | tf_op jit(solution)/shard_map/ppermute | solution.py:1085
  655.9 35.7 %collective-permute-start.54 = (bf16[128,3072]{1,0:T(8,128)(2,1)S(1)}, bf16[128,3072]{1,0:T(8,128)(2,1)}, u32[]{:S(2)}, u32[]{:S(2)}) collective-permute-start(bf16[128,3072]{1,0:T(8,128)(2,1)S(1)} %get-tuple-element.555), channel_id=1, source_target_pairs={{0,8},{4,12},{8,0},{12,4},{16,24},{20,28},{24,16},{28,20},{1,9},{5... | collective-permute-start | bytes 2359304 | tf_op jit(solution)/shard_map/ppermute | solution.py:747
  657.5 36.6 %collective-permute-start.55 = (bf16[128,3072]{1,0:T(8,128)(2,1)S(1)}, bf16[128,3072]{1,0:T(8,128)(2,1)}, u32[]{:S(2)}, u32[]{:S(2)}) collective-permute-start(bf16[128,3072]{1,0:T(8,128)(2,1)S(1)} %get-tuple-element.556), channel_id=1, source_target_pairs={{0,16},{4,20},{8,24},{12,28},{16,0},{20,4},{24,8},{28,12},{1,17},{... | collective-permute-start | bytes 2359304 | tf_op jit(solution)/shard_map/ppermute | solution.py:747
  658.9 35.1 %collective-permute-start.56 = (bf16[128,3072]{1,0:T(8,128)(2,1)S(1)}, bf16[128,3072]{1,0:T(8,128)(2,1)}, u32[]{:S(2)}, u32[]{:S(2)}) collective-permute-start(bf16[128,3072]{1,0:T(8,128)(2,1)S(1)} %get-tuple-element.557), channel_id=1, source_target_pairs={{0,24},{4,28},{8,16},{12,20},{16,8},{20,12},{24,0},{28,4},{1,25},{... | collective-permute-start | bytes 2359304 | tf_op jit(solution)/shard_map/ppermute | solution.py:747
  661.5 30.1 %collective-permute-start.58 = (bf16[128,1280]{1,0:T(8,128)(2,1)}, bf16[128,1280]{1,0:T(8,128)(2,1)}, u32[]{:S(2)}, u32[]{:S(2)}) collective-permute-start(bf16[128,1280]{1,0:T(8,128)(2,1)} %get-tuple-element.559), channel_id=1, source_target_pairs={{0,2},{1,3},{2,0},{3,1},{4,6},{5,7},{6,4},{7,5},{8,10},{9,11},{10,... | collective-permute-start | bytes 983048 | tf_op jit(solution)/shard_map/ppermute | solution.py:755
  (150 other events, 1678.7 us)
Sparse Core Ops, SparseCore 0:
  111.2 59.0 all-gather.2
  191.7 55.2 all-gather.4
  429.7 68.5 reduce-scatter.2
  504.3 50.1 reduce-scatter.4

commit v5 on v4

--- a/solution.py
+++ b/solution.py
@@ -1058,63 +1058,65 @@
             lift_sums = lax.psum_scatter(lift_sums, "high", scatter_dimension=2, tiled=True)
         lift_sums = lax.all_to_all(lift_sums, "low", split_axis=2, concat_axis=1, tiled=True)
         encoded_sum = lax.psum_scatter(encoded_part, "tensor", scatter_dimension=0, tiled=True)
-        dq, dks, dvs, own_sums, share = None, [None] * size, [None] * size, [], None
-        for group in [(r,) for r in range(size - 1, 1, -1)] + [(1, 0)]:
-            r = group[0]
-            dq, dk, dv = self_backward(
-                place_1, q1, ks, vs, mixed_one, do1, lse_one, bias, group, dq
-            )
-            for n, s in enumerate(group):
-                dks[s], dvs[s] = dk[n], dv[n]
-            if r > 1:
-                share, sums = share_grad([dk[0], dv[0]], [wk, wv], blocks[r], share, False)
-                own_sums.append(sums)
-            if r == size - 1:
-                share, do1, b_even, b_got, out_sum, lift_sums = together(
-                    share, do1, b_even, b_got, out_sum, lift_sums
-                )
-                share = lax.ppermute(share, "tensor", down_chain)
-                b_sums = [add_pair(b_even[p], b_got[p]) for p in range(4)]
-                b_back = [flip(b_sums[p], 2 * p) for p in (1, 2, 3)]
-            elif r > 1:
-                share, do1, encoded_sum = together(share, do1, encoded_sum)
-                share = lax.ppermute(share, "tensor", down_chain)
-        share, sums = share_grad([dk[0], dv[0]], [wk, wv], blocks[1], share, False)
+        dks, dvs, own_sums = [None] * size, [None] * size, []
+        far = tuple(range(size - 1, 1, -1))
+        dq, dk, dv = self_backward(place_1, q1, ks, vs, mixed_one, do1, lse_one, bias, far, None)
+        for n, r in enumerate(far):
+            dks[r], dvs[r] = dk[n], dv[n]
+        share, sums = share_grad([dks[far[0]], dvs[far[0]]], [wk, wv], blocks[far[0]], None, False)
         own_sums.append(sums)
-        share, dq, dks, dvs, b_back = together(share, dq, dks, dvs, b_back)
+        share, dq, b_even, b_got, out_sum, lift_sums = together(
+            share, dq, b_even, b_got, out_sum, lift_sums
+        )
         share = lax.ppermute(share, "tensor", down_chain)
+        b_sums = [add_pair(b_even[p], b_got[p]) for p in range(4)]
+        b_sums, dq = together(b_sums, dq)
+        b_back = [flip(b_sums[p], 2 * p) for p in (1, 2, 3)]
+        dq, dk, dv = self_backward(place_1, q1, ks, vs, mixed_one, do1, lse_one, bias, (1, 0), dq)
+        dks[1], dvs[1], dks[0], dvs[0] = dk[0], dv[0], dk[1], dv[1]
+        for r in far[1:]:
+            share, sums = share_grad([dks[r], dvs[r]], [wk, wv], blocks[r], share, False)
+            own_sums.append(sums)
+            share, dq, dks, dvs, encoded_sum = together(share, dq, dks, dvs, encoded_sum)
+            share = lax.ppermute(share, "tensor", down_chain)
         a_even, a_odd = shard_grads(low_1, [([ones[0]], [dq]), (ones, dks), (ones, dvs)])
         if sizes[0] > 1:
             a_even, a_odd = [
                 lax.psum_scatter(x, "high", scatter_dimension=1, tiled=True) for x in (a_even, a_odd)
             ]
-        a_even, a_odd, share, dq, dks, dvs, b_sums, b_back = together(
-            a_even, a_odd, share, dq, dks, dvs, b_sums, b_back
+        a_even, a_odd, share, dq, dks, dvs, b_back = together(
+            a_even, a_odd, share, dq, dks, dvs, b_back
         )
 
         a_got = flip(a_odd, 1)
+        share, sums = share_grad([dks[1], dvs[1]], [wk, wv], blocks[1], share, False)
+        own_sums.append(sums)
+        a_even, a_got, share = together(a_even, a_got, share)
+        share = lax.ppermute(share, "tensor", down_chain)
+        a_sums = [add_pair(a_even[p], a_got[p]) for p in range(4)]
+        a_sums, b_sums, b_back, dq, dks, dvs = together(a_sums, b_sums, b_back, dq, dks, dvs)
+        a_back = [flip(a_sums[p], 2 * p) for p in (1, 2, 3)]
         b_parts = sum_columns(place_1, [b_sums[0], *b_back], 5, size)
-        a_even, a_got, b_parts = together(a_even, a_got, b_parts)
-        a_sums = [add_pair(a_even[p], a_got[p]) for p in range(4)]
-        a_sums, b_parts, dq, dks, dvs, share = together(a_sums, b_parts, dq, dks, dvs, share)
-        a_back = [flip(a_sums[p], 2 * p) for p in (1, 2, 3)]
-        b_turned = [turn(b_parts[r], size - r, size) for r in range(1, size)]
+        b_turned = [turn(b_parts[1], size - 1, size)]
         own_share, sums = share_grad([dks[0], dvs[0], dq], [wk, wv, wq], tokens, None, True)
         own_sums.append(sums)
-        (tokens_grad,) = norm_backward(tokens, first_gain, [own_share, share], grad_hidden_one, False)
+        share, b_parts = together(share, b_parts)
+        b_turned += [turn(b_parts[r], size - r, size) for r in range(2, size)]
         whole_sums = jnp.concatenate([*whole_sums, sum(own_sums).reshape(-1)])
         place_sums += [
             column_sums(dq).reshape(size, part),
             sum(column_sums(v) for v in dvs).reshape(size, part),
         ]
         vectors = jnp.concatenate([whole_sums, jnp.concatenate(place_sums, axis=1).reshape(-1)])
-        a_back, b_turned, vectors, tokens_grad, out_sum, lift_sums = together(
-            a_back, b_turned, vectors, tokens_grad, out_sum, lift_sums
-        )
+        a_back, vectors, out_sum, lift_sums, share, own_share = together(
+            a_back, vectors, out_sum, lift_sums, share, own_share
+        )
+        vectors = sum_tensor(vectors, sizes)
         a_parts = sum_columns(place_1, [a_sums[0], *a_back], 3, size)
         a_turned = [turn(a_parts[r], size - r, size) for r in range(1, size)]
-        vectors, a_parts = together(vectors, a_parts)
-        vectors = sum_low(sum_tensor(vectors, sizes))
+        vectors, a_parts, share = together(vectors, a_parts, share)
+        vectors = sum_low(vectors)
+        (tokens_grad,) = norm_backward(tokens, first_gain, [own_share, share], grad_hidden_one, False)
         small = [vectors[i * width : (i + 1) * width] for i in range(9)]
         small = [small[i] for i in (7, 8, 0, 1, 3, 4, 2, 5, 6)]
         mine = lax.dynamic_index_in_dim(vectors[9 * width :].reshape(size, -1), place, 0, keepdims=False)

time: 755 us -> 746 us (0.988)
    ppermute x3, waiting for transfers between devices: 43.7 us -> 32.4 us  [run(): share = lax.ppermute(share, 'tensor', down_chain)]
    ppermute x24, waiting for transfers between devices: 48.5 us -> 58.4 us  [turn(): return lax.ppermute(x, 'tensor', [(i, (i + r) % size) for i in range(size)])]
    pallas_call x3 -> x2, Pallas kernels: 32 us -> 25.7 us  [self_backward(): pl.pallas_call(kernel, grid_spec=pltpu.PrefetchScalarGridSpec(num_scalar_...]
    unnamed x220 -> x226, local copies, waits for them, and re-layouts: 24.4 us -> 23.1 us
  transfers between devices with their start and end apart: 73 -> 73, of which waited for: 25 -> 23; matrix products, arithmetic and copies ran while one was open for 12% -> 13% of each run, Pallas kernels for 40% -> 41%
where the time goes in v5:
time: 746 us; the launch traced here: 736 us
  Pallas kernels  310 us (42%)
  waiting for transfers between devices  166 us (22%)
  starting transfers between devices  124 us (17%)
  matrix products  56.2 us (8%)
  local copies, waits for them, and re-layouts  32.9 us (4%)
  other arithmetic  30.7 us (4%)
  between operations  16.3 us (2%)
    pallas_call x4, Pallas kernels, feed_forward(): pl.pallas_call(kernel, grid_spec=pltpu.PrefetchScalarGridSpec(num_scalar_...  71.6 us
    ppermute x24, waiting for transfers between devices, turn(): return lax.ppermute(x, 'tensor', [(i, (i + r) % size) for i in range(size)])  58.4 us
    ppermute x24, starting transfers between devices, turn(): return lax.ppermute(x, 'tensor', [(i, (i + r) % size) for i in range(size)])  57.9 us
    dot_general x19, matrix products, dot(): lax.dot_general(a, b, (((ca,), (cb,)), ((), ())), preferred_element_type=...  54.7 us
    ppermute x36, waiting for transfers between devices, flip(): return lax.ppermute(x, 'low', [(i, i ^ k) for i in range(8)])  40.1 us
    ppermute x2, waiting for transfers between devices, run(): blocks.append(lax.ppermute(blocks[-1], 'tensor', up_chain))  34.3 us
    pallas_call x2, Pallas kernels, shard_grads(): pl.pallas_call(kernel, grid_spec=pltpu.PrefetchScalarGridSpec(num_scalar_...  33.5 us
    ppermute x3, waiting for transfers between devices, run(): share = lax.ppermute(share, 'tensor', down_chain)  32.4 us
  transfers between devices with their start and end apart: 73, of which 23 were waited for; matrix products, arithmetic and copies ran while one was open for 13% of the time, Pallas kernels for 41%

profile of v5, /device:TPU:0, one launch (start us, length us, event | category | flops | bytes accessed | tf_op | source)
XLA Modules:
  0.0 736.3 jit_solution(6526440696585901016)
XLA Ops:
  43.6 22.3 %collective-permute-done.6.refs_1_ = bf16[128,1280]{1,0:T(8,128)(2,1)} collective-permute-done((bf16[128,1280]{1,0:T(8,128)(2,1)S(1)}, bf16[128,1280]{1,0:T(8,128)(2,1)}, u32[]{:S(2)}, u32[]{:S(2)}) %collective-permute-start.6) | collective-permute-done | bytes 327712 | tf_op jit(solution)/shard_map/ppermute | solution.py:755
  66.0 9.3 %collective-permute-done.4.refs_4_ = bf16[4,128,768]{2,1,0:T(8,128)(2,1)} collective-permute-done((bf16[4,128,768]{2,1,0:T(8,128)(2,1)}, bf16[4,128,768]{2,1,0:T(8,128)(2,1)}, u32[]{:S(2)}, u32[]{:S(2)}) %collective-permute-start.4) | collective-permute-done | bytes 786464 | tf_op jit(solution)/shard_map/ppermute | solution.py:747
  111.4 10.6 %self_forward.3 = (f32[8,1,1024]{2,1,0:T(1,128)}, f32[8,1,1024]{2,1,0:T(1,128)}, f32[8,128,1024]{2,1,0:T(8,128)}) custom-call(s32[1]{0:T(128)} %bitcast.place_ref, bf16[512,1024]{1,0:T(8,128)(2,1)} %add_convert_fusion.20.q_ref, bf16[512,1024]{1,0:T(8,128)(2,1)} %convolution_convert_fusion.6.refs_0_.refs_1_, ...), custom_call_target="tpu_custom_call" | custom-call | flops 8589934592 | bytes 6291456 | tf_op jit(solution)/shard_map/self_forward/pallas_call | solution.py:156
  122.0 27.8 %collective-permute-done.17.refs_4_ = bf16[512,1024]{1,0:T(8,128)(2,1)S(1)} collective-permute-done((bf16[512,1024]{1,0:T(8,128)(2,1)S(1)}, bf16[512,1024]{1,0:T(8,128)(2,1)S(1)}, u32[]{:S(2)}, u32[]{:S(2)}) %collective-permute-start.17) | collective-permute-done | bytes 1048608 | tf_op jit(solution)/shard_map/ppermute | solution.py:927
  149.7 18.9 %collective-permute-start.20 = (bf16[512,1024]{1,0:T(8,128)(2,1)S(1)}, bf16[512,1024]{1,0:T(8,128)(2,1)S(1)}, u32[]{:S(2)}, u32[]{:S(2)}) collective-permute-start(bf16[512,1024]{1,0:T(8,128)(2,1)S(1)} %collective-permute-done.17.refs_4_), channel_id=1, source_target_pairs={{0,1},{1,2},{2,3},{4,5},{5,6},{6,7},{8,9},{9,10},{10,11},{12,13},{... | collective-permute-start | bytes 3145736 | tf_op jit(solution)/shard_map/ppermute | solution.py:952
  210.8 10.0 %collective-permute-done.26.refs_1_ = bf16[8,2,128,256]{3,2,1,0:T(8,128)(2,1)} collective-permute-done((bf16[8,2,128,256]{3,2,1,0:T(8,128)(2,1)}, bf16[8,2,128,256]{3,2,1,0:T(8,128)(2,1)}, u32[]{:S(2)}, u32[]{:S(2)}) %collective-permute-start.26) | collective-permute-done | bytes 1048608 | tf_op jit(solution)/shard_map/ppermute | solution.py:755
  223.9 9.4 %unpack_weights.3 = (bf16[1024,1024]{1,0:T(8,128)(2,1)}, bf16[1024,1024]{1,0:T(8,128)(2,1)}, bf16[1024,1024]{1,0:T(8,128)(2,1)}, bf16[1024,1024]{1,0:T(8,128)(2,1)}, bf16[1024,1024]{1,0:T(8,128)(2,1)}) custom-call(s32[2]{0:T(128)} %pad_add_fusion.scalars_ref, bf16[4,128,1280]{2,1,0:T(8,128)(2,1)} %stack_shards.3.refs_0_, bf16[4,128,1280]{2,1,0:T(8,128)(2,1)} %copy-done.22, ...), custom_call_target="tpu_custom_call" | custom-call | bytes 20971520 | tf_op jit(solution)/shard_map/unpack_weights/pallas_call | solution.py:49
  253.5 19.0 %cross_forward.1 = (bf16[512,1024]{1,0:T(8,128)(2,1)}, f32[8,1,1024]{2,1,0:T(1,128)}) custom-call(s32[1]{0:T(128)S(6)} %copy.125.length_ref, bf16[512,1024]{1,0:T(8,128)(2,1)} %add_convert_fusion.14.q_ref, bf16[1024,1024]{1,0:T(8,128)(2,1)} %convolution_convert_fusion.k_ref, bf16[1024,1024]{1,0:T(8,128)(2,1)} %add_convert_fusion.1.v_ref), custom_call_target="tpu_custom_call" | custom-call | flops 8589934592 | bytes 6291456 | tf_op jit(solution)/shard_map/cross_forward/pallas_call | solution.py:191
  282.0 17.7 %feed_forward.4 = (bf16[4096,1024]{1,0:T(8,128)(2,1)}, bf16[512,1024]{1,0:T(8,128)(2,1)}, bf16[512,1024]{1,0:T(8,128)(2,1)}, bf16[1024,1024]{1,0:T(8,128)(2,1)},...) custom-call(s32[1]{0:T(128)} %bitcast.2.low_ref, bf16[512,1024]{1,0:T(8,128)(2,1)} %copy-done.40, ...), custom_call_target="tpu_custom_call" | custom-call | flops 8589934592 | bytes 16777216 | tf_op jit(solution)/shard_map/feed_forward/pallas_call | solution.py:419
  306.6 18.1 %feed_forward.5 = (bf16[4096,1024]{1,0:T(8,128)(2,1)}, bf16[512,1024]{1,0:T(8,128)(2,1)}, bf16[512,1024]{1,0:T(8,128)(2,1)}, bf16[1024,1024]{1,0:T(8,128)(2,1)},...) custom-call(s32[1]{0:T(128)} %bitcast.2.low_ref, ...), custom_call_target="tpu_custom_call", output_to_operand_aliasing={{0}: (9, {})} | custom-call | flops 8589934592 | bytes 16777216 | tf_op jit(solution)/shard_map/feed_forward/pallas_call | solution.py:419
  326.0 17.8 %feed_forward.6 = (bf16[4096,1024]{1,0:T(8,128)(2,1)}, bf16[512,1024]{1,0:T(8,128)(2,1)}, bf16[512,1024]{1,0:T(8,128)(2,1)}, bf16[1024,1024]{1,0:T(8,128)(2,1)},...) custom-call(s32[1]{0:T(128)} %bitcast.2.low_ref, bf16[512,1024]{1,0:T(8,128)(2,1)} %copy-done.89, ...), custom_call_target="tpu_custom_call", output_to_operand_aliasing={{0}: (9, {})} | custom-call | flops 8589934592 | bytes 16777216 | tf_op jit(solution)/shard_map/feed_forward/pallas_call | solution.py:419
  347.5 18.0 %feed_forward.7 = (bf16[4096,1024]{1,0:T(8,128)(2,1)}, bf16[512,1024]{1,0:T(8,128)(2,1)}, bf16[512,1024]{1,0:T(8,128)(2,1)}, bf16[1024,1024]{1,0:T(8,128)(2,1)},...) custom-call(s32[1]{0:T(128)} %bitcast.2.low_ref, bf16[512,1024]{1,0:T(8,128)(2,1)} %copy-done.91, ...), custom_call_target="tpu_custom_call", output_to_operand_aliasing={{0}: (9, {})} | custom-call | flops 8589934592 | bytes 16777216 | tf_op jit(solution)/shard_map/feed_forward/pallas_call | solution.py:419
  369.4 15.3 %lift_grad.2 = (bf16[2,256,1024]{2,1,0:T(8,128)(2,1)}, bf16[2,256,1024]{2,1,0:T(8,128)(2,1)}, bf16[2,256,1024]{2,1,0:T(8,128)(2,1)}, bf16[2,256,1024]{2,1,0:T(8,128)(2,1)}) custom-call(s32[1]{0:T(128)} %bitcast.2.low_ref, bf16[1024,1024]{1,0:T(8,128)(2,1)} %get-tuple-element.426.refs_0_, bf16[1024,1024]{1,0:T(8,128)(2,1)} %get-tuple-element.427.refs_1_, ...), custom_call_target="tpu_custom_call" | custom-call | flops 8589934592 | bytes 18874368 | tf_op jit(solution)/shard_map/lift_grad/pallas_call | solution.py:468
  395.1 15.2 %lift_grad.3 = (bf16[2,256,1024]{2,1,0:T(8,128)(2,1)}, bf16[2,256,1024]{2,1,0:T(8,128)(2,1)}, bf16[2,256,1024]{2,1,0:T(8,128)(2,1)}, bf16[2,256,1024]{2,1,0:T(8,128)(2,1)}) custom-call(s32[1]{0:T(128)} %bitcast.2.low_ref, bf16[1024,1024]{1,0:T(8,128)(2,1)} %get-tuple-element.436.refs_0_, ...), custom_call_target="tpu_custom_call", output_to_operand_aliasing={{0}: (6, {}), {1}: (7, {}), {2}: (8, {}), {3}: (9, {})} | custom-call | flops 8589934592 | bytes 18874368 | tf_op jit(solution)/shard_map/lift_grad/pallas_call | solution.py:468
  430.9 24.7 %cross_backward.1 = (bf16[512,1024]{1,0:T(8,128)(2,1)}, bf16[1024,1024]{1,0:T(8,128)(2,1)}, bf16[1024,1024]{1,0:T(8,128)(2,1)}) custom-call(s32[1]{0:T(128)S(6)} %copy.125.length_ref, bf16[512,1024]{1,0:T(8,128)(2,1)} %add_convert_fusion.14.q_ref, bf16[1024,1024]{1,0:T(8,128)(2,1)} %convolution_convert_fusion.k_ref, ...), custom_call_target="tpu_custom_call" | custom-call | flops 21474836480 | bytes 12582912 | tf_op jit(solution)/shard_map/cross_backward/pallas_call | solution.py:333
  482.8 16.7 %shard_grads.2 = (bf16[4,128,5120]{2,1,0:T(8,128)(2,1)}, bf16[4,128,5120]{2,1,0:T(8,128)(2,1)}) custom-call(s32[1]{0:T(128)} %bitcast.2.low_ref, bf16[512,1024]{1,0:T(8,128)(2,1)} %get-tuple-element.465.refs_0_, bf16[512,1024]{1,0:T(8,128)(2,1)} %copy-done.37, bf16[1024,1024]{1,0:T(8,128)(2,1)} %all-gather.3.cloned.1.call-done.refs_2_.refs_3_, ...), custom_call_target="tpu_custom_call" | custom-call | flops 7516192768 | bytes 14680064 | tf_op jit(solution)/shard_map/shard_grads/pallas_call | solution.py:539
  537.4 16.9 %self_backward.3 = (bf16[512,1024]{1,0:T(8,128)(2,1)}, bf16[512,1024]{1,0:T(8,128)(2,1)}, bf16[512,1024]{1,0:T(8,128)(2,1)}, bf16[512,1024]{1,0:T(8,128)(2,1)}, bf16[512,1024]{1,0:T(8,128)(2,1)}) custom-call(s32[1]{0:T(128)} %bitcast.place_ref, bf16[512,1024]{1,0:T(8,128)(2,1)} %add_convert_fusion.20.q_ref, ...), custom_call_target="tpu_custom_call" | custom-call | flops 21474836480 | bytes 16777216 | tf_op jit(solution)/shard_map/self_backward/pallas_call | solution.py:294
  554.4 23.3 %collective-permute-done.47.refs_5_ = bf16[512,1024]{1,0:T(8,128)(2,1)S(1)} collective-permute-done((bf16[512,1024]{1,0:T(8,128)(2,1)S(1)}, bf16[512,1024]{1,0:T(8,128)(2,1)S(1)}, u32[]{:S(2)}, u32[]{:S(2)}) %collective-permute-start.47) | collective-permute-done | bytes 1048608 | tf_op jit(solution)/shard_map/ppermute | solution.py:1071
  587.4 16.8 %shard_grads.3 = (bf16[4,128,3072]{2,1,0:T(8,128)(2,1)}, bf16[4,128,3072]{2,1,0:T(8,128)(2,1)}) custom-call(s32[1]{0:T(128)} %bitcast.2.low_ref, bf16[512,1024]{1,0:T(8,128)(2,1)} %copy-done.33, bf16[512,1024]{1,0:T(8,128)(2,1)} %copy-done.33, bf16[512,1024]{1,0:T(8,128)(2,1)} %copy-done.34, bf16[512,1024]{1,0:T(8,128)(2,1)} %copy-done.35, ...), custom_call_target="tpu_custom_call" | custom-call | flops 9663676416 | bytes 18874368 | tf_op jit(solution)/shard_map/shard_grads/pallas_call | solution.py:539
  604.2 9.1 %collective-permute-done.48.refs_5_ = bf16[512,1024]{1,0:T(8,128)(2,1)S(1)} collective-permute-done((bf16[512,1024]{1,0:T(8,128)(2,1)}, bf16[512,1024]{1,0:T(8,128)(2,1)S(1)}, u32[]{:S(2)}, u32[]{:S(2)}) %collective-permute-start.48) | collective-permute-done | bytes 1048608 | tf_op jit(solution)/shard_map/ppermute | solution.py:1081
  636.5 9.1 %share_grad.7 = (f32[512,1024]{1,0:T(8,128)}, f32[2,1024]{1,0:T(2,128)}) custom-call(bf16[512,1024]{1,0:T(8,128)(2,1)} %get-tuple-element.553.refs_10_.refs_0_, bf16[512,1024]{1,0:T(8,128)(2,1)} %get-tuple-element.554.refs_14_.refs_1_, bf16[512,1024]{1,0:T(8,128)(2,1)} %get-tuple-element.555.refs_9_.refs_2_, ...), custom_call_target="tpu_custom_call" | custom-call | flops 3221225472 | bytes 3145728 | tf_op jit(solution)/shard_map/share_grad/pallas_call | solution.py:693
  650.7 12.0 %collective-permute-start.63 = (bf16[128,1280]{1,0:T(8,128)(2,1)}, bf16[128,1280]{1,0:T(8,128)(2,1)S(1)}, u32[]{:S(2)}, u32[]{:S(2)}) collective-permute-start(bf16[128,1280]{1,0:T(8,128)(2,1)} %get-tuple-element.571), channel_id=1, source_target_pairs={{0,3},{1,0},{2,1},{3,2},{4,7},{5,4},{6,5},{7,6},{8,11},{9,8},{10,9... | collective-permute-start | bytes 983048 | tf_op jit(solution)/shard_map/ppermute | solution.py:755
  667.4 9.1 %collective-permute-start.59 = (f32[21504]{0:T(1024)}, f32[21504]{0:T(1024)}, u32[]{:S(2)}, u32[]{:S(2)}) collective-permute-start(f32[21504]{0:T(1024)} %constant_dynamic-update-slice_fusion.19), channel_id=1, source_target_pairs={{0,3},{1,0},{2,1},{3,2},{4,7},{5,4},{6,5},{7,6},{8,11},{9,8},{10,9... | collective-permute-start | bytes 258056 | tf_op jit(solution)/shard_map/ppermute | solution.py:755
  708.5 16.1 %collective-permute-done.64 = bf16[128,1280]{1,0:T(8,128)(2,1)S(1)} collective-permute-done((bf16[128,1280]{1,0:T(8,128)(2,1)S(1)}, bf16[128,1280]{1,0:T(8,128)(2,1)S(1)}, u32[]{:S(2)}, u32[]{:S(2)}) %collective-permute-start.64) | collective-permute-done | bytes 327712 | tf_op jit(solution)/shard_map/ppermute | solution.py:755
  (497 shorter events, 336.7 us)
Async XLA Ops:
  22.7 43.3 %all-to-all-start = ((bf16[8,2,128,256]{3,2,1,0:T(8,128)(2,1)}), bf16[8,2,128,256]{3,2,1,0:T(8,128)(2,1)}, u32[]{:S(2)}, u32[]{:S(2)}) async-start(bf16[8,2,128,256]{3,2,1,0:T(8,128)(2,1)} %get-tuple-element.321), calls=%async_computation | async-start | bytes 2097152 | tf_op jit(solution)/shard_map/all_to_all | solution.py:904
  27.1 210.0 %all-gather.3.cloned.1.call-start = ((), (), s32[]{:S(2)}) async-start(), calls=%async_computation.5 | async-start | bytes 2621440 | tf_op jit(solution)/shard_map/all_gather | solution.py:928
  31.8 44.5 %collective-permute-start.7 = (bf16[512,1024]{1,0:T(8,128)(2,1)S(1)}, bf16[512,1024]{1,0:T(8,128)(2,1)S(1)}, u32[]{:S(2)}, u32[]{:S(2)}) collective-permute-start(bf16[512,1024]{1,0:T(8,128)(2,1)S(1)} %copy-done.4), channel_id=1, source_target_pairs={{0,1},{1,2},{2,3},{4,5},{5,6},{6,7},{8,9},{9,10},{10,11},{12,13},{... | collective-permute-start | bytes 3145736 | tf_op jit(solution)/shard_map/ppermute | solution.py:910
  40.2 35.1 %collective-permute-start.4 = (bf16[4,128,768]{2,1,0:T(8,128)(2,1)}, bf16[4,128,768]{2,1,0:T(8,128)(2,1)}, u32[]{:S(2)}, u32[]{:S(2)}) collective-permute-start(bf16[4,128,768]{2,1,0:T(8,128)(2,1)} %stack_shards.2.refs_0_), channel_id=1, source_target_pairs={{0,16},{4,20},{8,24},{12,28},{16,0},{20,4},{24,8},{28,12},{1,17},{... | collective-permute-start | bytes 2359304 | tf_op jit(solution)/shard_map/ppermute | solution.py:747
  41.7 34.6 %collective-permute-start.5 = (bf16[4,128,768]{2,1,0:T(8,128)(2,1)}, bf16[4,128,768]{2,1,0:T(8,128)(2,1)}, u32[]{:S(2)}, u32[]{:S(2)}) collective-permute-start(bf16[4,128,768]{2,1,0:T(8,128)(2,1)} %stack_shards.2.refs_0_), channel_id=1, source_target_pairs={{0,24},{4,28},{8,16},{12,20},{16,8},{20,12},{24,0},{28,4},{1,25},{... | collective-permute-start | bytes 2359304 | tf_op jit(solution)/shard_map/ppermute | solution.py:747
  106.3 43.5 %collective-permute-start.18 = (bf16[4,128,1280]{2,1,0:T(8,128)(2,1)}, bf16[4,128,1280]{2,1,0:T(8,128)(2,1)}, u32[]{:S(2)}, u32[]{:S(2)}) collective-permute-start(bf16[4,128,1280]{2,1,0:T(8,128)(2,1)} %stack_shards.3.refs_0_), channel_id=1, source_target_pairs={{0,8},{4,12},{8,0},{12,4},{16,24},{20,28},{24,16},{28,20},{1,9},{5... | collective-permute-start | bytes 3932168 | tf_op jit(solution)/shard_map/ppermute | solution.py:747
  107.5 42.2 %collective-permute-start.19 = (bf16[4,128,1280]{2,1,0:T(8,128)(2,1)}, bf16[4,128,1280]{2,1,0:T(8,128)(2,1)}, u32[]{:S(2)}, u32[]{:S(2)}) collective-permute-start(bf16[4,128,1280]{2,1,0:T(8,128)(2,1)} %stack_shards.3.refs_0_), channel_id=1, source_target_pairs={{0,16},{4,20},{8,24},{12,28},{16,0},{20,4},{24,8},{28,12},{1,17},{... | collective-permute-start | bytes 3932168 | tf_op jit(solution)/shard_map/ppermute | solution.py:747
  108.4 41.3 %collective-permute-start.17 = (bf16[512,1024]{1,0:T(8,128)(2,1)S(1)}, bf16[512,1024]{1,0:T(8,128)(2,1)S(1)}, u32[]{:S(2)}, u32[]{:S(2)}) collective-permute-start(bf16[512,1024]{1,0:T(8,128)(2,1)S(1)} %collective-permute-done.7.refs_4_), channel_id=1, source_target_pairs={{0,1},{1,2},{2,3},{4,5},{5,6},{6,7},{8,9},{9,10},{10,11},{12,13},{... | collective-permute-start | bytes 3145736 | tf_op jit(solution)/shard_map/ppermute | solution.py:927
  111.1 169.9 %all-gather.5.cloned.1.call-start = ((), (), s32[]{:S(2)}) async-start(), calls=%async_computation.6 | async-start | bytes 9437184 | tf_op jit(solution)/shard_map/all_gather | solution.py:959
  149.7 39.1 %collective-permute-start.20 = (bf16[512,1024]{1,0:T(8,128)(2,1)S(1)}, bf16[512,1024]{1,0:T(8,128)(2,1)S(1)}, u32[]{:S(2)}, u32[]{:S(2)}) collective-permute-start(bf16[512,1024]{1,0:T(8,128)(2,1)S(1)} %collective-permute-done.17.refs_4_), channel_id=1, source_target_pairs={{0,1},{1,2},{2,3},{4,5},{5,6},{6,7},{8,9},{9,10},{10,11},{12,13},{... | collective-permute-start | bytes 3145736 | tf_op jit(solution)/shard_map/ppermute | solution.py:952
  191.7 334.1 %reduce-scatter.3.cloned.1.call-start = ((), (), s32[]{:S(2)}) async-start(), calls=%async_computation.7 | async-start | bytes 9437184 | tf_op jit(solution)/shard_map/reduce_scatter | solution.py:1016
  220.9 30.7 %collective-permute-start.27 = (bf16[8,2,128,256]{3,2,1,0:T(8,128)(2,1)}, bf16[8,2,128,256]{3,2,1,0:T(8,128)(2,1)}, u32[]{:S(2)}, u32[]{:S(2)}) collective-permute-start(bf16[8,2,128,256]{3,2,1,0:T(8,128)(2,1)} %collective-permute-done.26.refs_1_), channel_id=1, source_target_pairs={{0,1},{1,2},{2,3},{3,0},{4,5},{5,6},{6,7},{7,4},{8,9},{9,10},{10,1... | collective-permute-start | bytes 3145736 | tf_op jit(solution)/shard_map/ppermute | solution.py:755
  305.6 38.2 %collective-permute-start.35 = (bf16[512,1024]{1,0:T(8,128)(2,1)}, bf16[512,1024]{1,0:T(8,128)(2,1)S(1)}, u32[]{:S(2)}, u32[]{:S(2)}) collective-permute-start(bf16[512,1024]{1,0:T(8,128)(2,1)} %copy-done.40), channel_id=1, source_target_pairs={{0,24},{4,28},{8,16},{12,20},{16,8},{20,12},{24,0},{28,4},{1,25},{... | collective-permute-start | bytes 3145736 | tf_op jit(solution)/shard_map/ppermute | solution.py:747
  508.3 77.6 %reduce-scatter.5.cloned.1.call-start = ((), (), s32[]{:S(2)}) async-start(), calls=%async_computation.8 | async-start | bytes 2621440 | tf_op jit(solution)/shard_map/reduce_scatter | solution.py:1060
  526.1 51.6 %collective-permute-start.47 = (bf16[512,1024]{1,0:T(8,128)(2,1)S(1)}, bf16[512,1024]{1,0:T(8,128)(2,1)S(1)}, u32[]{:S(2)}, u32[]{:S(2)}) collective-permute-start(bf16[512,1024]{1,0:T(8,128)(2,1)S(1)} %copy-done.94), channel_id=1, source_target_pairs={{1,0},{2,1},{3,2},{5,4},{6,5},{7,6},{9,8},{10,9},{11,10},{13,12},{... | collective-permute-start | bytes 3145736 | tf_op jit(solution)/shard_map/ppermute | solution.py:1071
  533.9 70.3 %collective-permute-start.49 = (bf16[128,5120]{1,0:T(8,128)(2,1)}, bf16[128,5120]{1,0:T(8,128)(2,1)S(1)}, u32[]{:S(2)}, u32[]{:S(2)}) collective-permute-start(bf16[128,5120]{1,0:T(8,128)(2,1)} %get-tuple-element.523), channel_id=1, source_target_pairs={{0,8},{4,12},{8,0},{12,4},{16,24},{20,28},{24,16},{28,20},{1,9},{5... | collective-permute-start | bytes 3932168 | tf_op jit(solution)/shard_map/ppermute | solution.py:747
  535.8 68.4 %collective-permute-start.50 = (bf16[128,5120]{1,0:T(8,128)(2,1)}, bf16[128,5120]{1,0:T(8,128)(2,1)}, u32[]{:S(2)}, u32[]{:S(2)}) collective-permute-start(bf16[128,5120]{1,0:T(8,128)(2,1)} %get-tuple-element.524), channel_id=1, source_target_pairs={{0,16},{4,20},{8,24},{12,28},{16,0},{20,4},{24,8},{28,12},{1,17},{... | collective-permute-start | bytes 3932168 | tf_op jit(solution)/shard_map/ppermute | solution.py:747
  537.3 66.9 %collective-permute-start.51 = (bf16[128,5120]{1,0:T(8,128)(2,1)}, bf16[128,5120]{1,0:T(8,128)(2,1)}, u32[]{:S(2)}, u32[]{:S(2)}) collective-permute-start(bf16[128,5120]{1,0:T(8,128)(2,1)} %get-tuple-element.525), channel_id=1, source_target_pairs={{0,24},{4,28},{8,16},{12,20},{16,8},{20,12},{24,0},{28,4},{1,25},{... | collective-permute-start | bytes 3932168 | tf_op jit(solution)/shard_map/ppermute | solution.py:747
  629.2 34.7 %collective-permute-start.53 = (bf16[128,3072]{1,0:T(8,128)(2,1)}, bf16[128,3072]{1,0:T(8,128)(2,1)}, u32[]{:S(2)}, u32[]{:S(2)}) collective-permute-start(bf16[128,3072]{1,0:T(8,128)(2,1)} %get-tuple-element.544), channel_id=1, source_target_pairs={{0,8},{4,12},{8,0},{12,4},{16,24},{20,28},{24,16},{28,20},{1,9},{5... | collective-permute-start | bytes 2359304 | tf_op jit(solution)/shard_map/ppermute | solution.py:747
  630.6 36.8 %collective-permute-start.54 = (bf16[128,3072]{1,0:T(8,128)(2,1)}, bf16[128,3072]{1,0:T(8,128)(2,1)}, u32[]{:S(2)}, u32[]{:S(2)}) collective-permute-start(bf16[128,3072]{1,0:T(8,128)(2,1)} %get-tuple-element.545), channel_id=1, source_target_pairs={{0,16},{4,20},{8,24},{12,28},{16,0},{20,4},{24,8},{28,12},{1,17},{... | collective-permute-start | bytes 2359304 | tf_op jit(solution)/shard_map/ppermute | solution.py:747
  632.1 35.3 %collective-permute-start.55 = (bf16[128,3072]{1,0:T(8,128)(2,1)}, bf16[128,3072]{1,0:T(8,128)(2,1)}, u32[]{:S(2)}, u32[]{:S(2)}) collective-permute-start(bf16[128,3072]{1,0:T(8,128)(2,1)} %get-tuple-element.546), channel_id=1, source_target_pairs={{0,24},{4,28},{8,16},{12,20},{16,8},{20,12},{24,0},{28,4},{1,25},{... | collective-permute-start | bytes 2359304 | tf_op jit(solution)/shard_map/ppermute | solution.py:747
  634.9 29.0 %collective-permute-start.56 = (bf16[512,1024]{1,0:T(8,128)(2,1)}, bf16[512,1024]{1,0:T(8,128)(2,1)S(1)}, u32[]{:S(2)}, u32[]{:S(2)}) collective-permute-start(bf16[512,1024]{1,0:T(8,128)(2,1)} %get-tuple-element.565), channel_id=1, source_target_pairs={{1,0},{2,1},{3,2},{5,4},{6,5},{7,6},{9,8},{10,9},{11,10},{13,12},{... | collective-permute-start | bytes 3145736 | tf_op jit(solution)/shard_map/ppermute | solution.py:1095
  650.7 57.8 %collective-permute-start.63 = (bf16[128,1280]{1,0:T(8,128)(2,1)}, bf16[128,1280]{1,0:T(8,128)(2,1)S(1)}, u32[]{:S(2)}, u32[]{:S(2)}) collective-permute-start(bf16[128,1280]{1,0:T(8,128)(2,1)} %get-tuple-element.571), channel_id=1, source_target_pairs={{0,3},{1,0},{2,1},{3,2},{4,7},{5,4},{6,5},{7,6},{8,11},{9,8},{10,9... | collective-permute-start | bytes 983048 | tf_op jit(solution)/shard_map/ppermute | solution.py:755
  694.1 32.8 %all-to-all-start.2 = ((f32[8,1,21504]{2,1,0:T(1,128)}), f32[8,1,21504]{2,1,0:T(1,128)S(1)}, u32[]{:S(2)}, u32[]{:S(2)}) async-start(f32[8,1,21504]{2,1,0:T(1,128)} %broadcast_in_dim.115), calls=%async_computation.4 | async-start | bytes 1376256 | tf_op jit(solution)/shard_map/all_to_all | solution.py:828
  (153 other events, 1792.7 us)
Sparse Core Ops, SparseCore 0:
  111.2 58.9 all-gather.2
  191.8 55.3 all-gather.4
  429.1 68.8 reduce-scatter.2
  511.2 56.7 reduce-scatter.4
